TPU v7x, 32 devices: a whole 2x2x4 slice. The times are simulated.
32 devices in a mesh: section: 2 (over y), dp: 16 (over z, x, core).
Axes of the slice: x: 2, y: 2, z: 4, core: 2. Of those that a mesh axis runs over, the one named last changes fastest.
Arguments:
- prev_act: bfloat16 [2, 16, 192, 1024], P('section', 'dp'), may hold values from -6 to 6
- memory: bfloat16 [16, 192, 1024], P('dp', None, 'section'), may hold values from -6 to 6
- out_cot: bfloat16 [2, 16, 192, 1024], P('section', 'dp'), may hold values from -6 to 6
- tgt_len: int32 [16], P('dp'), may hold values from 12 to 192, as said below
- src_len: int32 [16], P('dp'), may hold values from 12 to 192, as said below
- norm_gain: bfloat16 [2, 3, 1024], P('section', None, 'dp'), may hold values from 0.25 to 1.75
- norm_bias: bfloat16 [2, 3, 1024], P('section', None, 'dp'), may hold values from -2 to 2
- self_qkv: bfloat16 [2, 1024, 3072], P('section', 'dp'), may hold values from -0.1875 to 0.1875
- self_qv_bias: bfloat16 [2, 2048], P('section', 'dp'), may hold values from -2 to 2
- self_out: bfloat16 [2, 1024, 1024], P('section', 'dp'), may hold values from -0.75 to 0.75
- cross_q: bfloat16 [2, 1024, 1024], P('section', 'dp'), may hold values from -0.1875 to 0.1875
- cross_kv: bfloat16 [2, 1024, 2048], P('section', 'dp'), may hold values from -0.1875 to 0.1875
- cross_qv_bias: bfloat16 [2, 2048], P('section', 'dp'), may hold values from -2 to 2
- cross_out: bfloat16 [2, 1024, 1024], P('section', 'dp'), may hold values from -0.75 to 0.75
- out_bias: bfloat16 [2, 3, 1024], P('section', None, 'dp'), may hold values from -2 to 2
- fc1: bfloat16 [2, 1024, 4096], P('section', 'dp'), may hold values from -0.1875 to 0.1875
- fc1_bias: bfloat16 [2, 4096], P('section', 'dp'), may hold values from -2 to 2
- fc2: bfloat16 [2, 4096, 1024], P('section', 'dp'), may hold values from -0.09375 to 0.09375
Outputs:
- output: bfloat16 [2, 16, 192, 1024], P('section', 'dp')
- input_grad: bfloat16 [2, 16, 192, 1024], P('section', 'dp')
- memory_grad: bfloat16 [16, 192, 1024], P('dp', None, 'section')
- grad_norm_gain: float32 [2, 3, 1024], P('section', None, 'dp')
- grad_norm_bias: float32 [2, 3, 1024], P('section', None, 'dp')
- grad_self_qkv: float32 [2, 1024, 3072], P('section', 'dp')
- grad_self_qv_bias: float32 [2, 2048], P('section', 'dp')
- grad_self_out: float32 [2, 1024, 1024], P('section', 'dp')
- grad_cross_q: float32 [2, 1024, 1024], P('section', 'dp')
- grad_cross_kv: float32 [2, 1024, 2048], P('section', 'dp')
- grad_cross_qv_bias: float32 [2, 2048], P('section', 'dp')
- grad_cross_out: float32 [2, 1024, 1024], P('section', 'dp')
- grad_out_bias: float32 [2, 3, 1024], P('section', None, 'dp')
- grad_fc1: float32 [2, 1024, 4096], P('section', 'dp')
- grad_fc1_bias: float32 [2, 4096], P('section', 'dp')
- grad_fc2: float32 [2, 4096, 1024], P('section', 'dp')
Inputs may be any that keep to these rules, and one draw needn't show every extreme that they name: `tgt_len`: A row's target length; in every draw some row has exactly 192. `src_len`: A row's source length; in every draw some row has exactly 192.
All inputs are finite; a program needn't handle non-finite values.
Results may differ from a plain program's by a relative error of at most 0.019.
Values may be sent and summed in bfloat16 or wider, within the bound.
A program may use at most 192 MiB of HBM per device.

v0:
```python
import jax
import jax.numpy as jnp
from jax import lax
from jax.sharding import PartitionSpec as P

H = 16
HD = 64


EPSILON = 1e-05
MASKED = -1000000000.0


def passed_along(value, axis, by):
    length = lax.axis_size(axis)
    return lax.ppermute(value, axis, [(i, (i + by) % length) for i in range(length)])


def norm_fwd(rows, gain, shift_term):
    center = rows - jnp.mean(rows, -1, keepdims=True)
    scale = lax.rsqrt(jnp.mean(center * center, -1, keepdims=True) + EPSILON)
    return center * scale * gain + shift_term


def gelu_exact(values):
    return jax.nn.gelu(values, approximate=False)


def product(left, right):
    return jnp.dot(left, right, preferred_element_type=jnp.float32)


def product_right_t(left, right):
    return lax.dot_general(
        left, right, (((1,), (1,)), ((), ())), preferred_element_type=jnp.float32
    )


def product_left_t(left, right):
    return lax.dot_general(
        left, right, (((0,), (0,)), ((), ())), preferred_element_type=jnp.float32
    )


def split_heads(flat, batch_rows):
    return flat.reshape(batch_rows, -1, H, HD)


def softmax_probs(query, key_rows, allowed):
    scores = jnp.einsum(
        "rthd,rshd->rhts", query, key_rows, preferred_element_type=jnp.float32
    ) * HD ** (-0.5)
    scores = jnp.where(allowed[:, None], scores, MASKED)
    weights = jnp.exp(scores - jnp.max(scores, -1, keepdims=True))
    return weights / jnp.sum(weights, -1, keepdims=True)


def attend_fwd(query, key_rows, value_rows, allowed):
    probs = softmax_probs(query, key_rows, allowed)
    mixed = jnp.einsum(
        "rhts,rshd->rthd",
        probs.astype(jnp.bfloat16),
        value_rows,
        preferred_element_type=jnp.float32,
    )
    return mixed.reshape(mixed.shape[0] * mixed.shape[1], -1).astype(jnp.bfloat16)


def attend_back(query, key_rows, value_rows, allowed, grad_mixed):
    probs = softmax_probs(query, key_rows, allowed)
    grad_heads = grad_mixed.reshape(query.shape)
    grad_probs = jnp.einsum(
        "rthd,rshd->rhts", grad_heads, value_rows, preferred_element_type=jnp.float32
    )
    delta = jnp.sum(probs * grad_probs, -1, keepdims=True)
    grad_scores = (probs * (grad_probs - delta)).astype(jnp.bfloat16)
    scale = HD ** (-0.5)
    grad_query = (
        jnp.einsum("rhts,rshd->rthd", grad_scores, key_rows, preferred_element_type=jnp.float32)
        * scale
    )
    grad_keys = (
        jnp.einsum("rhts,rthd->rshd", grad_scores, query, preferred_element_type=jnp.float32)
        * scale
    )
    grad_values = jnp.einsum(
        "rhts,rthd->rshd",
        probs.astype(jnp.bfloat16),
        grad_heads,
        preferred_element_type=jnp.float32,
    )
    width = query.shape[2] * query.shape[3]
    return (
        grad_query.reshape(-1, width).astype(jnp.bfloat16),
        grad_keys.reshape(-1, width).astype(jnp.bfloat16),
        grad_values.reshape(-1, width).astype(jnp.bfloat16),
    )


def unpack(pieces):
    return tuple((piece[0] for piece in pieces))


def on_device(
    prev_act,
    memory,
    out_cot,
    tgt_len,
    src_len,
    norm_gain,
    norm_bias,
    self_qkv,
    self_qv_bias,
    self_out,
    cross_q,
    cross_kv,
    cross_qv_bias,
    cross_out,
    out_bias,
    fc1,
    fc1_bias,
    fc2,
):
    fetched = unpack(
        (
            lax.all_gather(norm_gain, "dp", axis=2, tiled=True),
            lax.all_gather(norm_bias, "dp", axis=2, tiled=True),
            lax.all_gather(self_qkv, "dp", axis=1, tiled=True),
            lax.all_gather(self_qv_bias, "dp", axis=1, tiled=True),
            lax.all_gather(self_out, "dp", axis=1, tiled=True),
            lax.all_gather(cross_q, "dp", axis=1, tiled=True),
            lax.all_gather(cross_kv, "dp", axis=1, tiled=True),
            lax.all_gather(cross_qv_bias, "dp", axis=1, tiled=True),
            lax.all_gather(cross_out, "dp", axis=1, tiled=True),
            lax.all_gather(out_bias, "dp", axis=2, tiled=True),
            lax.all_gather(fc1, "dp", axis=1, tiled=True),
            lax.all_gather(fc1_bias, "dp", axis=1, tiled=True),
            lax.all_gather(fc2, "dp", axis=1, tiled=True),
        )
    )
    gains, shifts, w_sqkv, b_sqv, w_sout, w_cq, w_ckv, b_cqv, w_cout, b_out, w_one, b_one, w_two = (
        fetched
    )
    gain_f = gains.astype(jnp.float32)
    shift_f = shifts.astype(jnp.float32)
    sqv_f = b_sqv.astype(jnp.float32)
    cqv_f = b_cqv.astype(jnp.float32)
    out_f = b_out.astype(jnp.float32)
    one_f = b_one.astype(jnp.float32)
    source = passed_along(prev_act, "section", 1)[0]
    batch_rows, length, width = source.shape
    encoded = lax.all_gather(memory, "section", axis=2, tiled=True)
    mem_flat = encoded.reshape(-1, width)
    places = jnp.arange(length)
    self_ok = (places[None, None, :] <= places[None, :, None]) & (
        places[None, None, :] < tgt_len[:, None, None]
    )
    cross_ok = jnp.arange(encoded.shape[1])[None, None, :] < src_len[:, None, None]
    resid = source.astype(jnp.float32).reshape(-1, width)
    normed_one, pull_one = jax.vjp(norm_fwd, resid, gain_f[0], shift_f[0])
    first_in = normed_one.astype(jnp.bfloat16)
    joint = product(first_in, w_sqkv)
    query_self = (joint[:, :width] + sqv_f[:width]).astype(jnp.bfloat16)
    keys_self = joint[:, width : 2 * width].astype(jnp.bfloat16)
    values_self = (joint[:, 2 * width :] + sqv_f[width:]).astype(jnp.bfloat16)
    self_mixed = attend_fwd(
        split_heads(query_self, batch_rows),
        split_heads(keys_self, batch_rows),
        split_heads(values_self, batch_rows),
        self_ok,
    )
    after_self = resid + (product(self_mixed, w_sout) + out_f[0])
    normed_two, pull_two = jax.vjp(norm_fwd, after_self, gain_f[1], shift_f[1])
    second_in = normed_two.astype(jnp.bfloat16)
    query_cross = (product(second_in, w_cq) + cqv_f[:width]).astype(jnp.bfloat16)
    memory_proj = product(mem_flat, w_ckv)
    keys_cross = memory_proj[:, :width].astype(jnp.bfloat16)
    values_cross = (memory_proj[:, width:] + cqv_f[width:]).astype(jnp.bfloat16)
    cross_mixed = attend_fwd(
        split_heads(query_cross, batch_rows),
        split_heads(keys_cross, batch_rows),
        split_heads(values_cross, batch_rows),
        cross_ok,
    )
    after_cross = after_self + (product(cross_mixed, w_cout) + out_f[1])
    normed_three, pull_three = jax.vjp(norm_fwd, after_cross, gain_f[2], shift_f[2])
    third_in = normed_three.astype(jnp.bfloat16)
    pre_act = product(third_in, w_one) + one_f
    activ, pull_gelu = jax.vjp(gelu_exact, pre_act)
    act_low = activ.astype(jnp.bfloat16)
    result = after_cross + (product(act_low, w_two) + out_f[2])
    output = result.astype(jnp.bfloat16).reshape(1, batch_rows, length, width)
    (
        unused_gains,
        unused_shifts,
        w_sqkv,
        unused_sqv,
        w_sout,
        w_cq,
        w_ckv,
        unused_cqv,
        w_cout,
        unused_out,
        w_one,
        unused_one,
        w_two,
    ) = fetched
    grad_out = passed_along(out_cot, "section", -1)[0].astype(jnp.float32).reshape(-1, width)
    ffn_grad = grad_out.astype(jnp.bfloat16)
    grad_fc2 = product_left_t(act_low, ffn_grad)
    grad_b2 = jnp.sum(ffn_grad, 0, dtype=jnp.float32)
    grad_act = product_right_t(ffn_grad, w_two)
    (grad_pre,) = pull_gelu(grad_act)
    pre_low = grad_pre.astype(jnp.bfloat16)
    grad_fc1 = product_left_t(third_in, pre_low)
    grad_b1 = jnp.sum(pre_low, 0, dtype=jnp.float32)
    grad_mid, grad_gain3, grad_shift3 = pull_three(product_right_t(pre_low, w_one))
    grad_mid = grad_mid + grad_out
    cross_grad = grad_mid.astype(jnp.bfloat16)
    grad_cout = product_left_t(cross_mixed, cross_grad)
    grad_bco = jnp.sum(cross_grad, 0, dtype=jnp.float32)
    grad_cmix = product_right_t(cross_grad, w_cout).astype(jnp.bfloat16)
    grad_qc, grad_kc, grad_vc = attend_back(
        split_heads(query_cross, batch_rows),
        split_heads(keys_cross, batch_rows),
        split_heads(values_cross, batch_rows),
        cross_ok,
        grad_cmix,
    )
    grad_cq = product_left_t(second_in, grad_qc)
    grad_kv = jnp.concatenate([grad_kc, grad_vc], -1)
    grad_ckv = product_left_t(mem_flat, grad_kv)
    grad_cqv = jnp.concatenate(
        [jnp.sum(grad_qc, 0, dtype=jnp.float32), jnp.sum(grad_vc, 0, dtype=jnp.float32)]
    )
    grad_memory = product_right_t(grad_kv, w_ckv).reshape(encoded.shape)
    memory_grad = lax.psum_scatter(
        grad_memory.astype(jnp.bfloat16), "section", scatter_dimension=2, tiled=True
    )
    grad_after, grad_gain2, grad_shift2 = pull_two(product_right_t(grad_qc, w_cq))
    grad_after = grad_after + grad_mid
    self_grad = grad_after.astype(jnp.bfloat16)
    grad_sout = product_left_t(self_mixed, self_grad)
    grad_bso = jnp.sum(self_grad, 0, dtype=jnp.float32)
    grad_smix = product_right_t(self_grad, w_sout).astype(jnp.bfloat16)
    grad_qs, grad_ks, grad_vs = attend_back(
        split_heads(query_self, batch_rows),
        split_heads(keys_self, batch_rows),
        split_heads(values_self, batch_rows),
        self_ok,
        grad_smix,
    )
    grad_qkv = jnp.concatenate([grad_qs, grad_ks, grad_vs], -1)
    grad_sqkv = product_left_t(first_in, grad_qkv)
    grad_sqv = jnp.concatenate(
        [jnp.sum(grad_qs, 0, dtype=jnp.float32), jnp.sum(grad_vs, 0, dtype=jnp.float32)]
    )
    grad_in, grad_gain1, grad_shift1 = pull_one(product_right_t(grad_qkv, w_sqkv))
    grad_in = grad_in + grad_after
    input_grad = passed_along(
        grad_in.astype(jnp.bfloat16).reshape(1, batch_rows, length, width), "section", -1
    )
    grad_gain = jnp.stack([grad_gain1, grad_gain2, grad_gain3])
    grad_shift = jnp.stack([grad_shift1, grad_shift2, grad_shift3])
    grad_obias = jnp.stack([grad_bso, grad_bco, grad_b2])
    sums = (
        lax.psum_scatter(
            grad_gain.astype(jnp.bfloat16), "dp", scatter_dimension=1, tiled=True
        ).astype(jnp.float32),
        lax.psum_scatter(
            grad_shift.astype(jnp.bfloat16), "dp", scatter_dimension=1, tiled=True
        ).astype(jnp.float32),
        lax.psum_scatter(
            grad_sqkv.astype(jnp.bfloat16), "dp", scatter_dimension=0, tiled=True
        ).astype(jnp.float32),
        lax.psum_scatter(
            grad_sqv.astype(jnp.bfloat16), "dp", scatter_dimension=0, tiled=True
        ).astype(jnp.float32),
        lax.psum_scatter(
            grad_sout.astype(jnp.bfloat16), "dp", scatter_dimension=0, tiled=True
        ).astype(jnp.float32),
        lax.psum_scatter(
            grad_cq.astype(jnp.bfloat16), "dp", scatter_dimension=0, tiled=True
        ).astype(jnp.float32),
        lax.psum_scatter(
            grad_ckv.astype(jnp.bfloat16), "dp", scatter_dimension=0, tiled=True
        ).astype(jnp.float32),
        lax.psum_scatter(
            grad_cqv.astype(jnp.bfloat16), "dp", scatter_dimension=0, tiled=True
        ).astype(jnp.float32),
        lax.psum_scatter(
            grad_cout.astype(jnp.bfloat16), "dp", scatter_dimension=0, tiled=True
        ).astype(jnp.float32),
        lax.psum_scatter(
            grad_obias.astype(jnp.bfloat16), "dp", scatter_dimension=1, tiled=True
        ).astype(jnp.float32),
        lax.psum_scatter(
            grad_fc1.astype(jnp.bfloat16), "dp", scatter_dimension=0, tiled=True
        ).astype(jnp.float32),
        lax.psum_scatter(
            grad_b1.astype(jnp.bfloat16), "dp", scatter_dimension=0, tiled=True
        ).astype(jnp.float32),
        lax.psum_scatter(
            grad_fc2.astype(jnp.bfloat16), "dp", scatter_dimension=0, tiled=True
        ).astype(jnp.float32),
    )
    return (
        output,
        input_grad,
        memory_grad,
        sums[0][None],
        sums[1][None],
        sums[2][None],
        sums[3][None],
        sums[4][None],
        sums[5][None],
        sums[6][None],
        sums[7][None],
        sums[8][None],
        sums[9][None],
        sums[10][None],
        sums[11][None],
        sums[12][None],
    )


def solution(mesh):
    in_specs = (
        P("section", "dp", None, None),
        P("dp", None, "section"),
        P("section", "dp", None, None),
        P("dp"),
        P("dp"),
        P("section", None, "dp"),
        P("section", None, "dp"),
        P("section", "dp", None),
        P("section", "dp"),
        P("section", "dp", None),
        P("section", "dp", None),
        P("section", "dp", None),
        P("section", "dp"),
        P("section", "dp", None),
        P("section", None, "dp"),
        P("section", "dp", None),
        P("section", "dp"),
        P("section", "dp", None),
    )
    out_specs = (
        P("section", "dp", None, None),
        P("section", "dp", None, None),
        P("dp", None, "section"),
        P("section", None, "dp"),
        P("section", None, "dp"),
        P("section", "dp", None),
        P("section", "dp"),
        P("section", "dp", None),
        P("section", "dp", None),
        P("section", "dp", None),
        P("section", "dp"),
        P("section", "dp", None),
        P("section", None, "dp"),
        P("section", "dp", None),
        P("section", "dp"),
        P("section", "dp", None),
    )
    return jax.shard_map(
        on_device, mesh=mesh, in_specs=in_specs, out_specs=out_specs, check_vma=False
    )
```

profile of v0, /device:TPU:1, one launch (start us, length us, event | category | flops | bytes accessed | tf_op | source)
XLA Modules:
  0.0 1223.2 jit_solution(17554845720823093163)
XLA Ops:
  16.4 25.2 %all_gather.47 = bf16[1,3,1024]{1,0,2:T(2,128)(2,1)S(1)} all-gather(bf16[1,3,64]{1,0,2:T(2,128)(2,1)S(1)} %copy.105), channel_id=1, replica_groups=mesh['section'=2,'dp'=16] {'dp'}, dimensions={2}, use_global_device_ids=true | all-gather | bytes 6528 | tf_op jit(solution)/shard_map/all_gather | solution.py:135
  42.2 20.7 %all_gather.43 = bf16[1,3,1024]{1,0,2:T(2,128)(2,1)S(1)} all-gather(bf16[1,3,64]{1,0,2:T(2,128)(2,1)S(1)} %copy.100), channel_id=1, replica_groups=mesh['section'=2,'dp'=16] {'dp'}, dimensions={2}, use_global_device_ids=true | all-gather | bytes 6528 | tf_op jit(solution)/shard_map/all_gather | solution.py:127
  63.4 18.7 %all_gather.45 = bf16[1,2048]{1,0:T(2,128)(2,1)S(1)} all-gather(bf16[1,128]{1,0:T(2,128)(2,1)S(1)} %copy-done.92), channel_id=1, replica_groups=mesh['section'=2,'dp'=16] {'dp'}, dimensions={1}, use_global_device_ids=true | all-gather | bytes 4352 | tf_op jit(solution)/shard_map/all_gather | solution.py:129
  82.1 17.3 %all_gather.50 = bf16[1,2048]{1,0:T(2,128)(2,1)S(1)} all-gather(bf16[1,128]{1,0:T(2,128)(2,1)S(1)} %copy-done.93), channel_id=1, replica_groups=mesh['section'=2,'dp'=16] {'dp'}, dimensions={1}, use_global_device_ids=true | all-gather | bytes 4352 | tf_op jit(solution)/shard_map/all_gather | solution.py:133
  99.4 7.2 all_gather.48
  106.8 10.3 slice_reduce_fusion
  117.1 10.8 slice_reduce_fusion.1
  128.0 19.5 %all_gather.54 = bf16[1,4096]{1,0:T(2,128)(2,1)S(1)} all-gather(bf16[1,256]{1,0:T(2,128)(2,1)S(1)} %copy-done.90), channel_id=1, replica_groups=mesh['section'=2,'dp'=16] {'dp'}, dimensions={1}, use_global_device_ids=true | all-gather | bytes 8704 | tf_op jit(solution)/shard_map/all_gather | solution.py:137
  148.3 20.4 %all_gather.42 = bf16[1,3,1024]{1,0,2:T(2,128)(2,1)S(1)} all-gather(bf16[1,3,64]{1,0,2:T(2,128)(2,1)S(1)} %copy.99), channel_id=1, replica_groups=mesh['section'=2,'dp'=16] {'dp'}, dimensions={2}, use_global_device_ids=true | all-gather | bytes 6528 | tf_op jit(solution)/shard_map/all_gather | solution.py:126
  169.2 10.3 slice_reduce_fusion.2
  203.9 14.1 %all-gather.14.cloned.1.call-done = bf16[1,1024,1024]{2,1,0:T(8,128)(2,1)} async-done(((bf16[1,64,1024]{2,1,0:T(8,128)(2,1)}), bf16[1,1024,1024]{2,1,0:T(8,128)(2,1)}) %all-gather.14.cloned.1.call-update) | async-done | bytes 2097168 | tf_op jit(solution)/shard_map/all_gather | solution.py:131
  225.8 34.4 %all-gather.16.cloned.1.call-done = bf16[1,1024,1024]{2,1,0:T(8,128)(2,1)} async-done(((bf16[1,64,1024]{2,1,0:T(8,128)(2,1)}), bf16[1,1024,1024]{2,1,0:T(8,128)(2,1)}) %all-gather.16.cloned.1.call-update) | async-done | bytes 2097168 | tf_op jit(solution)/shard_map/all_gather | solution.py:134
  262.7 73.2 %all-gather.18.cloned.1.call-done = bf16[1,1024,4096]{2,1,0:T(8,128)(2,1)} async-done(((bf16[1,64,4096]{2,1,0:T(8,128)(2,1)}), bf16[1,1024,4096]{2,1,0:T(8,128)(2,1)}) %all-gather.18.cloned.1.call-update) | async-done | bytes 8388624 | tf_op jit(solution)/shard_map/all_gather | solution.py:136
  335.9 13.0 %multiply_convert_fusion.2 = (bf16[192,4096]{1,0:T(8,128)(2,1)}, f32[192,4096]{1,0:T(8,128)}, f32[192,4096]{1,0:T(8,128)}) fusion(f32[4096]{0:T(1024)S(1)} %bitcast.321, bf16[1,1024,4096]{2,1,0:T(8,128)(2,1)} %all-gather.18.cloned.1.call-done, f32[192,1024]{1,0:T(8,128)S(1)} %get-tuple-element.125, f32[1024]{0:T(1024)S(1)} %get-tuple-element.96, ...), kind=kOutput, calls=%fused_computation.30 | convolution fusion | flops 1663500288 | bytes 17065472 | tf_op jit(solution)/shard_map/dot_general | solution.py:30
  348.9 62.3 %all-gather.20.cloned.1.call-done = bf16[1,4096,1024]{2,1,0:T(8,128)(2,1)} async-done(((bf16[1,256,1024]{2,1,0:T(8,128)(2,1)}), bf16[1,4096,1024]{2,1,0:T(8,128)(2,1)}) %all-gather.20.cloned.1.call-update) | async-done | bytes 8388624 | tf_op jit(solution)/shard_map/all_gather | solution.py:138
  411.2 9.8 fusion.169
  455.3 5.4 fusion.154
  487.5 6.5 copy.134
  501.6 5.6 convolution_convert_fusion
  508.7 5.7 convolution_convert_fusion.1
  519.6 4.8 fusion.89
  524.4 54.2 %all-reduce.3 = (bf16[2048]{0:T(1024)(128)(2,1)S(1)}, bf16[2048]{0:T(1024)(128)(2,1)S(1)}, bf16[4096]{0:T(1024)(128)(2,1)S(1)}) all-reduce(bf16[2048]{0:T(1024)(128)(2,1)S(1)} %pad_maximum_fusion.9, bf16[2048]{0:T(1024)(128)(2,1)S(1)} %pad_maximum_fusion.10, ...), channel_id=6, replica_groups=mesh['section'=2,'dp'=16] {'dp'}, use_global_device_ids=true, to_apply=%region_30.31.clone | all-reduce | flops 8192 | bytes 32768
  579.8 6.0 fusion.92
  588.6 34.6 %reduce-scatter.36.cloned.1.call-done = bf16[64,3]{1,0:T(8,128)(2,1)} async-done(((bf16[1024,3]{1,0:T(8,128)(2,1)}), bf16[64,3]{1,0:T(8,128)(2,1)}) %reduce-scatter.36.cloned.1.call-update) | async-done | bytes 400
  624.6 63.3 %reduce-scatter.28.cloned.1.call-done = bf16[64,1024]{1,0:T(8,128)(2,1)} async-done(((bf16[1024,1024]{1,0:T(8,128)(2,1)}), bf16[64,1024]{1,0:T(8,128)(2,1)}) %reduce-scatter.28.cloned.1.call-update) | async-done | bytes 131088 | tf_op jit(solution)/shard_map/reduce_scatter | solution.py:291
  689.6 63.1 %reduce-scatter.26.cloned.1.call-done = bf16[64,1024]{1,0:T(8,128)(2,1)} async-done(((bf16[1024,1024]{1,0:T(8,128)(2,1)}), bf16[64,1024]{1,0:T(8,128)(2,1)}) %reduce-scatter.26.cloned.1.call-update) | async-done | bytes 131088 | tf_op jit(solution)/shard_map/reduce_scatter | solution.py:282
  754.3 62.7 %reduce-scatter.24.cloned.1.call-done = bf16[64,1024]{1,0:T(8,128)(2,1)} async-done(((bf16[1024,1024]{1,0:T(8,128)(2,1)}), bf16[64,1024]{1,0:T(8,128)(2,1)}) %reduce-scatter.24.cloned.1.call-update) | async-done | bytes 131088 | tf_op jit(solution)/shard_map/reduce_scatter | solution.py:279
  818.6 74.1 %reduce-scatter.38.cloned.1.call-done = bf16[64,2048]{1,0:T(8,128)(2,1)} async-done(((bf16[1024,2048]{1,0:T(8,128)(2,1)}), bf16[64,2048]{1,0:T(8,128)(2,1)}) %reduce-scatter.38.cloned.1.call-update) | async-done | bytes 262160
  895.1 86.8 %reduce-scatter.22.cloned.1.call-done = bf16[64,3072]{1,0:T(8,128)(2,1)} async-done(((bf16[1024,3072]{1,0:T(8,128)(2,1)}), bf16[64,3072]{1,0:T(8,128)(2,1)}) %reduce-scatter.22.cloned.1.call-update) | async-done | bytes 393232 | tf_op jit(solution)/shard_map/reduce_scatter | solution.py:273
  983.8 107.2 %reduce-scatter.32.cloned.1.call-done = bf16[256,1024]{1,0:T(8,128)(2,1)} async-done(((bf16[4096,1024]{1,0:T(8,128)(2,1)}), bf16[256,1024]{1,0:T(8,128)(2,1)}) %reduce-scatter.32.cloned.1.call-update) | async-done | bytes 524304 | tf_op jit(solution)/shard_map/reduce_scatter | solution.py:303
  1093.1 106.7 %reduce-scatter.30.cloned.1.call-done = bf16[64,4096]{1,0:T(8,128)(2,1)} async-done(((bf16[1024,4096]{1,0:T(8,128)(2,1)}), bf16[64,4096]{1,0:T(8,128)(2,1)}) %reduce-scatter.30.cloned.1.call-update) | async-done | bytes 524304 | tf_op jit(solution)/shard_map/reduce_scatter | solution.py:297
  1201.9 13.5 %reduce-scatter.20.cloned.1.call-done = bf16[1,192,512]{2,1,0:T(8,128)(2,1)} async-done(((bf16[1,192,1024]{2,1,0:T(8,128)(2,1)}), bf16[1,192,512]{2,1,0:T(8,128)(2,1)}) %reduce-scatter.20.cloned.1.call-update) | async-done | bytes 196624 | tf_op jit(solution)/shard_map/reduce_scatter | solution.py:237
  (359 shorter events, 137.6 us)
Async XLA Ops:
  7.2 92.2 %copy-start.45 = (bf16[1,192,512]{2,1,0:T(8,128)(2,1)S(1)}, bf16[1,192,512]{2,1,0:T(8,128)(2,1)}, u32[]{:S(2)}) copy-start(bf16[1,192,512]{2,1,0:T(8,128)(2,1)} %param.19) | copy-start | bytes 589828
  7.2 173.5 %all-gather.12.cloned.1.call-start = ((), (), s32[]{:S(2)}) async-start(), calls=%async_computation.13 | async-start | bytes 4456448 | tf_op jit(solution)/shard_map/all_gather | solution.py:132
  7.9 179.8 %all-gather.8.cloned.1.call-start = ((), (), s32[]{:S(2)}) async-start(), calls=%async_computation.11 | async-start | bytes 6684672 | tf_op jit(solution)/shard_map/all_gather | solution.py:128
  8.7 192.4 %all-gather.10.cloned.1.call-start = ((), (), s32[]{:S(2)}) async-start(), calls=%async_computation.12 | async-start | bytes 2228224 | tf_op jit(solution)/shard_map/all_gather | solution.py:130
  9.4 208.5 %all-gather.14.cloned.1.call-start = ((), (), s32[]{:S(2)}) async-start(), calls=%async_computation.14 | async-start | bytes 2228224 | tf_op jit(solution)/shard_map/all_gather | solution.py:131
  10.0 250.2 %all-gather.16.cloned.1.call-start = ((), (), s32[]{:S(2)}) async-start(), calls=%async_computation.15 | async-start | bytes 2228224 | tf_op jit(solution)/shard_map/all_gather | solution.py:134
  10.6 325.3 %all-gather.18.cloned.1.call-start = ((), (), s32[]{:S(2)}) async-start(), calls=%async_computation.16 | async-start | bytes 8912896 | tf_op jit(solution)/shard_map/all_gather | solution.py:136
  11.2 400.0 %all-gather.20.cloned.1.call-start = ((), (), s32[]{:S(2)}) async-start(), calls=%async_computation.17 | async-start | bytes 8912896 | tf_op jit(solution)/shard_map/all_gather | solution.py:138
  11.9 573.9 %reduce-scatter.40.cloned.1.call-start = ((), (), s32[]{:S(2)}) async-start(), calls=%async_computation.28 | async-start | bytes 278528
  12.0 168.3 %collective-permute-start = (bf16[1,1,192,1024]{3,2,1,0:T(8,128)(2,1)}, bf16[1,1,192,1024]{3,2,1,0:T(8,128)(2,1)S(1)}, u32[]{:S(2)}, u32[]{:S(2)}) collective-permute-start(bf16[1,1,192,1024]{3,2,1,0:T(8,128)(2,1)} %param.18), channel_id=1, source_target_pairs={{0,16},{16,0},{1,17},{17,1},{2,18},{18,2},{3,19},{19,3},{4,20},{20... | collective-permute-start | bytes 1179656 | tf_op jit(solution)/shard_map/ppermute | solution.py:16
  14.1 165.4 %collective-permute-start.1 = (bf16[1,1,192,1024]{3,2,1,0:T(8,128)(2,1)}, bf16[1,1,192,1024]{3,2,1,0:T(8,128)(2,1)S(1)}, u32[]{:S(2)}, u32[]{:S(2)}) collective-permute-start(bf16[1,1,192,1024]{3,2,1,0:T(8,128)(2,1)} %param.20), channel_id=1, source_target_pairs={{0,16},{16,0},{1,17},{17,1},{2,18},{18,2},{3,19},{19,3},{4,20},{20... | collective-permute-start | bytes 1179656 | tf_op jit(solution)/shard_map/ppermute | solution.py:16
  41.7 86.3 %copy-start.90 = (bf16[1,256]{1,0:T(2,128)(2,1)S(1)}, bf16[1,256]{1,0:T(2,128)(2,1)}, u32[]{:S(2)}) copy-start(bf16[1,256]{1,0:T(2,128)(2,1)} %param.34) | copy-start | bytes 1540
  41.7 106.5 %copy-start.91 = (bf16[1,3,64]{2,1,0:T(4,128)(2,1)S(1)}, bf16[1,3,64]{2,1,0:T(4,128)(2,1)}, u32[]{:S(2)}) copy-start(bf16[1,3,64]{2,1,0:T(4,128)(2,1)} %param.23) | copy-start | bytes 1156
  128.0 90.0 %copy-start.54 = (f32[1024]{0:T(1024)}, f32[1024]{0:T(1024)S(1)}, u32[]{:S(2)}) copy-start(f32[1024]{0:T(1024)S(1)} %get-tuple-element.97) | copy-start | bytes 12292
  179.5 245.5 %copy-start.6 = (bf16[1,1,192,1024]{3,2,1,0:T(8,128)(2,1)}, bf16[1,1,192,1024]{3,2,1,0:T(8,128)(2,1)S(1)}, u32[]{:S(2)}) copy-start(bf16[1,1,192,1024]{3,2,1,0:T(8,128)(2,1)S(1)} %collective-permute-done.1) | copy-start | bytes 1179652
  223.4 205.1 %copy-start.50 = (f32[16,192]{1,0:T(8,128)}, f32[16,192]{1,0:T(8,128)S(1)}, u32[]{:S(2)}) copy-start(f32[16,192]{1,0:T(8,128)S(1)} %get-tuple-element.122) | copy-start | bytes 36868
  225.7 123.2 %copy-start.32 = (bf16[16,64,192]{2,1,0:T(8,128)(2,1)}, bf16[16,64,192]{2,1,0:T(8,128)(2,1)S(1)}, u32[]{:S(2)}) copy-start(bf16[16,64,192]{2,1,0:T(8,128)(2,1)S(1)} %convolution_convert_fusion.8) | copy-start | bytes 1179652
  262.5 162.2 %copy-start.46 = (f32[192]{0:T(256)}, f32[192]{0:T(256)S(1)}, u32[]{:S(2)}) copy-start(f32[192]{0:T(256)S(1)} %broadcast_multiply_fusion) | copy-start | bytes 2308
  262.7 161.9 %copy-start.58 = (f32[192]{0:T(256)}, f32[192]{0:T(256)S(1)}, u32[]{:S(2)}) copy-start(f32[192]{0:T(256)S(1)} %fusion.142) | copy-start | bytes 2308
  455.1 132.1 %reduce-scatter.34.cloned.1.call-start = ((), (), s32[]{:S(2)}) async-start(), calls=%async_computation.25 | async-start | bytes 278528
  466.7 156.6 %reduce-scatter.36.cloned.1.call-start = ((), (), s32[]{:S(2)}) async-start(), calls=%async_computation.26 | async-start | bytes 278528
  469.6 218.3 %reduce-scatter.28.cloned.1.call-start = ((), (), s32[]{:S(2)}) async-start(), calls=%async_computation.22 | async-start | bytes 2228224 | tf_op jit(solution)/shard_map/reduce_scatter | solution.py:291
  472.9 279.7 %reduce-scatter.26.cloned.1.call-start = ((), (), s32[]{:S(2)}) async-start(), calls=%async_computation.21 | async-start | bytes 2228224 | tf_op jit(solution)/shard_map/reduce_scatter | solution.py:282
  476.3 340.6 %reduce-scatter.24.cloned.1.call-start = ((), (), s32[]{:S(2)}) async-start(), calls=%async_computation.20 | async-start | bytes 2228224 | tf_op jit(solution)/shard_map/reduce_scatter | solution.py:279
  479.8 412.9 %reduce-scatter.38.cloned.1.call-start = ((), (), s32[]{:S(2)}) async-start(), calls=%async_computation.27 | async-start | bytes 4456448
  494.0 487.9 %reduce-scatter.22.cloned.1.call-start = ((), (), s32[]{:S(2)}) async-start(), calls=%async_computation.19 | async-start | bytes 6684672 | tf_op jit(solution)/shard_map/reduce_scatter | solution.py:273
  500.1 590.9 %reduce-scatter.32.cloned.1.call-start = ((), (), s32[]{:S(2)}) async-start(), calls=%async_computation.24 | async-start | bytes 8912896 | tf_op jit(solution)/shard_map/reduce_scatter | solution.py:303
  507.3 692.6 %reduce-scatter.30.cloned.1.call-start = ((), (), s32[]{:S(2)}) async-start(), calls=%async_computation.23 | async-start | bytes 8912896 | tf_op jit(solution)/shard_map/reduce_scatter | solution.py:297
  514.5 701.0 %reduce-scatter.20.cloned.1.call-start = ((), (), s32[]{:S(2)}) async-start(), calls=%async_computation.18 | async-start | bytes 589824 | tf_op jit(solution)/shard_map/reduce_scatter | solution.py:237
  518.4 106.2 %collective-permute-start.2 = (bf16[1,1,192,1024]{3,2,1,0:T(8,128)(2,1)}, bf16[1,1,192,1024]{3,2,1,0:T(8,128)(2,1)S(1)}, u32[]{:S(2)}, u32[]{:S(2)}) collective-permute-start(bf16[1,1,192,1024]{3,2,1,0:T(8,128)(2,1)} %fusion.119), channel_id=1, source_target_pairs={{0,16},{16,0},{1,17},{17,1},{2,18},{18,2},{3,19},{19,3},{4,20},{20... | collective-permute-start | bytes 1179656 | tf_op jit(solution)/shard_map/ppermute | solution.py:16
  624.6 268.1 %copy-start.43 = (bf16[1,1,192,1024]{3,2,1,0:T(8,128)(2,1)}, bf16[1,1,192,1024]{3,2,1,0:T(8,128)(2,1)S(1)}, u32[]{:S(2)}) copy-start(bf16[1,1,192,1024]{3,2,1,0:T(8,128)(2,1)S(1)} %collective-permute-done.2) | copy-start | bytes 1179652
  894.0 321.5 %copy-start.44 = (bf16[1,1,192,1024]{3,2,1,0:T(8,128)(2,1)S(1)}, bf16[1,1,192,1024]{3,2,1,0:T(8,128)(2,1)}, u32[]{:S(2)}) copy-start(bf16[1,1,192,1024]{3,2,1,0:T(8,128)(2,1)} %copy-done.43) | copy-start | bytes 1179652
  (86 other events, 743.9 us)
Sparse Core Ops, SparseCore 0:
  10.2 59.2 all-gather.11
  71.8 60.4 all-gather.7
  134.5 40.8 all-gather.9
  177.4 40.5 all-gather.13
  219.9 40.1 all-gather.15
  262.2 73.6 all-gather.17
  338.0 73.1 all-gather.19
  455.3 51.2 reduce-scatter.39
  510.6 54.3 reduce-scatter.33
  568.9 54.2 reduce-scatter.35
  627.0 60.9 reduce-scatter.27
  692.0 60.5 reduce-scatter.25
  756.4 60.5 reduce-scatter.23
  821.2 71.4 reduce-scatter.37
  896.4 85.3 reduce-scatter.21
  986.4 104.6 reduce-scatter.31
  1095.5 104.3 reduce-scatter.29
  1202.6 12.7 reduce-scatter.19
where the time goes:
time: 1230 us; the launch traced here: 1220 us
  waiting for transfers between devices  801 us (65%)
  blocking collectives  183 us (15%)
  matrix products  117 us (10%)
  local copies, waits for them, and re-layouts  74.3 us (6%)
  other arithmetic  26.2 us (2%)
  between operations  18.2 us (1%)
    unnamed x22, waiting for transfers between devices  113 us
    reduce_scatter x1, waiting for transfers between devices, on_device(): lax.psum_scatter(grad_fc2.astype(jnp.bfloat16), 'dp', scatter_dimension=0...  107 us
    reduce_scatter x1, waiting for transfers between devices, on_device(): lax.psum_scatter(grad_fc1.astype(jnp.bfloat16), 'dp', scatter_dimension=0...  107 us
    reduce_scatter x1, waiting for transfers between devices, on_device(): lax.psum_scatter(grad_sqkv.astype(jnp.bfloat16), 'dp', scatter_dimension=...  86.8 us
    all_gather x1, waiting for transfers between devices, on_device(): lax.all_gather(fc1, 'dp', axis=1, tiled=True)  73.2 us
    reduce_scatter x1, waiting for transfers between devices, on_device(): lax.psum_scatter(grad_cout.astype(jnp.bfloat16), 'dp', scatter_dimension=...  63.3 us
    reduce_scatter x1, waiting for transfers between devices, on_device(): lax.psum_scatter(grad_cq.astype(jnp.bfloat16), 'dp', scatter_dimension=0,...  63.1 us
    reduce_scatter x1, waiting for transfers between devices, on_device(): lax.psum_scatter(grad_sout.astype(jnp.bfloat16), 'dp', scatter_dimension=...  62.7 us
  transfers between devices with their start and end apart: 21, of which 13 were waited for; matrix products, arithmetic and copies ran while one was open for 14% of the time, Pallas kernels for 0%

commit v1 on v0

--- a/solution.py
+++ b/solution.py
@@ -1,6 +1,11 @@
+import functools
+from types import SimpleNamespace
+
 import jax
 import jax.numpy as jnp
 from jax import lax
+from jax.experimental import pallas as pl
+from jax.experimental.pallas import tpu as pltpu
 from jax.sharding import PartitionSpec as P
 
 H = 16
@@ -324,6 +329,880 @@
     )
 
 
+Z = 4
+P_IN = 4
+L = 192
+D = 1024
+T = P_IN * L
+FL = 1024
+TILE = 32
+MESH = pl.DeviceIdType.MESH
+F32 = jnp.float32
+BF16 = jnp.bfloat16
+
+WEIGHTS = dict(
+    qkv=(256, 768, True),
+    so=(64, 1024, False),
+    ckv=(256, 512, True),
+    cq=(256, 256, True),
+    co=(64, 1024, False),
+    f1=(256, 1024, True),
+    f2=(256, 1024, False),
+)
+SEMS = 200
+
+
+def run_if(cond, fn):
+    if cond is None:
+        fn()
+    else:
+        pl.when(cond)(fn)
+
+
+def part(index, size, step=None):
+    return pl.ds(pl.multiple_of(index * size, size), size if step is None else step)
+
+
+def nn(left, right):
+    return jnp.dot(left, right, preferred_element_type=F32)
+
+
+def nt(left, right):
+    return lax.dot_general(left, right, (((1,), (1,)), ((), ())), preferred_element_type=F32)
+
+
+def tn(left, right):
+    return lax.dot_general(left, right, (((0,), (0,)), ((), ())), preferred_element_type=F32)
+
+
+def loop(count, body):
+    def step(index, carry):
+        body(index)
+        return carry
+
+    lax.fori_loop(0, count, step, 0)
+
+
+def gelu_pair(values):
+    bell = jnp.exp(-0.5 * values * values)
+    step = 1.0 / (1.0 + 0.3275911 * 0.7071067811865476 * jnp.abs(values))
+    series = step * (
+        0.254829592
+        + step
+        * (-0.284496736 + step * (1.421413741 + step * (-1.453152027 + step * 1.061405429)))
+    )
+    above = 0.5 * series * bell
+    below = jnp.where(values < 0, above, 1.0 - above)
+    return values * below, below + values * bell * 0.3989422804014327
+
+
+def whiten(rows):
+    center = rows - jnp.mean(rows, -1, keepdims=True)
+    scale = lax.rsqrt(jnp.mean(center * center, -1, keepdims=True) + EPSILON)
+    return center * scale, scale
+
+
+def whole_kernel(n_sec, mem_cols, *refs):
+    given = iter(refs)
+
+    def take(names):
+        return SimpleNamespace(**{name: next(given) for name in names})
+
+    def take_weights(**fields):
+        for name in WEIGHTS:
+            for field in fields:
+                setattr(getattr(wt, name), field, next(given))
+
+    wt = SimpleNamespace(**{name: SimpleNamespace() for name in WEIGHTS})
+    io = take(dict(prev=0, mem=0, cot=0, small=0))
+    take_weights(source=0)
+    vars(io).update(vars(take(dict(output=0, input_grad=0, memory_grad=0))))
+    take_weights(result=0)
+    vars(io).update(vars(take(dict(sums_out=0))))
+    buf = take(buffer_shapes(n_sec, mem_cols))
+    set_a, set_b, set_c = (take(REDUCE_SHAPES) for _ in range(3))
+    take_weights(weight=0, grad=0, to_diag=0, to_opp=0, near=0, far=0)
+    send_sems, recv_sems, local_sems = given
+
+    s = lax.axis_index("section")
+    d = lax.axis_index("dp")
+    z, q = d // P_IN, d % P_IN
+    x, c = q // 2, q % 2
+    end = (z % 3) == 0
+    mid = (z % 3) != 0
+    q_core = q + 1 - 2 * c
+    q_x = q + 2 - 4 * x
+    q_xc = q_x + 1 - 2 * c
+    z_adj = z + 1 - 2 * (z % 2)
+    z_opp = 3 - z
+    z_diag = (z + 2) % 4
+    dev_core, dev_x, dev_xc = (s, z * P_IN + q_core), (s, z * P_IN + q_x), (s, z * P_IN + q_xc)
+    dev_adj, dev_opp, dev_diag = (s, z_adj * P_IN + q), (s, z_opp * P_IN + q), (s, z_diag * P_IN + q)
+    in_plane = ((q_core, dev_core), (q_x, dev_x), (q_xc, dev_xc))
+
+    counter = [0]
+    started = []
+    local_counter = [0]
+
+    def slot(count=1):
+        counter[0] += count
+        return counter[0] - count
+
+    def remote(src, dst, k, device):
+        return pltpu.make_async_remote_copy(
+            src_ref=src, dst_ref=dst, send_sem=send_sems.at[k], recv_sem=recv_sems.at[k],
+            device_id=device, device_id_type=MESH,
+        )
+
+    def send(src, dst, k, device, cond=None):
+        copy = remote(src, dst, k, device)
+        run_if(cond, copy.start)
+        record = [copy, cond]
+        started.append(record)
+        return record
+
+    def sent(record):
+        run_if(record[1], record[0].wait_send)
+        started[:] = [other for other in started if other is not record]
+
+    def arrived(dst, k, cond=None):
+        run_if(cond, remote(dst, dst, k, dev_core).wait_recv)
+
+    def local(src, dst):
+        copy = pltpu.make_async_copy(src, dst, local_sems.at[local_counter[0]])
+        local_counter[0] += 1
+        copy.start()
+        return copy
+
+    def rows(rows_of, index):
+        return rows_of.at[part(index, L)]
+
+    for name, (count, _, by_column) in WEIGHTS.items():
+        weight = getattr(wt, name)
+        weight.count, weight.by_column = count, by_column
+        weight.to_use, weight.swap, weight.to_sum, weight.last = slot(5), slot(3), slot(5), slot(3)
+
+    def block(name, index):
+        return name.weight.at[part(index, name.count)]
+
+    def weight_send(name, src):
+        k = name.to_use
+        send(src, block(name, z), k, dev_adj)
+        send(src, block(name, z), k + 1, dev_opp, mid)
+        send(src, block(name, z), k + 2, dev_diag, end)
+
+    def weight_relay(name):
+        k = name.to_use
+        arrived(block(name, z_opp), k + 1, mid)
+        send(block(name, z_opp), block(name, z_opp), k + 3, dev_adj, mid)
+        arrived(block(name, z_diag), k + 2, mid)
+        send(block(name, z_diag), block(name, z_diag), k + 4, dev_adj, mid)
+
+    def weight_ready(name):
+        k = name.to_use
+        arrived(block(name, z_adj), k)
+        arrived(block(name, z_diag), k + 3, end)
+        arrived(block(name, z_opp), k + 4, end)
+
+
+    def swap_start(name):
+        size = name.count // P_IN
+        place = name.weight.at[part(z * P_IN + q, size)]
+        for j, (q_to, device) in enumerate(in_plane):
+            send(name.source.at[q_to], place, name.swap + j, device)
+        name.own_copy = local(name.source.at[q], place)
+
+    def swap_wait(name):
+        size = name.count // P_IN
+        for j, (q_from, _) in enumerate(in_plane):
+            arrived(name.weight.at[part(z * P_IN + q_from, size)], name.swap + j)
+        name.own_copy.wait()
+
+    def grad_block(name, index):
+        return name.grad.at[part(index, name.count)]
+
+    def grad_send(name):
+        k = name.to_sum
+        send(grad_block(name, z_opp), name.to_diag, k, dev_adj, end)
+        send(grad_block(name, z_diag), name.to_opp, k + 1, dev_adj, end)
+        send(grad_block(name, z_adj), name.near, k + 2, dev_adj)
+
+    def add_rows(count, body):
+        size = min(count, 64)
+        loop(count // size, lambda i: body(part(i, size)))
+
+    def grad_combine(name):
+        k = name.to_sum
+        count = name.count
+
+        def add(landed, index):
+            def one(place):
+                own = grad_block(name, index)[place, :].astype(F32)
+                landed[place, :] = (own + landed[place, :].astype(F32)).astype(BF16)
+
+            add_rows(count, one)
+
+        def work():
+            arrived(name.to_diag, k)
+            add(name.to_diag, z_diag)
+
+        run_if(mid, work)
+        send(name.to_diag, name.far, k + 3, dev_diag, mid)
+
+        def more():
+            arrived(name.to_opp, k + 1)
+            add(name.to_opp, z_opp)
+
+        run_if(mid, more)
+        send(name.to_opp, name.far, k + 4, dev_opp, mid)
+
+    result_copies = []
+
+    def grad_final(name):
+        k = name.to_sum
+        count = name.count
+        arrived(name.near, k + 2)
+        arrived(name.far, k + 3, end)
+        arrived(name.far, k + 4, mid)
+
+        def one(place):
+            total = grad_block(name, z)[place, :].astype(F32)
+            total = total + name.near[place, :].astype(F32)
+            total = total + name.far[place, :].astype(F32)
+            name.near[place, :] = total.astype(BF16)
+
+        add_rows(count, one)
+        if name.by_column:
+            size = count // P_IN
+            for j, (q_to, device) in enumerate(in_plane):
+                src = name.near.at[part(q_to, size)]
+                send(src, name.result.at[q], name.last + j, device)
+            src = name.near.at[part(q, size)]
+            result_copies.append(local(src, name.result.at[q]))
+        else:
+            result_copies.append(local(name.near, name.result))
+
+    def last_wait(name):
+        for j, (q_from, _) in enumerate(in_plane):
+            arrived(name.result.at[q_from], name.last + j)
+
+    def gather_start(name):
+        k = slot(3)
+        send(rows(name, q), rows(name, q), k, dev_x)
+        send(rows(name, q), rows(name, q), k + 1, dev_core)
+        return name, k
+
+    def gather_relay(ticket):
+        name, k = ticket
+        arrived(rows(name, q_x), k)
+        send(rows(name, q_x), rows(name, q_x), k + 2, dev_core)
+
+    def gather_ready(ticket):
+        name, k = ticket
+        arrived(rows(name, q_core), k + 1)
+        arrived(rows(name, q_xc), k + 2)
+
+    def gather_finish(ticket):
+        gather_relay(ticket)
+        gather_ready(ticket)
+
+    def reduce_start(which):
+        k = slot(3)
+        out = which.parts
+        first = send(rows(out, q_xc), rows(which.core, 1), k, dev_core)
+        second = send(rows(out, q_core), rows(which.core, 0), k + 1, dev_core)
+        return which, k, [first, second]
+
+    def reduce_relay(ticket):
+        which, k, records = ticket
+        out = which.parts
+        arrived(rows(which.core, 1), k)
+
+        def one(i):
+            mine = rows(out, q_x)
+            place = part(i, TILE)
+            total = mine[place, :].astype(F32) + rows(which.core, 1)[place, :].astype(F32)
+            mine[place, :] = total.astype(BF16)
+
+        loop(L // TILE, one)
+        records.append(send(rows(out, q_x), which.across, k + 2, dev_x))
+
+    def reduce_ready(ticket):
+        which, k, records = ticket
+        arrived(rows(which.core, 0), k + 1)
+        arrived(which.across, k + 2)
+
+    def reduced(ticket, place):
+        which = ticket[0]
+        total = rows(which.parts, q)[place, :].astype(F32)
+        total = total + rows(which.core, 0)[place, :].astype(F32)
+        return total + which.across[place, :].astype(F32)
+
+    def reduce_done(ticket):
+        for record in ticket[2]:
+            sent(record)
+
+    def spread_start(name, src):
+        k = slot(8)
+        place = name.at[q, z]
+        copy = None
+        if src is not None:
+            copy = local(src, place)
+        else:
+            src = place
+        send(src, place, k, dev_adj)
+        send(src, place, k + 1, dev_opp, mid)
+        send(src, place, k + 2, dev_diag, end)
+        return name, k, copy
+
+    def spread_relay(ticket):
+        name, k, copy = ticket
+        arrived(name.at[q, z_opp], k + 1, mid)
+        send(name.at[q, z_opp], name.at[q, z_opp], k + 3, dev_adj, mid)
+        arrived(name.at[q, z_diag], k + 2, mid)
+        send(name.at[q, z_diag], name.at[q, z_diag], k + 4, dev_adj, mid)
+        arrived(name.at[q, z_adj], k)
+        arrived(name.at[q, z_diag], k + 3, end)
+        arrived(name.at[q, z_opp], k + 4, end)
+        if copy is not None:
+            copy.wait()
+        for j, (_, device) in enumerate(in_plane):
+            send(name.at[q], name.at[q], k + 5 + j, device)
+
+    def spread_ready(ticket):
+        name, k, _ = ticket
+        for j, (q_from, _) in enumerate(in_plane):
+            arrived(name.at[q_from], k + 5 + j)
+
+    def lanes(j, size=256):
+        return part(j, size)
+
+    def matmul(left, right, dst, bias=None, bias_row=0, bias_at=0):
+        count = right.shape[1] // 256
+
+        def one(j):
+            tile = nn(left[...], right[:, lanes(j)])
+            if bias is not None:
+                tile = tile + bias[bias_row:bias_row + 1, part(j + bias_at, 256)]
+            dst[:, lanes(j)] = tile.astype(BF16)
+
+        loop(count, one)
+
+    def matmul_back(left, right, dst):
+        def one(j):
+            dst[:, lanes(j)] = nt(left[...], right[lanes(j), :]).astype(BF16)
+
+        loop(right.shape[0] // 256, one)
+
+    def weight_grad(left, right, name):
+        def one(j):
+            name.grad[lanes(j), :] = tn(left[:, lanes(j)], right[...]).astype(BF16)
+
+        loop(left.shape[1] // 256, one)
+
+    low_half = lax.broadcasted_iota(jnp.int32, (L, 128), 1) < 64
+    keep_low = low_half.astype(F32).astype(BF16)
+    keep_high = (1.0 - low_half.astype(F32)).astype(BF16)
+
+    def both(pair):
+        return jnp.concatenate([pair * keep_low, pair * keep_high], axis=0)
+
+    def merge(stacked):
+        return jnp.where(low_half, stacked[:L], stacked[L:])
+
+    def attention(qref, q_at, kref, k_at, v_at, causal, length_row, probs, dst):
+        def one(i):
+            r, pair = i // 2, i % 2
+            place = part(r, L)
+            query = both(qref[place, part(pair + q_at, 128)])
+            scores = nt(query, kref[place, part(pair + k_at, 128)]) * HD ** (-0.5)
+            key = lax.broadcasted_iota(jnp.int32, scores.shape, 1)
+            limit = buf.sva[r, z][length_row:length_row + 1, 0:1].astype(F32)
+            allowed = key.astype(F32) < limit
+            if causal:
+                at = lax.broadcasted_iota(jnp.int32, scores.shape, 0)
+                at = jnp.where(at < L, at, at - L)
+                allowed = allowed & (key <= at)
+            scores = jnp.where(allowed, scores, MASKED)
+            raised = jnp.exp(scores - jnp.max(scores, -1, keepdims=True))
+            weights = (raised * (1.0 / jnp.sum(raised, -1, keepdims=True))).astype(BF16)
+            probs[i] = weights
+            mixed = nn(weights, kref[place, part(pair + v_at, 128)])
+            dst[place, part(pair, 128)] = merge(mixed).astype(BF16)
+
+        loop(2 * P_IN, one)
+
+    def attention_back(qref, q_at, kref, k_at, v_at, probs, grad):
+        def one(i):
+            r, pair = i // 2, i % 2
+            place = part(r, L)
+            query = both(qref[place, part(pair + q_at, 128)])
+            key = kref[place, part(pair + k_at, 128)]
+            value = kref[place, part(pair + v_at, 128)]
+            mixed_grad = both(grad[place, part(pair, 128)])
+            weights = probs[i]
+            soft = weights.astype(F32)
+            grad_probs = nt(mixed_grad, value)
+            delta = jnp.sum(soft * grad_probs, -1, keepdims=True)
+            grad_scores = (soft * (grad_probs - delta)).astype(BF16)
+            scale = HD ** (-0.5)
+            grad_query = merge(nn(grad_scores, key)) * scale
+            grad_key = tn(grad_scores, query) * scale
+            grad_value = tn(weights, mixed_grad)
+            qref[place, part(pair + q_at, 128)] = grad_query.astype(BF16)
+            kref[place, part(pair + k_at, 128)] = grad_key.astype(BF16)
+            kref[place, part(pair + v_at, 128)] = grad_value.astype(BF16)
+
+        loop(2 * P_IN, one)
+
+    def column_sums(source, first, count, row, at):
+        def one(j):
+            values = source[:, part(j + first, 256)].astype(F32)
+            buf.sg[row:row + 1, part(j + at, 256)] = jnp.sum(values, 0, keepdims=True)
+
+        loop(count, one)
+
+    def norm(load, index, dst):
+        def one(i):
+            place = part(i, TILE)
+            normed, _ = whiten(load(place))
+            gain, shift = buf.vec[index:index + 1, :], buf.vec[index + 3:index + 4, :]
+            rows(dst, q)[place, :] = (normed * gain + shift).astype(BF16)
+
+        loop(L // TILE, one)
+
+    def norm_back(load, ticket, index, base, dst, low):
+        zero = jnp.zeros((1, D), F32)
+
+        def one(i, carry):
+            gain_sum, shift_sum, out_sum = carry
+            place = part(i, TILE)
+            normed, scale = whiten(load(place))
+            grad = reduced(ticket, place)
+            gained = grad * buf.vec[index:index + 1, :]
+            back = gained - jnp.mean(gained, -1, keepdims=True)
+            back = back - normed * jnp.mean(gained * normed, -1, keepdims=True)
+            total = base(place) + scale * back
+            if dst is not None:
+                dst[place, :] = total
+            rounded = total.astype(BF16)
+            low(place, rounded)
+            return (
+                gain_sum + jnp.sum(grad * normed, 0, keepdims=True),
+                shift_sum + jnp.sum(grad, 0, keepdims=True),
+                out_sum + jnp.sum(rounded.astype(F32), 0, keepdims=True),
+            )
+
+        gain_sum, shift_sum, out_sum = lax.fori_loop(0, L // TILE, one, (zero, zero, zero))
+        buf.sg[index:index + 1, :] = gain_sum
+        buf.sg[index + 3:index + 4, :] = shift_sum
+        return out_sum
+
+    gate = pltpu.get_barrier_semaphore()
+    partners = [device for _, device in in_plane] + [dev_adj, dev_opp, dev_diag]
+    partners += [((s + j) % n_sec, d) for j in range(1, n_sec)]
+    for device in partners:
+        pl.semaphore_signal(gate, inc=1, device_id=device, device_id_type=MESH)
+    pl.semaphore_wait(gate, len(partners))
+
+    sv = spread_start(buf.sva, io.small)
+    k_prev, k_cot, k_mem = slot(), slot(), slot(n_sec)
+    send(io.prev, buf.hb, k_prev, ((s + 1) % n_sec, d))
+    swap_start(wt.qkv)
+    mem_slot = rows(buf.m, q)
+    for j in range(1, n_sec):
+        send(io.mem, mem_slot.at[:, part(s, mem_cols)], k_mem + j, ((s + j) % n_sec, d))
+    mem_copy = local(io.mem, mem_slot.at[:, part(s, mem_cols)])
+    send(io.cot, rows(buf.e3, q), k_cot, ((s + n_sec - 1) % n_sec, d))
+    for weight in (wt.so, wt.co, wt.f2):
+        weight.own_copy = local(weight.source, block(weight, z))
+    swap_start(wt.ckv)
+    swap_start(wt.cq)
+
+    spread_relay(sv)
+    swap_wait(wt.qkv)
+    weight_send(wt.qkv, block(wt.qkv, z))
+    weight_send(wt.so, wt.so.source)
+    spread_ready(sv)
+
+    for tile in range(D // 128):
+        pair = buf.sva[2 * (tile % 2), tile // 2].astype(F32)
+        pair = pair + buf.sva[2 * (tile % 2) + 1, tile // 2].astype(F32)
+        buf.vec[:, tile * 128:(tile + 1) * 128] = pair
+    half = lax.broadcasted_iota(jnp.int32, (16, 128), 1) < 64
+    even = (jnp.zeros((16, 128), jnp.int32) + c) == 0
+    buf.bias[...] = jnp.zeros((8, D), F32)
+    for kind in range(2):
+        for tile in range(2):
+            first = buf.sva[x, tile + 2 * kind].astype(F32)
+            second = buf.sva[2 + x, tile + 2 * kind].astype(F32)
+            lower = jnp.where(even, first, pltpu.roll(first, 64, 1))
+            upper = jnp.where(even, pltpu.roll(second, 64, 1), second)
+            both_heads = jnp.where(half, lower, upper)
+            for which in range(2):
+                at = 512 * kind + 128 * tile
+                buf.bias[which:which + 1, at:at + 128] = both_heads[9 + which:10 + which]
+    for tile in range(Z):
+        unit = buf.sva[q, tile].astype(F32)
+        buf.bias[2:3, 256 * tile:256 * tile + 128] = unit[11:12]
+        buf.bias[2:3, 256 * tile + 128:256 * tile + 256] = unit[12:13]
+    buf.sg[...] = jnp.zeros((16, D), F32)
+
+    arrived(buf.hb, k_prev)
+
+    def hidden(place):
+        return buf.hb[place, :].astype(F32)
+
+    norm(hidden, 0, buf.a1)
+    a1 = gather_start(buf.a1)
+    swap_wait(wt.ckv)
+    swap_wait(wt.cq)
+    weight_send(wt.ckv, block(wt.ckv, z))
+    weight_send(wt.cq, block(wt.cq, z))
+    weight_send(wt.co, wt.co.source)
+    for j in range(1, n_sec):
+        origin = (s + n_sec - j) % n_sec
+        arrived(mem_slot.at[:, part(origin, mem_cols)], k_mem + j)
+    mem_copy.wait()
+    gather_relay(a1)
+    memory = gather_start(buf.m)
+    swap_start(wt.f1)
+    gather_ready(a1)
+    weight_relay(wt.qkv)
+    weight_ready(wt.qkv)
+    matmul(buf.a1, wt.qkv.weight, buf.qkv, buf.bias, 0)
+    weight_relay(wt.so)
+    gather_finish(memory)
+    attention(buf.qkv, 0, buf.qkv, 2, 4, True, 13, buf.p1, buf.o1)
+    wt.so.own_copy.wait()
+    weight_ready(wt.so)
+    matmul(buf.o1, wt.so.weight, set_a.parts)
+    step = reduce_start(set_a)
+    swap_wait(wt.f1)
+    weight_send(wt.f1, block(wt.f1, z))
+    weight_relay(wt.ckv)
+    reduce_relay(step)
+    weight_ready(wt.ckv)
+    matmul(buf.m, wt.ckv.weight, buf.kv, buf.bias, 1, 1)
+    reduce_ready(step)
+
+    def after_self(i):
+        place = part(i, TILE)
+        buf.h1[place, :] = hidden(place) + (reduced(step, place) + buf.vec[6:7, :])
+
+    loop(L // TILE, after_self)
+    norm(lambda place: buf.h1[place, :], 1, buf.a2)
+    a2 = gather_start(buf.a2)
+    reduce_done(step)
+
+    weight_send(wt.f2, wt.f2.source)
+    weight_relay(wt.cq)
+    weight_relay(wt.co)
+    arrived(rows(buf.e3, q), k_cot)
+    gather_finish(a2)
+    e3 = gather_start(buf.e3)
+    weight_ready(wt.cq)
+    matmul(buf.a2, wt.cq.weight, buf.q2, buf.bias, 1)
+    attention(buf.q2, 0, buf.kv, 0, 2, False, 14, buf.p2, buf.o2)
+    wt.co.own_copy.wait()
+    weight_ready(wt.co)
+    matmul(buf.o2, wt.co.weight, set_b.parts)
+    step = reduce_start(set_b)
+    gather_finish(e3)
+    reduce_relay(step)
+    reduce_ready(step)
+
+    def after_cross(i):
+        place = part(i, TILE)
+        buf.h2[place, :] = buf.h1[place, :] + (reduced(step, place) + buf.vec[7:8, :])
+
+    loop(L // TILE, after_cross)
+    norm(lambda place: buf.h2[place, :], 2, buf.a3)
+    a3 = gather_start(buf.a3)
+    reduce_done(step)
+
+    weight_relay(wt.f1)
+    gather_finish(a3)
+    weight_ready(wt.f1)
+
+    def units(j):
+        value = nn(buf.a3[...], wt.f1.weight[:, lanes(j)]) + buf.bias[2:3, lanes(j)]
+        activ, slope = gelu_pair(value)
+        buf.g[:, lanes(j)] = activ.astype(BF16)
+        buf.gp[:, lanes(j)] = slope.astype(BF16)
+
+    loop(FL // 256, units)
+    weight_grad(buf.g, buf.e3, wt.f2)
+    grad_send(wt.f2)
+    weight_relay(wt.f2)
+    wt.f2.own_copy.wait()
+    weight_ready(wt.f2)
+
+    def units_back(j):
+        value = nt(buf.e3[...], wt.f2.weight[lanes(j), :])
+        low = (value * buf.gp[:, lanes(j)].astype(F32)).astype(BF16)
+        buf.gp[:, lanes(j)] = low
+        buf.sg[10:11, lanes(j)] = jnp.sum(low.astype(F32), 0, keepdims=True)
+
+    loop(FL // 256, units_back)
+    matmul_back(buf.gp, wt.f1.weight, set_a.parts)
+    step = reduce_start(set_a)
+    weight_grad(buf.a3, buf.gp, wt.f1)
+    grad_send(wt.f1)
+    reduce_relay(step)
+    matmul(buf.g, wt.f2.weight, set_c.parts)
+    final = reduce_start(set_c)
+    reduce_ready(step)
+    zero = jnp.zeros((1, D), F32)
+
+    def cot_sum(i, carry):
+        return carry + jnp.sum(rows(buf.e3, q)[part(i, TILE), :].astype(F32), 0, keepdims=True)
+
+    buf.sg[8:9, :] = lax.fori_loop(0, L // TILE, cot_sum, zero)
+
+    def store(name):
+        def low(place, value):
+            rows(name, q)[place, :] = value
+
+        return low
+
+    buf.sg[7:8, :] = norm_back(
+        lambda place: buf.h2[place, :], step, 2,
+        lambda place: rows(buf.e3, q)[place, :].astype(F32), buf.dh, store(buf.e2),
+    )
+    e2 = gather_start(buf.e2)
+    reduce_done(step)
+    reduce_relay(final)
+    grad_combine(wt.f2)
+    gather_finish(e2)
+
+    matmul_back(buf.e2, wt.co.weight, buf.do)
+    attention_back(buf.q2, 0, buf.kv, 0, 2, buf.p2, buf.do)
+    matmul_back(buf.q2, wt.cq.weight, set_b.parts)
+    step = reduce_start(set_b)
+    weight_grad(buf.o2, buf.e2, wt.co)
+    grad_send(wt.co)
+    weight_grad(buf.a2, buf.q2, wt.cq)
+    grad_send(wt.cq)
+    reduce_relay(step)
+    weight_grad(buf.m, buf.kv, wt.ckv)
+    grad_send(wt.ckv)
+    matmul_back(buf.kv, wt.ckv.weight, set_a.parts)
+    mem_step = reduce_start(set_a)
+    reduce_ready(final)
+
+    def finish(i):
+        place = part(i, TILE)
+        total = buf.h2[place, :] + (reduced(final, place) + buf.vec[8:9, :])
+        buf.stage[place, :] = total.astype(BF16)
+
+    loop(L // TILE, finish)
+    result_copies.append(local(buf.stage, io.output))
+    reduce_done(final)
+    column_sums(buf.q2, 0, 1, 9, 2)
+    column_sums(buf.kv, 1, 1, 9, 3)
+    reduce_ready(step)
+    buf.sg[6:7, :] = norm_back(
+        lambda place: buf.h1[place, :], step, 1,
+        lambda place: buf.dh[place, :], buf.dh, store(buf.e1),
+    )
+    e1 = gather_start(buf.e1)
+    reduce_done(step)
+    reduce_relay(mem_step)
+    grad_combine(wt.f1)
+    gather_finish(e1)
+
+    matmul_back(buf.e1, wt.so.weight, buf.do)
+    attention_back(buf.qkv, 0, buf.qkv, 2, 4, buf.p1, buf.do)
+    matmul_back(buf.qkv, wt.qkv.weight, set_b.parts)
+    step = reduce_start(set_b)
+    weight_grad(buf.o1, buf.e1, wt.so)
+    grad_send(wt.so)
+    weight_grad(buf.a1, buf.qkv, wt.qkv)
+    grad_send(wt.qkv)
+    reduce_relay(step)
+    column_sums(buf.qkv, 0, 1, 9, 0)
+    column_sums(buf.qkv, 2, 1, 9, 1)
+
+    reduce_ready(mem_step)
+
+    def memory_row(i):
+        place = part(i, TILE)
+        buf.mb[place, :] = reduced(mem_step, place).astype(BF16)
+
+    loop(L // TILE, memory_row)
+    k_back = slot(n_sec)
+    for j in range(1, n_sec):
+        to = (s + j) % n_sec
+        send(buf.mb.at[:, part(to, mem_cols)], buf.ml.at[j], k_back + j, (to, d))
+    grad_combine(wt.co)
+    grad_combine(wt.cq)
+    reduce_ready(step)
+
+    def store_stage(place, value):
+        buf.ig[place, :] = value
+
+    norm_back(
+        hidden, step, 0, lambda place: buf.dh[place, :], None, store_stage,
+    )
+    k_in = slot()
+    send(buf.ig, io.input_grad, k_in, ((s + n_sec - 1) % n_sec, d))
+    buf.sga[q, z] = buf.sg[...].astype(BF16)
+    sums = spread_start(buf.sga, None)
+    grad_combine(wt.ckv)
+    grad_final(wt.f2)
+    grad_final(wt.f1)
+    spread_relay(sums)
+    for j in range(1, n_sec):
+        arrived(buf.ml.at[j], k_back + j)
+
+    def memory_total(i):
+        place = part(i, TILE)
+        total = buf.mb[place, part(s, mem_cols)].astype(F32)
+        for j in range(1, n_sec):
+            total = total + buf.ml[j, place, :].astype(F32)
+        buf.mo[place, :] = total.astype(BF16)
+
+    loop(L // TILE, memory_total)
+    result_copies.append(local(buf.mo, io.memory_grad))
+    grad_combine(wt.so)
+    grad_combine(wt.qkv)
+    for weight in (wt.co, wt.cq, wt.ckv, wt.so, wt.qkv):
+        grad_final(weight)
+    spread_ready(sums)
+    result_copies.append(local(buf.sga, io.sums_out))
+    for weight in (wt.qkv, wt.ckv, wt.cq, wt.f1):
+        last_wait(weight)
+    arrived(io.input_grad, k_in)
+    for copy in result_copies:
+        copy.wait()
+    for record in list(started):
+        sent(record)
+    assert counter[0] <= SEMS
+
+
+def buffer_shapes(n_sec, mem_cols):
+    tokens, row = (T, D), (L, D)
+    shapes = dict(
+        sva=(P_IN, Z, 16, 128),
+        sga=(P_IN, Z, 16, D),
+        hb=row, ig=row, stage=row, mb=row,
+        ml=(n_sec, L, mem_cols),
+        mo=(L, mem_cols),
+        qkv=(T, 768), q2=(T, 256), kv=(T, 512), o1=(T, 256), o2=(T, 256), do=(T, 256),
+        p1=(2 * P_IN, 2 * L, L), p2=(2 * P_IN, 2 * L, L),
+        g=(T, FL), gp=(T, FL),
+        a1=tokens, a2=tokens, a3=tokens, m=tokens, e3=tokens, e2=tokens, e1=tokens,
+    )
+    exact = dict(vec=(16, D), bias=(8, D), sg=(16, D), h1=row, h2=row, dh=row)
+    kinds = {name: pltpu.VMEM(shape, BF16) for name, shape in shapes.items()}
+    kinds.update({name: pltpu.VMEM(shape, F32) for name, shape in exact.items()})
+    return kinds
+
+
+REDUCE_SHAPES = dict(
+    parts=pltpu.VMEM((T, D), BF16),
+    core=pltpu.VMEM((2 * L, D), BF16),
+    across=pltpu.VMEM((L, D), BF16),
+)
+
+
+def scratch_of(n_sec, mem_cols):
+    scratch = list(buffer_shapes(n_sec, mem_cols).values())
+    scratch += 3 * list(REDUCE_SHAPES.values())
+    for count, columns, _ in WEIGHTS.values():
+        scratch += 2 * [pltpu.VMEM((Z * count, columns), BF16)]
+        scratch += 4 * [pltpu.VMEM((count, columns), BF16)]
+    return scratch + [
+        pltpu.SemaphoreType.DMA((SEMS,)),
+        pltpu.SemaphoreType.DMA((SEMS,)),
+        pltpu.SemaphoreType.DMA((32,)),
+    ]
+
+
+def on_device_planes(
+    prev_act, memory, out_cot, tgt_len, src_len, norm_gain, norm_bias, self_qkv, self_qv_bias,
+    self_out, cross_q, cross_kv, cross_qv_bias, cross_out, out_bias, fc1, fc1_bias, fc2,
+):
+    n_sec = lax.axis_size("section")
+    d = lax.axis_index("dp")
+    mem_cols = memory.shape[2]
+    pieces = jnp.concatenate([norm_gain[0], norm_bias[0], out_bias[0]], 0)
+    odd = (d % 2).astype(BF16)
+    spaced = jnp.concatenate([pieces * (1 - odd), pieces * odd], 1)
+    ones = jnp.ones((1, 128), BF16)
+    small = jnp.concatenate(
+        [
+            spaced,
+            self_qv_bias,
+            cross_qv_bias,
+            fc1_bias.reshape(2, 128),
+            ones * tgt_len.astype(BF16)[:, None],
+            ones * src_len.astype(BF16)[:, None],
+            ones,
+        ],
+        0,
+    )
+
+    def to_columns(weight, groups, unit):
+        split = weight[0].reshape(-1, groups, Z, P_IN, unit)
+        return split.transpose(3, 0, 1, 2, 4).reshape(P_IN, -1, groups * Z * unit)
+
+    def from_columns(grad, groups, unit):
+        split = grad.reshape(P_IN, -1, groups, Z, unit)
+        return split.transpose(1, 2, 3, 0, 4).reshape(1, -1, groups * Z * P_IN * unit).astype(F32)
+
+    operands = (
+        prev_act[0, 0], memory[0], out_cot[0, 0], small,
+        to_columns(self_qkv, 3, HD), self_out[0], to_columns(cross_kv, 2, HD),
+        to_columns(cross_q, 1, HD), cross_out[0], to_columns(fc1, 1, FL // Z), fc2[0],
+    )
+    out_shapes = [(L, D), (L, D), (L, mem_cols)]
+    for count, columns, by_column in WEIGHTS.values():
+        out_shapes.append((P_IN, count // P_IN, columns) if by_column else (count, columns))
+    out_shapes.append((P_IN, Z, 16, D))
+    results = pl.pallas_call(
+        functools.partial(whole_kernel, n_sec, mem_cols),
+        out_shape=[jax.ShapeDtypeStruct(shape, BF16) for shape in out_shapes],
+        in_specs=[pl.BlockSpec(memory_space=pl.ANY)] * len(operands),
+        out_specs=[pl.BlockSpec(memory_space=pl.ANY)] * len(out_shapes),
+        scratch_shapes=scratch_of(n_sec, mem_cols),
+        compiler_params=pltpu.CompilerParams(
+            collective_id=0, has_side_effects=True, vmem_limit_bytes=63 * 2**20
+        ),
+        cost_estimate=pl.CostEstimate(
+            flops=21 * 10**9, bytes_accessed=20 * 2**20, transcendentals=3 * 10**6
+        ),
+    )(*operands)
+    output, input_grad, memory_grad, g_qkv, g_so, g_ckv, g_cq, g_co, g_f1, g_f2, sums = results
+    sums = sums.astype(F32)
+    by_feature = jnp.sum(sums[:, :, :9], (0, 1))
+    own = lax.dynamic_slice_in_dim(by_feature, d * 64, 64, 1)
+    by_head = jnp.sum(sums[:, :, 9], 1).reshape(P_IN, 4, Z, 64).transpose(1, 2, 0, 3)
+    by_head = by_head.reshape(2, 2048)
+    by_unit = jnp.sum(sums[:, :, 10], 1).reshape(P_IN, Z, 256).transpose(1, 0, 2).reshape(1, 4096)
+    own_head = lax.dynamic_slice_in_dim(by_head, d * 128, 128, 1)
+    own_unit = lax.dynamic_slice_in_dim(by_unit, d * 256, 256, 1)
+    return (
+        output[None, None],
+        input_grad[None, None],
+        memory_grad[None],
+        own[None, 0:3],
+        own[None, 3:6],
+        from_columns(g_qkv, 3, HD),
+        own_head[0:1],
+        g_so[None].astype(F32),
+        from_columns(g_cq, 1, HD),
+        from_columns(g_ckv, 2, HD),
+        own_head[1:2],
+        g_co[None].astype(F32),
+        own[None, 6:9],
+        from_columns(g_f1, 1, FL // Z),
+        own_unit,
+        g_f2[None].astype(F32),
+    )
+
+
 def solution(mesh):
     in_specs = (
         P("section", "dp", None, None),
@@ -363,6 +1242,8 @@
         P("section", "dp"),
         P("section", "dp", None),
     )
+    planes = Z * P_IN
+    fits = mesh.shape["dp"] == planes
     return jax.shard_map(
-        on_device, mesh=mesh, in_specs=in_specs, out_specs=out_specs, check_vma=False
-    )
+        on_device_planes if fits else on_device, mesh=mesh, in_specs=in_specs, out_specs=out_specs, check_vma=False
+    )

time: 1230 us -> 348 us (0.28)
  waiting for transfers between devices: 801 us -> 0 us
  Pallas kernels: 0 us -> 307 us
  blocking collectives: 183 us -> 0 us
  matrix products: 117 us -> 0 us
  local copies, waits for them, and re-layouts: 74.3 us -> 26.9 us
  other arithmetic: 26.2 us -> 4.77 us
  between operations: 18.2 us -> 2.22 us
    reduce_scatter x7 -> x0, waiting for transfers between devices: 503 us -> none  [the longest x1 107 us: on_device(): lax.psum_scatter(grad_fc2.astype(jnp.bfloat16), 'dp', scatter_dimension=0...]
    pallas_call x0 -> x1, Pallas kernels: none -> 307 us  [on_device_planes(): pl.pallas_call(functools.partial(whole_kernel, n_sec, mem_cols), out_shap...]
    all_gather x7 -> x0, waiting for transfers between devices: 184 us -> none  [the longest x1 73.2 us: on_device(): lax.all_gather(fc1, 'dp', axis=1, tiled=True)]
    all_gather x7 -> x0, blocking collectives: 129 us -> none  [the longest x1 25.2 us: on_device(): lax.all_gather(out_bias, 'dp', axis=2, tiled=True)]
    unnamed x22 -> x0, waiting for transfers between devices: 113 us -> none
    dot_general x31 -> x0, matrix products: 111 us -> none  [the longest x7 33.5 us: product(): return jnp.dot(left, right, preferred_element_type=jnp.float32)]
    unnamed x1 -> x0, blocking collectives: 54.2 us -> none
    slice x9 -> x2, local copies, waits for them, and re-layouts: 34 us -> 0.61 us  [the longest x1 0.52 us: on_device_planes(): own_head[1:2]]
  transfers between devices with their start and end apart: 21 -> 0, of which waited for: 13 -> 0; matrix products, arithmetic and copies ran while one was open for 14% -> 0% of each run, Pallas kernels for 0% -> 0%
where the time goes in v1:
time: 348 us; the launch traced here: 341 us
  Pallas kernels  307 us (88%)
  local copies, waits for them, and re-layouts  26.9 us (8%)
  other arithmetic  4.77 us (1%)
    pallas_call x1, Pallas kernels, on_device_planes(): pl.pallas_call(functools.partial(whole_kernel, n_sec, mem_cols), out_shap...  307 us
    convert_element_type x12, local copies, waits for them, and re-layouts, from_columns(): split.transpose(1, 2, 3, 0, 4).reshape(1, -1, groups * Z * P_IN * unit)  12 us

profile of v1, /device:TPU:1, one launch (start us, length us, event | category | flops | bytes accessed | tf_op | source)
XLA Modules:
  0.0 341.4 jit_solution(2648769025568131436)
XLA Ops:
  0.7 0.7 fusion.1
  2.8 0.7 reduce.2
  3.5 1.9 concatenate.11.refs_3_
  5.4 1.5 reshape_squeeze.12
  7.3 1.2 reshape.144.refs_4_
  8.5 0.4 reshape_squeeze.15
  9.1 1.2 reshape.147.refs_9_
  10.2 0.5 reshape_squeeze.13
  11.0 1.0 reshape.145.refs_6_
  12.3 0.9 reshape.146.refs_7_
  13.2 307.5 %shard_map.297 = (bf16[192,1024]{1,0:T(8,128)(2,1)}, bf16[192,1024]{1,0:T(8,128)(2,1)}, bf16[192,512]{1,0:T(8,128)(2,1)}, bf16[4,64,768]{2,1,0:T(8,128)(2,1)}, b...) custom-call(bf16[192,1024]{1,0:T(8,128)(2,1)} %bitcast.70, ...), custom_call_target="tpu_custom_call" | custom-call | flops 20999999488 | bytes 20971520 | tf_op jit(solution)/shard_map/pallas_call | solution.py:1164
  320.7 1.8 bitcast_convert_fusion.1
  322.5 1.8 reshape.159
  324.3 1.0 copy.54
  325.3 2.0 reshape.152
  327.3 0.5 reshape.162
  327.8 0.7 copy.58
  328.5 1.5 reshape.157
  330.0 0.6 reshape.161
  330.6 0.7 copy.57
  331.3 1.6 reshape.155
  333.1 0.3 copy.56
  333.5 1.1 reshape.154
  335.2 0.5 fusion.3
  335.8 0.6 broadcast_in_dim.30
  336.4 0.6 broadcast_in_dim.31
  337.0 0.6 broadcast_in_dim.32
  337.6 0.6 constant_dynamic-slice_fusion.1
  338.1 1.1 bitcast_convert_fusion
  339.2 0.7 copy.72
  340.0 0.7 copy.73
  340.7 0.7 copy.74
  (41 shorter events, 2.1 us)
Async XLA Ops:
  6.9 1.5 copy-start.3
  8.5 1.8 copy-start.6
  10.2 1.8 copy-start.9
  325.3 2.0 copy-start.2
  328.5 1.5 copy-start.7
  330.6 2.3 copy-start.10
  332.9 1.7 copy-start.1
  334.6 3.5 %copy-start = (bf16[256,1024]{1,0:T(8,128)(2,1)S(1)}, bf16[256,1024]{1,0:T(8,128)(2,1)}, u32[]{:S(2)}) copy-start(bf16[256,1024]{1,0:T(8,128)(2,1)} %get-tuple-element.37) | copy-start | bytes 1572868
  334.7 4.5 %copy-start.5 = (bf16[192,1024]{1,0:T(8,128)(2,1)S(1)}, bf16[192,1024]{1,0:T(8,128)(2,1)}, u32[]{:S(2)}) copy-start(bf16[192,1024]{1,0:T(8,128)(2,1)} %get-tuple-element.27) | copy-start | bytes 1179652
  335.7 4.3 %copy-start.4 = (bf16[192,1024]{1,0:T(8,128)(2,1)S(1)}, bf16[192,1024]{1,0:T(8,128)(2,1)}, u32[]{:S(2)}) copy-start(bf16[192,1024]{1,0:T(8,128)(2,1)} %get-tuple-element.28) | copy-start | bytes 1179652
  338.1 2.6 copy-start.8

commit v2 on v1

--- a/solution.py
+++ b/solution.py
@@ -349,7 +349,7 @@
     f1=(256, 1024, True),
     f2=(256, 1024, False),
 )
-SEMS = 200
+SEMS = 240
 
 
 def run_if(cond, fn):
@@ -414,7 +414,12 @@
                 setattr(getattr(wt, name), field, next(given))
 
     wt = SimpleNamespace(**{name: SimpleNamespace() for name in WEIGHTS})
-    io = take(dict(prev=0, mem=0, cot=0, small=0))
+    io = take(
+        dict(
+            prev=0, mem=0, cot=0, tgt=0, src=0, gain=0, shift=0, out_bias=0,
+            self_bias=0, cross_bias=0, unit_bias=0,
+        )
+    )
     take_weights(source=0)
     vars(io).update(vars(take(dict(output=0, input_grad=0, memory_grad=0))))
     take_weights(result=0)
@@ -422,6 +427,8 @@
     buf = take(buffer_shapes(n_sec, mem_cols))
     set_a, set_b, set_c = (take(REDUCE_SHAPES) for _ in range(3))
     take_weights(weight=0, grad=0, to_diag=0, to_opp=0, near=0, far=0)
+    for weight in (wt.qkv, wt.ckv, wt.cq):
+        weight.raw, weight.sorted = next(given), next(given)
     send_sems, recv_sems, local_sems = given
 
     s = lax.axis_index("section")
@@ -508,15 +515,71 @@
     def swap_start(name):
         size = name.count // P_IN
         place = name.weight.at[part(z * P_IN + q, size)]
-        for j, (q_to, device) in enumerate(in_plane):
-            send(name.source.at[q_to], place, name.swap + j, device)
-        name.own_copy = local(name.source.at[q], place)
+        name.swapped = [
+            send(name.sorted.at[q_to], place, name.swap + j, device)
+            for j, (q_to, device) in enumerate(in_plane)
+        ]
+        name.own_copy = [local(name.sorted.at[q], place)]
 
     def swap_wait(name):
         size = name.count // P_IN
         for j, (q_from, _) in enumerate(in_plane):
             arrived(name.weight.at[part(z * P_IN + q_from, size)], name.swap + j)
-        name.own_copy.wait()
+        for copy in name.own_copy:
+            copy.wait()
+        for record in name.swapped:
+            sent(record)
+
+    def halves(first, second, odd):
+        if odd:
+            first = pltpu.roll(first, 64, 1)
+        else:
+            second = pltpu.roll(second, 64, 1)
+        lane = lax.broadcasted_iota(jnp.int32, first.shape, 1)
+        return jnp.where(lane < 64, first, second)
+
+    def tile_of(index):
+        return slice(index * 128, index * 128 + 128)
+
+    def sort_columns(name):
+        for q_to in range(P_IN):
+            for tile in range(name.sorted.shape[2] // 128):
+                at = 4 * tile + q_to // 2
+                first = name.raw[:, tile_of(at)].astype(F32)
+                second = name.raw[:, tile_of(at + 2)].astype(F32)
+                name.sorted[q_to, :, tile_of(tile)] = halves(first, second, q_to % 2).astype(BF16)
+
+    def unsort_columns(name):
+        for tile in range(name.raw.shape[1] // 128):
+            group, u = tile // 8, tile % 8
+            at = 2 * group + u // 4
+            first = name.sorted[2 * (u % 2), :, tile_of(at)].astype(F32)
+            second = name.sorted[2 * (u % 2) + 1, :, tile_of(at)].astype(F32)
+            name.raw[:, tile_of(tile)] = halves(first, second, (u // 2) % 2).astype(BF16)
+
+    unit_swap, unit_last = slot(3 * Z), slot(3 * Z)
+
+    def unit_columns(rows_of, tile, q_at):
+        return rows_of.at[:, part(tile * P_IN + q_at, 256)]
+
+    def unit_swap_start():
+        size = wt.f1.count // P_IN
+        place = wt.f1.weight.at[part(z * P_IN + q, size)]
+        wt.f1.own_copy = []
+        for tile in range(Z):
+            at = place.at[:, part(tile, 256)]
+            for j, (q_to, device) in enumerate(in_plane):
+                send(unit_columns(wt.f1.source, tile, q_to), at, unit_swap + 3 * tile + j, device)
+            wt.f1.own_copy.append(local(unit_columns(wt.f1.source, tile, q), at))
+
+    def unit_swap_wait():
+        size = wt.f1.count // P_IN
+        for tile in range(Z):
+            for j, (q_from, _) in enumerate(in_plane):
+                place = wt.f1.weight.at[part(z * P_IN + q_from, size)]
+                arrived(place.at[:, part(tile, 256)], unit_swap + 3 * tile + j)
+        for copy in wt.f1.own_copy:
+            copy.wait()
 
     def grad_block(name, index):
         return name.grad.at[part(index, name.count)]
@@ -572,19 +635,37 @@
             name.near[place, :] = total.astype(BF16)
 
         add_rows(count, one)
-        if name.by_column:
-            size = count // P_IN
+        size = count // P_IN
+        if name is wt.f1:
+            for tile in range(Z):
+                for j, (q_to, device) in enumerate(in_plane):
+                    src = name.near.at[part(q_to, size), part(tile, 256)]
+                    dst = unit_columns(name.result, tile, q)
+                    send(src, dst, unit_last + 3 * tile + j, device)
+                src = name.near.at[part(q, size), part(tile, 256)]
+                result_copies.append(local(src, unit_columns(name.result, tile, q)))
+        elif name.by_column:
             for j, (q_to, device) in enumerate(in_plane):
                 src = name.near.at[part(q_to, size)]
-                send(src, name.result.at[q], name.last + j, device)
+                send(src, name.sorted.at[q], name.last + j, device)
             src = name.near.at[part(q, size)]
-            result_copies.append(local(src, name.result.at[q]))
+            name.own_copy = [local(src, name.sorted.at[q])]
         else:
             result_copies.append(local(name.near, name.result))
 
     def last_wait(name):
         for j, (q_from, _) in enumerate(in_plane):
-            arrived(name.result.at[q_from], name.last + j)
+            arrived(name.sorted.at[q_from], name.last + j)
+        for copy in name.own_copy:
+            copy.wait()
+        unsort_columns(name)
+        result_copies.append(local(name.raw, name.result))
+
+    def unit_last_wait():
+        for tile in range(Z):
+            for j, (q_from, _) in enumerate(in_plane):
+                place = unit_columns(wt.f1.result, tile, q_from)
+                arrived(place, unit_last + 3 * tile + j)
 
     def gather_start(name):
         k = slot(3)
@@ -798,26 +879,46 @@
         buf.sg[index + 3:index + 4, :] = shift_sum
         return out_sum
 
+    raw_copies = [local(weight.source, weight.raw) for weight in (wt.qkv, wt.ckv, wt.cq)]
+    low_lanes = lax.broadcasted_iota(jnp.int32, (3, 128), 1) < 64
+    even_lanes = (jnp.zeros((3, 128), jnp.int32) + c) == 0
+    for row, pieces in ((0, io.gain), (3, io.shift), (6, io.out_bias)):
+        value = pieces[...].astype(F32)
+        twice = jnp.concatenate([value, value], 1)
+        buf.sg[row:row + 3, 0:128] = jnp.where(low_lanes == even_lanes, twice, 0.0)
+    buf.sg[9:10, 0:128] = io.self_bias[...].astype(F32)
+    buf.sg[10:11, 0:128] = io.cross_bias[...].astype(F32)
+    buf.sg[11:12, 0:128] = io.unit_bias[:, 0:128].astype(F32)
+    buf.sg[12:13, 0:128] = io.unit_bias[:, 128:256].astype(F32)
+    buf.sg[13:14, 0:128] = jnp.zeros((1, 128), F32) + io.tgt[0].astype(F32)
+    buf.sg[14:15, 0:128] = jnp.zeros((1, 128), F32) + io.src[0].astype(F32)
+    buf.sg[15:16, 0:128] = jnp.zeros((1, 128), F32)
+    buf.sva[q, z] = buf.sg[:, 0:128].astype(BF16)
+
     gate = pltpu.get_barrier_semaphore()
     partners = [device for _, device in in_plane] + [dev_adj, dev_opp, dev_diag]
     partners += [((s + j) % n_sec, d) for j in range(1, n_sec)]
     for device in partners:
         pl.semaphore_signal(gate, inc=1, device_id=device, device_id_type=MESH)
+    raw_copies[0].wait()
+    sort_columns(wt.qkv)
     pl.semaphore_wait(gate, len(partners))
 
-    sv = spread_start(buf.sva, io.small)
+    sv = spread_start(buf.sva, None)
+    swap_start(wt.qkv)
     k_prev, k_cot, k_mem = slot(), slot(), slot(n_sec)
     send(io.prev, buf.hb, k_prev, ((s + 1) % n_sec, d))
-    swap_start(wt.qkv)
     mem_slot = rows(buf.m, q)
     for j in range(1, n_sec):
         send(io.mem, mem_slot.at[:, part(s, mem_cols)], k_mem + j, ((s + j) % n_sec, d))
     mem_copy = local(io.mem, mem_slot.at[:, part(s, mem_cols)])
     send(io.cot, rows(buf.e3, q), k_cot, ((s + n_sec - 1) % n_sec, d))
     for weight in (wt.so, wt.co, wt.f2):
-        weight.own_copy = local(weight.source, block(weight, z))
-    swap_start(wt.ckv)
-    swap_start(wt.cq)
+        weight.own_copy = [local(weight.source, block(weight, z))]
+    for weight, copy in ((wt.ckv, raw_copies[1]), (wt.cq, raw_copies[2])):
+        copy.wait()
+        sort_columns(weight)
+        swap_start(weight)
 
     spread_relay(sv)
     swap_wait(wt.qkv)
@@ -866,7 +967,7 @@
     mem_copy.wait()
     gather_relay(a1)
     memory = gather_start(buf.m)
-    swap_start(wt.f1)
+    unit_swap_start()
     gather_ready(a1)
     weight_relay(wt.qkv)
     weight_ready(wt.qkv)
@@ -874,11 +975,11 @@
     weight_relay(wt.so)
     gather_finish(memory)
     attention(buf.qkv, 0, buf.qkv, 2, 4, True, 13, buf.p1, buf.o1)
-    wt.so.own_copy.wait()
+    wt.so.own_copy[0].wait()
     weight_ready(wt.so)
     matmul(buf.o1, wt.so.weight, set_a.parts)
     step = reduce_start(set_a)
-    swap_wait(wt.f1)
+    unit_swap_wait()
     weight_send(wt.f1, block(wt.f1, z))
     weight_relay(wt.ckv)
     reduce_relay(step)
@@ -904,7 +1005,7 @@
     weight_ready(wt.cq)
     matmul(buf.a2, wt.cq.weight, buf.q2, buf.bias, 1)
     attention(buf.q2, 0, buf.kv, 0, 2, False, 14, buf.p2, buf.o2)
-    wt.co.own_copy.wait()
+    wt.co.own_copy[0].wait()
     weight_ready(wt.co)
     matmul(buf.o2, wt.co.weight, set_b.parts)
     step = reduce_start(set_b)
@@ -935,7 +1036,7 @@
     weight_grad(buf.g, buf.e3, wt.f2)
     grad_send(wt.f2)
     weight_relay(wt.f2)
-    wt.f2.own_copy.wait()
+    wt.f2.own_copy[0].wait()
     weight_ready(wt.f2)
 
     def units_back(j):
@@ -1049,10 +1150,6 @@
     send(buf.ig, io.input_grad, k_in, ((s + n_sec - 1) % n_sec, d))
     buf.sga[q, z] = buf.sg[...].astype(BF16)
     sums = spread_start(buf.sga, None)
-    grad_combine(wt.ckv)
-    grad_final(wt.f2)
-    grad_final(wt.f1)
-    spread_relay(sums)
     for j in range(1, n_sec):
         arrived(buf.ml.at[j], k_back + j)
 
@@ -1065,14 +1162,49 @@
 
     loop(L // TILE, memory_total)
     result_copies.append(local(buf.mo, io.memory_grad))
+    grad_final(wt.f2)
+    grad_final(wt.f1)
+    grad_combine(wt.ckv)
+    for weight in (wt.co, wt.cq, wt.ckv):
+        grad_final(weight)
     grad_combine(wt.so)
     grad_combine(wt.qkv)
-    for weight in (wt.co, wt.cq, wt.ckv, wt.so, wt.qkv):
+    unit_last_wait()
+    last_wait(wt.ckv)
+    last_wait(wt.cq)
+    spread_relay(sums)
+    for weight in (wt.so, wt.qkv):
         grad_final(weight)
     spread_ready(sums)
-    result_copies.append(local(buf.sga, io.sums_out))
-    for weight in (wt.qkv, wt.ckv, wt.cq, wt.f1):
-        last_wait(weight)
+
+    def per_unit(q_at, at):
+        total = buf.sga[q_at, 0, :, at].astype(F32)
+        for plane in range(1, Z):
+            total = total + buf.sga[q_at, plane, :, at].astype(F32)
+        return total
+
+    at = part(d // 2, 128)
+    feature = per_unit(0, at)
+    for q_at in range(1, P_IN):
+        feature = feature + per_unit(q_at, at)
+    swapped = pltpu.roll(feature, 64, 1)
+    buf.sums[...] = jnp.where((jnp.zeros((16, 128), jnp.int32) + c) == 0, feature, swapped)
+    head = d % 8
+    at = part(2 * (d // 8) + head // 4, 128)
+    low_head, high_head = per_unit(2 * c, at), per_unit(2 * c + 1, at)
+    first_half = (jnp.zeros((16, 128), jnp.int32) + (head // 2) % 2) == 0
+    low_head = jnp.where(first_half, low_head, pltpu.roll(low_head, 64, 1))
+    high_head = jnp.where(first_half, pltpu.roll(high_head, 64, 1), high_head)
+    buf.sums[9:10, :] = jnp.where(half, low_head, high_head)[9:10]
+    at = part(2 * (d // 8) + 4 + head // 4, 128)
+    low_head, high_head = per_unit(2 * c, at), per_unit(2 * c + 1, at)
+    low_head = jnp.where(first_half, low_head, pltpu.roll(low_head, 64, 1))
+    high_head = jnp.where(first_half, pltpu.roll(high_head, 64, 1), high_head)
+    buf.sums[10:11, :] = jnp.where(half, low_head, high_head)[9:10]
+    buf.sums[11:12, :] = per_unit(q, part(2 * z, 128))[10:11]
+    buf.sums[12:13, :] = per_unit(q, part(2 * z + 1, 128))[10:11]
+    result_copies.append(local(buf.sums, io.sums_out))
+    last_wait(wt.qkv)
     arrived(io.input_grad, k_in)
     for copy in result_copies:
         copy.wait()
@@ -1094,7 +1226,7 @@
         g=(T, FL), gp=(T, FL),
         a1=tokens, a2=tokens, a3=tokens, m=tokens, e3=tokens, e2=tokens, e1=tokens,
     )
-    exact = dict(vec=(16, D), bias=(8, D), sg=(16, D), h1=row, h2=row, dh=row)
+    exact = dict(vec=(16, D), bias=(8, D), sg=(16, D), sums=(16, 128), h1=row, h2=row, dh=row)
     kinds = {name: pltpu.VMEM(shape, BF16) for name, shape in shapes.items()}
     kinds.update({name: pltpu.VMEM(shape, F32) for name, shape in exact.items()})
     return kinds
@@ -1113,10 +1245,13 @@
     for count, columns, _ in WEIGHTS.values():
         scratch += 2 * [pltpu.VMEM((Z * count, columns), BF16)]
         scratch += 4 * [pltpu.VMEM((count, columns), BF16)]
+    for columns in (768, 512, 256):
+        scratch.append(pltpu.VMEM((64, P_IN * columns), BF16))
+        scratch.append(pltpu.VMEM((P_IN, 64, columns), BF16))
     return scratch + [
         pltpu.SemaphoreType.DMA((SEMS,)),
         pltpu.SemaphoreType.DMA((SEMS,)),
-        pltpu.SemaphoreType.DMA((32,)),
+        pltpu.SemaphoreType.DMA((48,)),
     ]
 
 
@@ -1125,47 +1260,24 @@
     self_out, cross_q, cross_kv, cross_qv_bias, cross_out, out_bias, fc1, fc1_bias, fc2,
 ):
     n_sec = lax.axis_size("section")
-    d = lax.axis_index("dp")
     mem_cols = memory.shape[2]
-    pieces = jnp.concatenate([norm_gain[0], norm_bias[0], out_bias[0]], 0)
-    odd = (d % 2).astype(BF16)
-    spaced = jnp.concatenate([pieces * (1 - odd), pieces * odd], 1)
-    ones = jnp.ones((1, 128), BF16)
-    small = jnp.concatenate(
-        [
-            spaced,
-            self_qv_bias,
-            cross_qv_bias,
-            fc1_bias.reshape(2, 128),
-            ones * tgt_len.astype(BF16)[:, None],
-            ones * src_len.astype(BF16)[:, None],
-            ones,
-        ],
-        0,
-    )
-
-    def to_columns(weight, groups, unit):
-        split = weight[0].reshape(-1, groups, Z, P_IN, unit)
-        return split.transpose(3, 0, 1, 2, 4).reshape(P_IN, -1, groups * Z * unit)
-
-    def from_columns(grad, groups, unit):
-        split = grad.reshape(P_IN, -1, groups, Z, unit)
-        return split.transpose(1, 2, 3, 0, 4).reshape(1, -1, groups * Z * P_IN * unit).astype(F32)
-
     operands = (
-        prev_act[0, 0], memory[0], out_cot[0, 0], small,
-        to_columns(self_qkv, 3, HD), self_out[0], to_columns(cross_kv, 2, HD),
-        to_columns(cross_q, 1, HD), cross_out[0], to_columns(fc1, 1, FL // Z), fc2[0],
-    )
+        prev_act[0, 0], memory[0], out_cot[0, 0], tgt_len, src_len,
+        norm_gain[0], norm_bias[0], out_bias[0], self_qv_bias, cross_qv_bias, fc1_bias,
+        self_qkv[0], self_out[0], cross_kv[0], cross_q[0], cross_out[0], fc1[0], fc2[0],
+    )
+    anywhere = pl.BlockSpec(memory_space=pl.ANY)
+    in_specs = 3 * [anywhere] + 2 * [pl.BlockSpec(memory_space=pltpu.SMEM)]
+    in_specs += 6 * [pl.BlockSpec(memory_space=pltpu.VMEM)] + 7 * [anywhere]
     out_shapes = [(L, D), (L, D), (L, mem_cols)]
     for count, columns, by_column in WEIGHTS.values():
-        out_shapes.append((P_IN, count // P_IN, columns) if by_column else (count, columns))
-    out_shapes.append((P_IN, Z, 16, D))
+        out_shapes.append((count // P_IN, P_IN * columns) if by_column else (count, columns))
+    sums_shape = jax.ShapeDtypeStruct((16, 128), F32)
     results = pl.pallas_call(
         functools.partial(whole_kernel, n_sec, mem_cols),
-        out_shape=[jax.ShapeDtypeStruct(shape, BF16) for shape in out_shapes],
-        in_specs=[pl.BlockSpec(memory_space=pl.ANY)] * len(operands),
-        out_specs=[pl.BlockSpec(memory_space=pl.ANY)] * len(out_shapes),
+        out_shape=[jax.ShapeDtypeStruct(shape, BF16) for shape in out_shapes] + [sums_shape],
+        in_specs=in_specs,
+        out_specs=[anywhere] * (len(out_shapes) + 1),
         scratch_shapes=scratch_of(n_sec, mem_cols),
         compiler_params=pltpu.CompilerParams(
             collective_id=0, has_side_effects=True, vmem_limit_bytes=63 * 2**20
@@ -1175,30 +1287,22 @@
         ),
     )(*operands)
     output, input_grad, memory_grad, g_qkv, g_so, g_ckv, g_cq, g_co, g_f1, g_f2, sums = results
-    sums = sums.astype(F32)
-    by_feature = jnp.sum(sums[:, :, :9], (0, 1))
-    own = lax.dynamic_slice_in_dim(by_feature, d * 64, 64, 1)
-    by_head = jnp.sum(sums[:, :, 9], 1).reshape(P_IN, 4, Z, 64).transpose(1, 2, 0, 3)
-    by_head = by_head.reshape(2, 2048)
-    by_unit = jnp.sum(sums[:, :, 10], 1).reshape(P_IN, Z, 256).transpose(1, 0, 2).reshape(1, 4096)
-    own_head = lax.dynamic_slice_in_dim(by_head, d * 128, 128, 1)
-    own_unit = lax.dynamic_slice_in_dim(by_unit, d * 256, 256, 1)
     return (
         output[None, None],
         input_grad[None, None],
         memory_grad[None],
-        own[None, 0:3],
-        own[None, 3:6],
-        from_columns(g_qkv, 3, HD),
-        own_head[0:1],
+        sums[None, 0:3, 0:64],
+        sums[None, 3:6, 0:64],
+        g_qkv[None].astype(F32),
+        sums[9:10],
         g_so[None].astype(F32),
-        from_columns(g_cq, 1, HD),
-        from_columns(g_ckv, 2, HD),
-        own_head[1:2],
+        g_cq[None].astype(F32),
+        g_ckv[None].astype(F32),
+        sums[10:11],
         g_co[None].astype(F32),
-        own[None, 6:9],
-        from_columns(g_f1, 1, FL // Z),
-        own_unit,
+        sums[None, 6:9, 0:64],
+        g_f1[None].astype(F32),
+        sums[11:13].reshape(1, 256),
         g_f2[None].astype(F32),
     )
 

time: 348 us -> 317 us (0.911); the launches traced: 341 us -> 317 us
  local copies, waits for them, and re-layouts: 26.9 us -> 6.03 us
  Pallas kernels: 307 us -> 302 us
    convert_element_type x12 -> x0, local copies, waits for them, and re-layouts: 12 us -> none  [from_columns(): split.transpose(1, 2, 3, 0, 4).reshape(1, -1, groups * Z * P_IN * unit)]
    pallas_call x1, Pallas kernels: 307 us -> 302 us  [on_device_planes(): pl.pallas_call(functools.partial(whole_kernel, n_sec, mem_cols), out_shap...]
    reshape x7 -> x0, local copies, waits for them, and re-layouts: 4.48 us -> none  [the longest x4 4.27 us: to_columns(): return split.transpose(3, 0, 1, 2, 4).reshape(P_IN, -1, groups * Z * unit)]
where the time goes in v2:
time: 317 us
  Pallas kernels  302 us (95%)
  other arithmetic  6.48 us (2%)
  local copies, waits for them, and re-layouts  6.03 us (2%)
    pallas_call x1, Pallas kernels, on_device_planes(): pl.pallas_call(functools.partial(whole_kernel, n_sec, mem_cols), out_shap...  302 us

profile of v2, /device:TPU:1, one launch (start us, length us, event | category | flops | bytes accessed | tf_op | source)
XLA Modules:
  0.0 316.8 jit_solution(12502018102032329021)
XLA Ops:
  1.9 302.3 %shard_map.297 = (bf16[192,1024]{1,0:T(8,128)(2,1)}, bf16[192,1024]{1,0:T(8,128)(2,1)}, bf16[192,512]{1,0:T(8,128)(2,1)}, bf16[64,3072]{1,0:T(8,128)(2,1)}, bf16...) custom-call(bf16[192,1024]{1,0:T(8,128)(2,1)} %bitcast.50, ...), custom_call_target="tpu_custom_call" | custom-call | flops 20999999488 | bytes 20971520 | tf_op jit(solution)/shard_map/pallas_call | solution.py:1276
  304.3 0.0 copy-start.1
  304.3 0.0 copy-start.8
  304.3 1.9 bitcast_convert_fusion.4
  306.2 0.0 copy-done.8
  306.2 0.6 copy.34
  306.8 0.6 copy.35
  307.3 0.6 copy.36
  307.9 0.5 fusion
  308.4 0.6 slice.23
  309.0 0.0 copy-done.1
  309.0 0.0 copy-start
  309.0 1.1 bitcast_convert_fusion
  310.1 0.0 copy-done
  310.1 0.0 copy-start.4
  310.1 1.0 bitcast_convert_fusion.1
  311.1 0.0 copy-done.4
  311.1 0.0 copy-start.5
  311.1 0.9 bitcast_convert_fusion.2
  312.1 0.0 copy-done.5
  312.1 0.0 copy-start.7
  312.1 0.8 bitcast_convert_fusion.3
  312.9 0.0 copy-start.3
  312.9 0.1 copy-done.7
  313.0 0.7 bitcast_convert_fusion.6
  313.8 0.2 copy-done.3
  313.9 0.0 copy-start.2
  313.9 0.7 copy.42
  314.7 0.4 copy-done.2
  315.1 0.7 copy.43
  315.8 0.3 copy-done.6
  316.2 0.7 copy.44
  (2 shorter events, 0.0 us)
Async XLA Ops:
  304.3 4.7 %copy-start.1 = (bf16[256,1024]{1,0:T(8,128)(2,1)S(1)}, bf16[256,1024]{1,0:T(8,128)(2,1)}, u32[]{:S(2)}) copy-start(bf16[256,1024]{1,0:T(8,128)(2,1)} %get-tuple-element.37) | copy-start | bytes 1572868
  304.3 1.9 copy-start.8
  309.0 1.1 copy-start
  310.1 1.1 copy-start.4
  311.1 1.0 copy-start.5
  312.1 0.9 copy-start.7
  312.9 1.0 copy-start.3
  313.9 1.1 copy-start.2
  315.1 1.1 copy-start.6

commit v3 on v2

--- a/solution.py
+++ b/solution.py
@@ -375,12 +375,12 @@
     return lax.dot_general(left, right, (((0,), (0,)), ((), ())), preferred_element_type=F32)
 
 
-def loop(count, body):
+def loop(count, body, unroll=1):
     def step(index, carry):
         body(index)
         return carry
 
-    lax.fori_loop(0, count, step, 0)
+    lax.fori_loop(0, count, step, 0, unroll=unroll)
 
 
 def gelu_pair(values):
@@ -426,7 +426,9 @@
     vars(io).update(vars(take(dict(sums_out=0))))
     buf = take(buffer_shapes(n_sec, mem_cols))
     set_a, set_b, set_c = (take(REDUCE_SHAPES) for _ in range(3))
-    take_weights(weight=0, grad=0, to_diag=0, to_opp=0, near=0, far=0)
+    take_weights(weight=0, grad=0, near=0, far=0)
+    for weight in (wt.qkv, wt.so, wt.ckv, wt.cq, wt.co):
+        weight.to_diag, weight.to_opp, weight.through = next(given), next(given), next(given)
     for weight in (wt.qkv, wt.ckv, wt.cq):
         weight.raw, weight.sorted = next(given), next(given)
     send_sems, recv_sems, local_sems = given
@@ -487,29 +489,45 @@
     for name, (count, _, by_column) in WEIGHTS.items():
         weight = getattr(wt, name)
         weight.count, weight.by_column = count, by_column
-        weight.to_use, weight.swap, weight.to_sum, weight.last = slot(5), slot(3), slot(5), slot(3)
+        weight.to_use, weight.swap, weight.to_sum, weight.last = slot(5), slot(3), slot(6), slot(3)
 
     def block(name, index):
         return name.weight.at[part(index, name.count)]
 
-    def weight_send(name, src):
+    def send_inward(name, src):
+        send(src, block(name, z), name.to_use, dev_adj, end)
+
+    def send_across(name, src):
+        send(src, block(name, z), name.to_use + 1, dev_opp, mid)
+
+    def weight_outward(name, src):
+        send(src, block(name, z), name.to_use, dev_adj, mid)
+
+    def relay_inward(name):
         k = name.to_use
-        send(src, block(name, z), k, dev_adj)
-        send(src, block(name, z), k + 1, dev_opp, mid)
-        send(src, block(name, z), k + 2, dev_diag, end)
-
-    def weight_relay(name):
+        arrived(block(name, z_adj), k, mid)
+        send(block(name, z_adj), block(name, z_adj), k + 2, dev_opp, mid)
+
+    def relay_near(name):
         k = name.to_use
         arrived(block(name, z_opp), k + 1, mid)
         send(block(name, z_opp), block(name, z_opp), k + 3, dev_adj, mid)
+
+    def relay_far(name):
+        k = name.to_use
         arrived(block(name, z_diag), k + 2, mid)
         send(block(name, z_diag), block(name, z_diag), k + 4, dev_adj, mid)
 
     def weight_ready(name):
         k = name.to_use
-        arrived(block(name, z_adj), k)
+        arrived(block(name, z_adj), k, end)
         arrived(block(name, z_diag), k + 3, end)
         arrived(block(name, z_opp), k + 4, end)
+
+    def inner_ready(name):
+        k = name.to_use
+        arrived(block(name, z_opp), k + 1, mid)
+        arrived(block(name, z_diag), k + 2, mid)
 
 
     def swap_start(name):
@@ -572,69 +590,125 @@
                 send(unit_columns(wt.f1.source, tile, q_to), at, unit_swap + 3 * tile + j, device)
             wt.f1.own_copy.append(local(unit_columns(wt.f1.source, tile, q), at))
 
-    def unit_swap_wait():
+    def unit_swap_wait(cond):
         size = wt.f1.count // P_IN
         for tile in range(Z):
             for j, (q_from, _) in enumerate(in_plane):
                 place = wt.f1.weight.at[part(z * P_IN + q_from, size)]
-                arrived(place.at[:, part(tile, 256)], unit_swap + 3 * tile + j)
+                arrived(place.at[:, part(tile, 256)], unit_swap + 3 * tile + j, cond)
         for copy in wt.f1.own_copy:
-            copy.wait()
+            run_if(cond, copy.wait)
 
     def grad_block(name, index):
         return name.grad.at[part(index, name.count)]
 
+    def grad_send_far(name):
+        return send(grad_block(name, z_opp), name.to_diag, name.to_sum, dev_adj, end)
+
+    def grad_send_middle(name):
+        return send(grad_block(name, z_diag), name.to_opp, name.to_sum + 1, dev_adj, end)
+
+    def grad_send_near(name):
+        return send(grad_block(name, z_adj), name.near, name.to_sum + 2, dev_adj, end)
+
     def grad_send(name):
-        k = name.to_sum
-        send(grad_block(name, z_opp), name.to_diag, k, dev_adj, end)
-        send(grad_block(name, z_diag), name.to_opp, k + 1, dev_adj, end)
-        send(grad_block(name, z_adj), name.near, k + 2, dev_adj)
+        grad_send_far(name)
+        grad_send_middle(name)
+        grad_send_near(name)
 
     def add_rows(count, body):
         size = min(count, 64)
         loop(count // size, lambda i: body(part(i, size)))
 
+    def grad_add(name, landed, index):
+        def one(place):
+            own = grad_block(name, index)[place, :].astype(F32)
+            landed[place, :] = (own + landed[place, :].astype(F32)).astype(BF16)
+
+        add_rows(name.count, one)
+
+    def grad_combine_far(name):
+        k = name.to_sum
+        arrived(name.to_diag, k, mid)
+        run_if(mid, lambda: grad_add(name, name.to_diag, z_diag))
+        send(name.to_diag, name.through, k + 3, dev_opp, mid)
+
+    def grad_combine_middle(name):
+        k = name.to_sum
+        arrived(name.to_opp, k + 1, mid)
+        run_if(mid, lambda: grad_add(name, name.to_opp, z_opp))
+        send(name.to_opp, name.far, k + 4, dev_opp, mid)
+
     def grad_combine(name):
+        grad_combine_far(name)
+        grad_combine_middle(name)
+
+    def grad_outward(name):
         k = name.to_sum
+        arrived(name.through, k + 3, mid)
+        run_if(mid, lambda: grad_add(name, name.through, z_adj))
+        send(name.through, name.near, k + 5, dev_adj, mid)
+
+    result_copies = []
+
+    def inner_grad_far(name):
+        send(grad_block(name, z_diag), name.far, name.to_sum, dev_opp, mid)
+
+    def inner_grad_near(name):
+        send(grad_block(name, z_opp), name.near, name.to_sum + 1, dev_opp, mid)
+
+    def inner_grad_combine(name):
+        k = name.to_sum
+
+        def add():
+            arrived(name.far, k)
+
+            def one(place):
+                own = grad_block(name, z_adj)[place, :].astype(F32)
+                name.far[place, :] = (own + name.far[place, :].astype(F32)).astype(BF16)
+
+            add_rows(name.count, one)
+
+        run_if(mid, add)
+        send(name.far, name.near, k + 2, dev_adj, mid)
+
+    def inner_grad_total(name):
+        k = name.to_sum
+        arrived(name.near, k + 2, end)
+
+        def add():
+            arrived(name.near, k + 1)
+
+            def one(place):
+                own = grad_block(name, z)[place, :].astype(F32)
+                name.near[place, :] = (own + name.near[place, :].astype(F32)).astype(BF16)
+
+            add_rows(name.count, one)
+
+        run_if(mid, add)
+
+    def grad_total(name):
+        k = name.to_sum
+        arrived(name.near, k + 5, end)
+        arrived(name.near, k + 2, mid)
+        arrived(name.far, k + 4, mid)
+
+        def add_far():
+            def one(place):
+                total = name.near[place, :].astype(F32) + name.far[place, :].astype(F32)
+                name.near[place, :] = (total + grad_block(name, z)[place, :].astype(F32)).astype(BF16)
+
+            add_rows(name.count, one)
+
+        run_if(mid, add_far)
+        run_if(end, lambda: grad_add(name, name.near, z))
+
+    def grad_final(name):
         count = name.count
-
-        def add(landed, index):
-            def one(place):
-                own = grad_block(name, index)[place, :].astype(F32)
-                landed[place, :] = (own + landed[place, :].astype(F32)).astype(BF16)
-
-            add_rows(count, one)
-
-        def work():
-            arrived(name.to_diag, k)
-            add(name.to_diag, z_diag)
-
-        run_if(mid, work)
-        send(name.to_diag, name.far, k + 3, dev_diag, mid)
-
-        def more():
-            arrived(name.to_opp, k + 1)
-            add(name.to_opp, z_opp)
-
-        run_if(mid, more)
-        send(name.to_opp, name.far, k + 4, dev_opp, mid)
-
-    result_copies = []
-
-    def grad_final(name):
-        k = name.to_sum
-        count = name.count
-        arrived(name.near, k + 2)
-        arrived(name.far, k + 3, end)
-        arrived(name.far, k + 4, mid)
-
-        def one(place):
-            total = grad_block(name, z)[place, :].astype(F32)
-            total = total + name.near[place, :].astype(F32)
-            total = total + name.far[place, :].astype(F32)
-            name.near[place, :] = total.astype(BF16)
-
-        add_rows(count, one)
+        if name is wt.f1 or name is wt.f2:
+            inner_grad_total(name)
+        else:
+            grad_total(name)
         size = count // P_IN
         if name is wt.f1:
             for tile in range(Z):
@@ -667,51 +741,54 @@
                 place = unit_columns(wt.f1.result, tile, q_from)
                 arrived(place, unit_last + 3 * tile + j)
 
-    def gather_start(name):
+    def gather_start(name, cond=None):
         k = slot(3)
-        send(rows(name, q), rows(name, q), k, dev_x)
-        send(rows(name, q), rows(name, q), k + 1, dev_core)
-        return name, k
+        first = send(rows(name, q), rows(name, q), k, dev_x, cond)
+        second = send(rows(name, q), rows(name, q), k + 1, dev_core, cond)
+        return name, k, [first, second], cond
 
     def gather_relay(ticket):
-        name, k = ticket
-        arrived(rows(name, q_x), k)
-        send(rows(name, q_x), rows(name, q_x), k + 2, dev_core)
+        name, k, records, cond = ticket
+        arrived(rows(name, q_x), k, cond)
+        records.append(send(rows(name, q_x), rows(name, q_x), k + 2, dev_core, cond))
 
     def gather_ready(ticket):
-        name, k = ticket
-        arrived(rows(name, q_core), k + 1)
-        arrived(rows(name, q_xc), k + 2)
+        name, k, _, cond = ticket
+        arrived(rows(name, q_core), k + 1, cond)
+        arrived(rows(name, q_xc), k + 2, cond)
 
     def gather_finish(ticket):
         gather_relay(ticket)
         gather_ready(ticket)
 
-    def reduce_start(which):
+    def reduce_start(which, cond=None):
         k = slot(3)
         out = which.parts
-        first = send(rows(out, q_xc), rows(which.core, 1), k, dev_core)
-        second = send(rows(out, q_core), rows(which.core, 0), k + 1, dev_core)
-        return which, k, [first, second]
+        first = send(rows(out, q_xc), rows(which.core, 1), k, dev_core, cond)
+        second = send(rows(out, q_core), rows(which.core, 0), k + 1, dev_core, cond)
+        return which, k, [first, second], cond
 
     def reduce_relay(ticket):
-        which, k, records = ticket
+        which, k, records, cond = ticket
         out = which.parts
-        arrived(rows(which.core, 1), k)
-
-        def one(i):
-            mine = rows(out, q_x)
-            place = part(i, TILE)
-            total = mine[place, :].astype(F32) + rows(which.core, 1)[place, :].astype(F32)
-            mine[place, :] = total.astype(BF16)
-
-        loop(L // TILE, one)
-        records.append(send(rows(out, q_x), which.across, k + 2, dev_x))
+        arrived(rows(which.core, 1), k, cond)
+
+        def add():
+            def one(i):
+                mine = rows(out, q_x)
+                place = part(i, TILE)
+                total = mine[place, :].astype(F32) + rows(which.core, 1)[place, :].astype(F32)
+                mine[place, :] = total.astype(BF16)
+
+            loop(L // TILE, one)
+
+        run_if(cond, add)
+        records.append(send(rows(out, q_x), which.across, k + 2, dev_x, cond))
 
     def reduce_ready(ticket):
-        which, k, records = ticket
-        arrived(rows(which.core, 0), k + 1)
-        arrived(which.across, k + 2)
+        which, k, _, cond = ticket
+        arrived(rows(which.core, 0), k + 1, cond)
+        arrived(which.across, k + 2, cond)
 
     def reduced(ticket, place):
         which = ticket[0]
@@ -811,7 +888,7 @@
             mixed = nn(weights, kref[place, part(pair + v_at, 128)])
             dst[place, part(pair, 128)] = merge(mixed).astype(BF16)
 
-        loop(2 * P_IN, one)
+        loop(2 * P_IN, one, 2)
 
     def attention_back(qref, q_at, kref, k_at, v_at, probs, grad):
         def one(i):
@@ -834,7 +911,7 @@
             kref[place, part(pair + k_at, 128)] = grad_key.astype(BF16)
             kref[place, part(pair + v_at, 128)] = grad_value.astype(BF16)
 
-        loop(2 * P_IN, one)
+        loop(2 * P_IN, one, 2)
 
     def column_sums(source, first, count, row, at):
         def one(j):
@@ -852,14 +929,14 @@
 
         loop(L // TILE, one)
 
-    def norm_back(load, ticket, index, base, dst, low):
+    def norm_back(load, incoming, index, base, dst, low, out_row=None):
         zero = jnp.zeros((1, D), F32)
 
         def one(i, carry):
             gain_sum, shift_sum, out_sum = carry
             place = part(i, TILE)
             normed, scale = whiten(load(place))
-            grad = reduced(ticket, place)
+            grad = incoming(place)
             gained = grad * buf.vec[index:index + 1, :]
             back = gained - jnp.mean(gained, -1, keepdims=True)
             back = back - normed * jnp.mean(gained * normed, -1, keepdims=True)
@@ -877,8 +954,14 @@
         gain_sum, shift_sum, out_sum = lax.fori_loop(0, L // TILE, one, (zero, zero, zero))
         buf.sg[index:index + 1, :] = gain_sum
         buf.sg[index + 3:index + 4, :] = shift_sum
-        return out_sum
-
+        if out_row is not None:
+            buf.sg[out_row:out_row + 1, :] = out_sum
+
+    gate = pltpu.get_barrier_semaphore()
+    partners = [device for _, device in in_plane] + [dev_adj, dev_opp, dev_diag]
+    partners += [((s + j) % n_sec, d) for j in range(1, n_sec)]
+    for device in partners:
+        pl.semaphore_signal(gate, inc=1, device_id=device, device_id_type=MESH)
     raw_copies = [local(weight.source, weight.raw) for weight in (wt.qkv, wt.ckv, wt.cq)]
     low_lanes = lax.broadcasted_iota(jnp.int32, (3, 128), 1) < 64
     even_lanes = (jnp.zeros((3, 128), jnp.int32) + c) == 0
@@ -895,11 +978,6 @@
     buf.sg[15:16, 0:128] = jnp.zeros((1, 128), F32)
     buf.sva[q, z] = buf.sg[:, 0:128].astype(BF16)
 
-    gate = pltpu.get_barrier_semaphore()
-    partners = [device for _, device in in_plane] + [dev_adj, dev_opp, dev_diag]
-    partners += [((s + j) % n_sec, d) for j in range(1, n_sec)]
-    for device in partners:
-        pl.semaphore_signal(gate, inc=1, device_id=device, device_id_type=MESH)
     raw_copies[0].wait()
     sort_columns(wt.qkv)
     pl.semaphore_wait(gate, len(partners))
@@ -922,8 +1000,9 @@
 
     spread_relay(sv)
     swap_wait(wt.qkv)
-    weight_send(wt.qkv, block(wt.qkv, z))
-    weight_send(wt.so, wt.so.source)
+    send_inward(wt.qkv, block(wt.qkv, z))
+    send_across(wt.qkv, block(wt.qkv, z))
+    weight_outward(wt.qkv, block(wt.qkv, z))
     spread_ready(sv)
 
     for tile in range(D // 128):
@@ -956,11 +1035,12 @@
 
     norm(hidden, 0, buf.a1)
     a1 = gather_start(buf.a1)
+    relay_inward(wt.qkv)
+    relay_near(wt.qkv)
+    weight_outward(wt.so, wt.so.source)
+    send_inward(wt.so, wt.so.source)
     swap_wait(wt.ckv)
-    swap_wait(wt.cq)
-    weight_send(wt.ckv, block(wt.ckv, z))
-    weight_send(wt.cq, block(wt.cq, z))
-    weight_send(wt.co, wt.co.source)
+    send_inward(wt.ckv, block(wt.ckv, z))
     for j in range(1, n_sec):
         origin = (s + n_sec - j) % n_sec
         arrived(mem_slot.at[:, part(origin, mem_cols)], k_mem + j)
@@ -968,23 +1048,42 @@
     gather_relay(a1)
     memory = gather_start(buf.m)
     unit_swap_start()
+    send_across(wt.so, wt.so.source)
+    relay_inward(wt.so)
+    swap_wait(wt.cq)
+    send_inward(wt.cq, block(wt.cq, z))
+    send_inward(wt.co, wt.co.source)
+    relay_far(wt.qkv)
+    arrived(rows(buf.e3, q), k_cot)
+    k_units = slot(4)
+    to_middle = send(rows(buf.e3, q), rows(buf.e3b, q), k_units, dev_adj, end)
     gather_ready(a1)
-    weight_relay(wt.qkv)
     weight_ready(wt.qkv)
     matmul(buf.a1, wt.qkv.weight, buf.qkv, buf.bias, 0)
-    weight_relay(wt.so)
-    gather_finish(memory)
+    send_across(wt.ckv, block(wt.ckv, z))
+    unit_swap_wait(end)
+    send_inward(wt.f1, block(wt.f1, z))
     attention(buf.qkv, 0, buf.qkv, 2, 4, True, 13, buf.p1, buf.o1)
+    relay_inward(wt.ckv)
+    relay_near(wt.so)
+    relay_far(wt.so)
+    weight_outward(wt.ckv, block(wt.ckv, z))
+    send_across(wt.cq, block(wt.cq, z))
     wt.so.own_copy[0].wait()
     weight_ready(wt.so)
     matmul(buf.o1, wt.so.weight, set_a.parts)
     step = reduce_start(set_a)
-    unit_swap_wait()
-    weight_send(wt.f1, block(wt.f1, z))
-    weight_relay(wt.ckv)
+    send_inward(wt.f2, wt.f2.source)
+    relay_inward(wt.cq)
+    weight_outward(wt.cq, block(wt.cq, z))
     reduce_relay(step)
-    weight_ready(wt.ckv)
-    matmul(buf.m, wt.ckv.weight, buf.kv, buf.bias, 1, 1)
+    relay_near(wt.ckv)
+    gather_finish(memory)
+    relay_far(wt.ckv)
+    send_across(wt.co, wt.co.source)
+    relay_inward(wt.co)
+    unit_swap_wait(mid)
+    send_across(wt.f1, block(wt.f1, z))
     reduce_ready(step)
 
     def after_self(i):
@@ -995,13 +1094,18 @@
     norm(lambda place: buf.h1[place, :], 1, buf.a2)
     a2 = gather_start(buf.a2)
     reduce_done(step)
-
-    weight_send(wt.f2, wt.f2.source)
-    weight_relay(wt.cq)
-    weight_relay(wt.co)
-    arrived(rows(buf.e3, q), k_cot)
+    relay_near(wt.cq)
+    weight_outward(wt.co, wt.co.source)
+    relay_far(wt.cq)
+    weight_ready(wt.ckv)
+    matmul(buf.m, wt.ckv.weight, buf.kv, buf.bias, 1, 1)
+    relay_near(wt.co)
+    send_across(wt.f2, wt.f2.source)
+    relay_far(wt.co)
+    relay_inward(wt.f1)
+
     gather_finish(a2)
-    e3 = gather_start(buf.e3)
+    e3 = gather_start(buf.e3, mid)
     weight_ready(wt.cq)
     matmul(buf.a2, wt.cq.weight, buf.q2, buf.bias, 1)
     attention(buf.q2, 0, buf.kv, 0, 2, False, 14, buf.p2, buf.o2)
@@ -1009,6 +1113,7 @@
     weight_ready(wt.co)
     matmul(buf.o2, wt.co.weight, set_b.parts)
     step = reduce_start(set_b)
+    relay_inward(wt.f2)
     gather_finish(e3)
     reduce_relay(step)
     reduce_ready(step)
@@ -1019,47 +1124,84 @@
 
     loop(L // TILE, after_cross)
     norm(lambda place: buf.h2[place, :], 2, buf.a3)
-    a3 = gather_start(buf.a3)
+    send(rows(buf.a3, q), rows(buf.a3b, q), k_units + 1, dev_adj, end)
+    a3 = gather_start(buf.a3, mid)
     reduce_done(step)
 
-    weight_relay(wt.f1)
-    gather_finish(a3)
-    weight_ready(wt.f1)
-
-    def units(j):
-        value = nn(buf.a3[...], wt.f1.weight[:, lanes(j)]) + buf.bias[2:3, lanes(j)]
-        activ, slope = gelu_pair(value)
-        buf.g[:, lanes(j)] = activ.astype(BF16)
-        buf.gp[:, lanes(j)] = slope.astype(BF16)
-
-    loop(FL // 256, units)
-    weight_grad(buf.g, buf.e3, wt.f2)
-    grad_send(wt.f2)
-    weight_relay(wt.f2)
-    wt.f2.own_copy[0].wait()
-    weight_ready(wt.f2)
-
-    def units_back(j):
-        value = nt(buf.e3[...], wt.f2.weight[lanes(j), :])
-        low = (value * buf.gp[:, lanes(j)].astype(F32)).astype(BF16)
-        buf.gp[:, lanes(j)] = low
-        buf.sg[10:11, lanes(j)] = jnp.sum(low.astype(F32), 0, keepdims=True)
-
-    loop(FL // 256, units_back)
-    matmul_back(buf.gp, wt.f1.weight, set_a.parts)
-    step = reduce_start(set_a)
-    weight_grad(buf.a3, buf.gp, wt.f1)
-    grad_send(wt.f1)
-    reduce_relay(step)
-    matmul(buf.g, wt.f2.weight, set_c.parts)
-    final = reduce_start(set_c)
-    reduce_ready(step)
-    zero = jnp.zeros((1, D), F32)
+    def units(normed, activs, slopes):
+        def one(j):
+            value = nn(normed[...], wt.f1.weight[:, lanes(j)]) + buf.bias[2:3, lanes(j)]
+            activ, slope = gelu_pair(value)
+            activs[:, lanes(j)] = activ.astype(BF16)
+            slopes[:, lanes(j)] = slope.astype(BF16)
+
+        loop(FL // 256, one)
+
+    def units_back(grad, slopes):
+        def one(j):
+            value = nt(grad[...], wt.f2.weight[lanes(j), :])
+            low = (value * slopes[:, lanes(j)].astype(F32)).astype(BF16)
+            slopes[:, lanes(j)] = low
+            total = jnp.sum(low.astype(F32), 0, keepdims=True)
+            buf.sg[10:11, lanes(j)] = buf.sg[10:11, lanes(j)] + total
+
+        loop(FL // 256, one)
+
+    def weight_grads(left, right, left_b, right_b, name):
+        def one(j):
+            total = tn(left[:, lanes(j)], right[...]) + tn(left_b[:, lanes(j)], right_b[...])
+            name.grad[lanes(j), :] = total.astype(BF16)
+
+        loop(left.shape[1] // 256, one)
+
+    def fold(ticket, dst):
+        def one(i):
+            place = part(i, TILE)
+            dst[place, :] = reduced(ticket, place).astype(BF16)
+
+        loop(L // TILE, one)
+
+    def on_mid(fn, *args):
+        run_if(mid, lambda: fn(*args))
 
     def cot_sum(i, carry):
         return carry + jnp.sum(rows(buf.e3, q)[part(i, TILE), :].astype(F32), 0, keepdims=True)
 
-    buf.sg[8:9, :] = lax.fori_loop(0, L // TILE, cot_sum, zero)
+    buf.sg[8:9, :] = lax.fori_loop(0, L // TILE, cot_sum, jnp.zeros((1, D), F32))
+
+    gather_relay(a3)
+    arrived(rows(buf.e3b, q), k_units, mid)
+    e3b = gather_start(buf.e3b, mid)
+    gather_ready(a3)
+    inner_ready(wt.f1)
+    on_mid(units, buf.a3, buf.g, buf.gp)
+    wt.f2.own_copy[0].wait()
+    inner_ready(wt.f2)
+    on_mid(units_back, buf.e3, buf.gp)
+    arrived(rows(buf.a3b, q), k_units + 1, mid)
+    a3b = gather_start(buf.a3b, mid)
+    gather_relay(e3b)
+    on_mid(matmul_back, buf.gp, wt.f1.weight, set_a.parts)
+    step = reduce_start(set_a, mid)
+    gather_ready(e3b)
+    gather_finish(a3b)
+    reduce_relay(step)
+    on_mid(units, buf.a3b, buf.gb, buf.gpb)
+    on_mid(units_back, buf.e3b, buf.gpb)
+    on_mid(matmul_back, buf.gpb, wt.f1.weight, set_b.parts)
+    step_b = reduce_start(set_b, mid)
+    on_mid(matmul, buf.gb, wt.f2.weight, set_c.parts)
+    reduce_relay(step_b)
+    final = reduce_start(set_c, mid)
+    on_mid(weight_grads, buf.g, buf.e3, buf.gb, buf.e3b, wt.f2)
+    inner_grad_far(wt.f2)
+    on_mid(weight_grads, buf.a3, buf.gp, buf.a3b, buf.gpb, wt.f1)
+    inner_grad_far(wt.f1)
+    inner_grad_near(wt.f2)
+    inner_grad_near(wt.f1)
+    reduce_ready(step_b)
+    on_mid(fold, step_b, buf.back)
+    send(buf.back, buf.back, k_units + 2, dev_adj, mid)
 
     def store(name):
         def low(place, value):
@@ -1067,22 +1209,30 @@
 
         return low
 
-    buf.sg[7:8, :] = norm_back(
-        lambda place: buf.h2[place, :], step, 2,
-        lambda place: rows(buf.e3, q)[place, :].astype(F32), buf.dh, store(buf.e2),
-    )
+    def units_norm_back(incoming):
+        norm_back(
+            lambda place: buf.h2[place, :], incoming, 2,
+            lambda place: rows(buf.e3, q)[place, :].astype(F32), buf.dh, store(buf.e2), 7,
+        )
+
+    reduce_done(e3)
+    sent(to_middle)
+    reduce_ready(step)
+    on_mid(units_norm_back, lambda place: reduced(step, place))
+    arrived(buf.back, k_units + 2, end)
+    run_if(end, lambda: units_norm_back(lambda place: buf.back[place, :].astype(F32)))
     e2 = gather_start(buf.e2)
     reduce_done(step)
+    reduce_done(step_b)
+    gather_finish(e2)
     reduce_relay(final)
-    grad_combine(wt.f2)
-    gather_finish(e2)
-
+
+    weight_grad(buf.o2, buf.e2, wt.co)
+    grad_send(wt.co)
     matmul_back(buf.e2, wt.co.weight, buf.do)
     attention_back(buf.q2, 0, buf.kv, 0, 2, buf.p2, buf.do)
     matmul_back(buf.q2, wt.cq.weight, set_b.parts)
     step = reduce_start(set_b)
-    weight_grad(buf.o2, buf.e2, wt.co)
-    grad_send(wt.co)
     weight_grad(buf.a2, buf.q2, wt.cq)
     grad_send(wt.cq)
     reduce_relay(step)
@@ -1090,66 +1240,80 @@
     grad_send(wt.ckv)
     matmul_back(buf.kv, wt.ckv.weight, set_a.parts)
     mem_step = reduce_start(set_a)
-    reduce_ready(final)
-
-    def finish(i):
-        place = part(i, TILE)
-        total = buf.h2[place, :] + (reduced(final, place) + buf.vec[8:9, :])
-        buf.stage[place, :] = total.astype(BF16)
-
-    loop(L // TILE, finish)
-    result_copies.append(local(buf.stage, io.output))
-    reduce_done(final)
     column_sums(buf.q2, 0, 1, 9, 2)
     column_sums(buf.kv, 1, 1, 9, 3)
+    reduce_ready(final)
+    on_mid(fold, final, buf.tail)
+    send(buf.tail, buf.tail, k_units + 3, dev_adj, mid)
+    reduce_done(final)
+    grad_combine(wt.co)
     reduce_ready(step)
-    buf.sg[6:7, :] = norm_back(
-        lambda place: buf.h1[place, :], step, 1,
-        lambda place: buf.dh[place, :], buf.dh, store(buf.e1),
-    )
-    e1 = gather_start(buf.e1)
+    norm_back(
+        lambda place: buf.h1[place, :], lambda place: reduced(step, place), 1,
+        lambda place: buf.dh[place, :], buf.dh, store(buf.e3), 6,
+    )
+    e1 = gather_start(buf.e3)
     reduce_done(step)
+    grad_combine(wt.cq)
+    grad_outward(wt.co)
+    gather_finish(e1)
     reduce_relay(mem_step)
-    grad_combine(wt.f1)
-    gather_finish(e1)
-
-    matmul_back(buf.e1, wt.so.weight, buf.do)
+
+    weight_grad(buf.o1, buf.e3, wt.so)
+    grad_send(wt.so)
+    matmul_back(buf.e3, wt.so.weight, buf.do)
     attention_back(buf.qkv, 0, buf.qkv, 2, 4, buf.p1, buf.do)
+    weight_grad(buf.a1, buf.qkv, wt.qkv)
+    far_part = grad_send_far(wt.qkv)
     matmul_back(buf.qkv, wt.qkv.weight, set_b.parts)
     step = reduce_start(set_b)
-    weight_grad(buf.o1, buf.e1, wt.so)
-    grad_send(wt.so)
-    weight_grad(buf.a1, buf.qkv, wt.qkv)
-    grad_send(wt.qkv)
-    reduce_relay(step)
     column_sums(buf.qkv, 0, 1, 9, 0)
     column_sums(buf.qkv, 2, 1, 9, 1)
+    inner_grad_combine(wt.f2)
+    inner_grad_combine(wt.f1)
+    reduce_relay(step)
+    grad_combine(wt.ckv)
+    grad_outward(wt.cq)
+    on_mid(matmul, buf.g, wt.f2.weight, set_c.parts)
+    final = reduce_start(set_c, mid)
 
     reduce_ready(mem_step)
-
-    def memory_row(i):
-        place = part(i, TILE)
-        buf.mb[place, :] = reduced(mem_step, place).astype(BF16)
-
-    loop(L // TILE, memory_row)
+    fold(mem_step, buf.mb)
     k_back = slot(n_sec)
     for j in range(1, n_sec):
         to = (s + j) % n_sec
         send(buf.mb.at[:, part(to, mem_cols)], buf.ml.at[j], k_back + j, (to, d))
-    grad_combine(wt.co)
-    grad_combine(wt.cq)
+    sent(far_part)
+    middle_part = grad_send_middle(wt.qkv)
+    grad_outward(wt.ckv)
     reduce_ready(step)
 
     def store_stage(place, value):
         buf.ig[place, :] = value
 
     norm_back(
-        hidden, step, 0, lambda place: buf.dh[place, :], None, store_stage,
+        hidden, lambda place: reduced(step, place), 0,
+        lambda place: buf.dh[place, :], None, store_stage,
     )
     k_in = slot()
     send(buf.ig, io.input_grad, k_in, ((s + n_sec - 1) % n_sec, d))
     buf.sga[q, z] = buf.sg[...].astype(BF16)
     sums = spread_start(buf.sga, None)
+    reduce_relay(final)
+    grad_combine(wt.so)
+    sent(middle_part)
+    grad_send_near(wt.qkv)
+
+    def finish(incoming):
+        def one(i):
+            place = part(i, TILE)
+            total = buf.h2[place, :] + (incoming(place) + buf.vec[8:9, :])
+            buf.stage[place, :] = total.astype(BF16)
+
+        loop(L // TILE, one)
+
+    arrived(buf.tail, k_units + 3, end)
+    run_if(end, lambda: finish(lambda place: buf.tail[place, :].astype(F32)))
     for j in range(1, n_sec):
         arrived(buf.ml.at[j], k_back + j)
 
@@ -1162,19 +1326,21 @@
 
     loop(L // TILE, memory_total)
     result_copies.append(local(buf.mo, io.memory_grad))
-    grad_final(wt.f2)
-    grad_final(wt.f1)
-    grad_combine(wt.ckv)
-    for weight in (wt.co, wt.cq, wt.ckv):
+    grad_outward(wt.so)
+    grad_combine_far(wt.qkv)
+    for weight in (wt.co, wt.cq, wt.ckv, wt.f2, wt.f1):
         grad_final(weight)
-    grad_combine(wt.so)
-    grad_combine(wt.qkv)
-    unit_last_wait()
+    spread_relay(sums)
+    grad_combine_middle(wt.qkv)
+    reduce_ready(final)
+    on_mid(finish, lambda place: reduced(final, place))
+    result_copies.append(local(buf.stage, io.output))
+    grad_outward(wt.qkv)
+    grad_final(wt.so)
     last_wait(wt.ckv)
     last_wait(wt.cq)
-    spread_relay(sums)
-    for weight in (wt.so, wt.qkv):
-        grad_final(weight)
+    unit_last_wait()
+    grad_final(wt.qkv)
     spread_ready(sums)
 
     def per_unit(q_at, at):
@@ -1224,7 +1390,8 @@
         qkv=(T, 768), q2=(T, 256), kv=(T, 512), o1=(T, 256), o2=(T, 256), do=(T, 256),
         p1=(2 * P_IN, 2 * L, L), p2=(2 * P_IN, 2 * L, L),
         g=(T, FL), gp=(T, FL),
-        a1=tokens, a2=tokens, a3=tokens, m=tokens, e3=tokens, e2=tokens, e1=tokens,
+        a1=tokens, a2=tokens, a3=tokens, m=tokens, e3=tokens, e2=tokens,
+        a3b=tokens, e3b=tokens, gb=(T, FL), gpb=(T, FL), back=row, tail=row,
     )
     exact = dict(vec=(16, D), bias=(8, D), sg=(16, D), sums=(16, 128), h1=row, h2=row, dh=row)
     kinds = {name: pltpu.VMEM(shape, BF16) for name, shape in shapes.items()}
@@ -1244,7 +1411,9 @@
     scratch += 3 * list(REDUCE_SHAPES.values())
     for count, columns, _ in WEIGHTS.values():
         scratch += 2 * [pltpu.VMEM((Z * count, columns), BF16)]
-        scratch += 4 * [pltpu.VMEM((count, columns), BF16)]
+        scratch += 2 * [pltpu.VMEM((count, columns), BF16)]
+    for count, columns, _ in list(WEIGHTS.values())[:5]:
+        scratch += 3 * [pltpu.VMEM((count, columns), BF16)]
     for columns in (768, 512, 256):
         scratch.append(pltpu.VMEM((64, P_IN * columns), BF16))
         scratch.append(pltpu.VMEM((P_IN, 64, columns), BF16))
@@ -1253,6 +1422,46 @@
         pltpu.SemaphoreType.DMA((SEMS,)),
         pltpu.SemaphoreType.DMA((48,)),
     ]
+
+
+def finish_kernel(*refs):
+    moved, low, sums = refs[:3], refs[3:10], refs[10]
+    moved_out, high, small = refs[11:14], refs[14:21], refs[21:27]
+    low_buf, high_buf, moved_buf, sems = refs[27:34], refs[34:41], refs[41:44], refs[44]
+    inward = [
+        pltpu.make_async_copy(src, dst, sems.at[i])
+        for i, (src, dst) in enumerate(zip(low + moved, low_buf + moved_buf))
+    ]
+    for copy in inward:
+        copy.start()
+    outward = []
+    gain, shift, out_bias, self_bias, cross_bias, unit_bias = small
+    gain[0] = sums[0:3, 0:64]
+    shift[0] = sums[3:6, 0:64]
+    out_bias[0] = sums[6:9, 0:64]
+    self_bias[...] = sums[9:10, :]
+    cross_bias[...] = sums[10:11, :]
+    unit_bias[:, 0:128] = sums[11:12, :]
+    unit_bias[:, 128:256] = sums[12:13, :]
+    for i, copy in enumerate(inward[:7]):
+        copy.wait()
+        rows_in = low_buf[i].shape[0]
+
+        def one(j, i=i):
+            place = part(j, 16)
+            high_buf[i][place, :] = low_buf[i][place, :].astype(F32)
+
+        loop(rows_in // 16, one)
+        back = pltpu.make_async_copy(high_buf[i], high[i], sems.at[10 + i])
+        back.start()
+        outward.append(back)
+    for i, copy in enumerate(inward[7:]):
+        copy.wait()
+        back = pltpu.make_async_copy(moved_buf[i], moved_out[i], sems.at[17 + i])
+        back.start()
+        outward.append(back)
+    for copy in outward:
+        copy.wait()
 
 
 def on_device_planes(
@@ -1280,30 +1489,49 @@
         out_specs=[anywhere] * (len(out_shapes) + 1),
         scratch_shapes=scratch_of(n_sec, mem_cols),
         compiler_params=pltpu.CompilerParams(
-            collective_id=0, has_side_effects=True, vmem_limit_bytes=63 * 2**20
+            collective_id=0, has_side_effects=True, vmem_limit_bytes=64 * 2**20 - 2**16
         ),
         cost_estimate=pl.CostEstimate(
             flops=21 * 10**9, bytes_accessed=20 * 2**20, transcendentals=3 * 10**6
         ),
     )(*operands)
-    output, input_grad, memory_grad, g_qkv, g_so, g_ckv, g_cq, g_co, g_f1, g_f2, sums = results
+    shapes = [result.shape for result in results]
+    vmem = pl.BlockSpec(memory_space=pltpu.VMEM)
+    finished = pl.pallas_call(
+        finish_kernel,
+        out_shape=[jax.ShapeDtypeStruct(shape, BF16) for shape in shapes[:3]]
+        + [jax.ShapeDtypeStruct(shape, F32) for shape in shapes[3:10]]
+        + [jax.ShapeDtypeStruct(shape, F32) for shape in [(1, 3, 64)] * 3 + [(1, 128), (1, 128), (1, 256)]],
+        in_specs=10 * [anywhere] + [vmem],
+        out_specs=10 * [anywhere] + 6 * [vmem],
+        scratch_shapes=[pltpu.VMEM(shape, BF16) for shape in shapes[3:10]]
+        + [pltpu.VMEM(shape, F32) for shape in shapes[3:10]]
+        + [pltpu.VMEM(shape, BF16) for shape in shapes[:3]]
+        + [pltpu.SemaphoreType.DMA((20,))],
+        compiler_params=pltpu.CompilerParams(vmem_limit_bytes=63 * 2**20),
+        cost_estimate=pl.CostEstimate(flops=0, bytes_accessed=9 * 2**20, transcendentals=0),
+    )(*results)
+    (
+        output, input_grad, memory_grad, g_qkv, g_so, g_ckv, g_cq, g_co, g_f1, g_f2,
+        gain, shift, biases, self_biases, cross_biases, units,
+    ) = finished
     return (
         output[None, None],
         input_grad[None, None],
         memory_grad[None],
-        sums[None, 0:3, 0:64],
-        sums[None, 3:6, 0:64],
-        g_qkv[None].astype(F32),
-        sums[9:10],
-        g_so[None].astype(F32),
-        g_cq[None].astype(F32),
-        g_ckv[None].astype(F32),
-        sums[10:11],
-        g_co[None].astype(F32),
-        sums[None, 6:9, 0:64],
-        g_f1[None].astype(F32),
-        sums[11:13].reshape(1, 256),
-        g_f2[None].astype(F32),
+        gain,
+        shift,
+        g_qkv[None],
+        self_biases,
+        g_so[None],
+        g_cq[None],
+        g_ckv[None],
+        cross_biases,
+        g_co[None],
+        biases,
+        g_f1[None],
+        units,
+        g_f2[None],
     )
 
 

time: 317 us -> 268 us (0.85)
  Pallas kernels: 302 us -> 262 us
  other arithmetic: 6.48 us -> 0 us
  local copies, waits for them, and re-layouts: 6.03 us -> 2.6 us
    pallas_call x1, Pallas kernels: 302 us -> 258 us  [on_device_planes(): pl.pallas_call(functools.partial(whole_kernel, n_sec, mem_cols), out_shap...]
    convert_element_type x6 -> x0, other arithmetic: 6.48 us -> none  [the longest x1 1.87 us: on_device_planes(): g_co[None].astype(F32)]
    pallas_call x0 -> x1, Pallas kernels: none -> 4.85 us  [on_device_planes(): pl.pallas_call(finish_kernel, out_shape=[jax.ShapeDtypeStruct(shape, BF16...]
where the time goes in v3:
time: 268 us; the launch traced here: 267 us
  Pallas kernels  262 us (98%)
    pallas_call x1, Pallas kernels, on_device_planes(): pl.pallas_call(functools.partial(whole_kernel, n_sec, mem_cols), out_shap...  258 us

profile of v3, /device:TPU:1, one launch (start us, length us, event | category | flops | bytes accessed | tf_op | source)
XLA Modules:
  0.0 267.0 jit_solution(12715693514979543963)
XLA Ops:
  1.9 257.6 %shard_map.297 = (bf16[192,1024]{1,0:T(8,128)(2,1)}, bf16[192,1024]{1,0:T(8,128)(2,1)}, bf16[192,512]{1,0:T(8,128)(2,1)}, bf16[64,3072]{1,0:T(8,128)(2,1)}, bf16...) custom-call(bf16[192,1024]{1,0:T(8,128)(2,1)} %bitcast.29, ...), custom_call_target="tpu_custom_call" | custom-call | flops 20999999488 | bytes 20971520 | tf_op jit(solution)/shard_map/pallas_call | solution.py:1485
  259.6 4.9 %shard_map.298 = (bf16[192,1024]{1,0:T(8,128)(2,1)}, bf16[192,1024]{1,0:T(8,128)(2,1)}, bf16[192,512]{1,0:T(8,128)(2,1)}, f32[64,3072]{1,0:T(8,128)}, f32[64,102...) custom-call(bf16[192,1024]{1,0:T(8,128)(2,1)} %get-tuple-element.43., ...), custom_call_target="tpu_custom_call" | custom-call | bytes 9437184 | tf_op jit(solution)/shard_map/pallas_call | solution.py:1500
  264.4 0.0 copy-start.2
  264.4 0.7 copy-done.2
  265.1 0.0 copy-start.1
  265.1 0.6 copy.34
  265.7 0.1 copy-done.1
  265.8 0.0 copy-start
  265.8 0.6 copy.35
  266.4 0.1 copy-done
  266.5 0.6 copy.36
Async XLA Ops:
  264.4 0.7 copy-start.2
  265.1 0.7 copy-start.1
  265.8 0.7 copy-start

commit v4 on v3

--- a/solution.py
+++ b/solution.py
@@ -349,7 +349,7 @@
     f1=(256, 1024, True),
     f2=(256, 1024, False),
 )
-SEMS = 240
+SEMS = 320
 
 
 def run_if(cond, fn):
@@ -375,12 +375,16 @@
     return lax.dot_general(left, right, (((0,), (0,)), ((), ())), preferred_element_type=F32)
 
 
-def loop(count, body, unroll=1):
+def loop(count, body, unroll=1, first=0):
     def step(index, carry):
         body(index)
         return carry
 
-    lax.fori_loop(0, count, step, 0, unroll=unroll)
+    lax.fori_loop(first, first + count, step, 0, unroll=unroll)
+
+
+HALF = L // 2
+TILES = HALF // TILE
 
 
 def gelu_pair(values):
@@ -477,11 +481,14 @@
     def arrived(dst, k, cond=None):
         run_if(cond, remote(dst, dst, k, dev_core).wait_recv)
 
-    def local(src, dst):
+    def local(src, dst, cond=None):
         copy = pltpu.make_async_copy(src, dst, local_sems.at[local_counter[0]])
         local_counter[0] += 1
-        copy.start()
+        run_if(cond, copy.start)
         return copy
+
+    def keep(src, dst, cond=None):
+        result_copies.append((local(src, dst, cond), cond))
 
     def rows(rows_of, index):
         return rows_of.at[part(index, L)]
@@ -672,20 +679,13 @@
         run_if(mid, add)
         send(name.far, name.near, k + 2, dev_adj, mid)
 
-    def inner_grad_total(name):
+    def inner_grad_total(name, cond):
         k = name.to_sum
-        arrived(name.near, k + 2, end)
-
-        def add():
-            arrived(name.near, k + 1)
-
-            def one(place):
-                own = grad_block(name, z)[place, :].astype(F32)
-                name.near[place, :] = (own + name.near[place, :].astype(F32)).astype(BF16)
-
-            add_rows(name.count, one)
-
-        run_if(mid, add)
+        if cond is end:
+            arrived(name.near, k + 2, end)
+        else:
+            arrived(name.near, k + 1, mid)
+            run_if(mid, lambda: grad_add(name, name.near, z))
 
     def grad_total(name):
         k = name.to_sum
@@ -704,28 +704,28 @@
         run_if(end, lambda: grad_add(name, name.near, z))
 
     def grad_final(name):
-        count = name.count
-        if name is wt.f1 or name is wt.f2:
-            inner_grad_total(name)
-        else:
-            grad_total(name)
-        size = count // P_IN
-        if name is wt.f1:
-            for tile in range(Z):
-                for j, (q_to, device) in enumerate(in_plane):
-                    src = name.near.at[part(q_to, size), part(tile, 256)]
-                    dst = unit_columns(name.result, tile, q)
-                    send(src, dst, unit_last + 3 * tile + j, device)
-                src = name.near.at[part(q, size), part(tile, 256)]
-                result_copies.append(local(src, unit_columns(name.result, tile, q)))
-        elif name.by_column:
+        grad_total(name)
+        if name.by_column:
+            size = name.count // P_IN
             for j, (q_to, device) in enumerate(in_plane):
                 src = name.near.at[part(q_to, size)]
                 send(src, name.sorted.at[q], name.last + j, device)
             src = name.near.at[part(q, size)]
             name.own_copy = [local(src, name.sorted.at[q])]
         else:
-            result_copies.append(local(name.near, name.result))
+            keep(name.near, name.result)
+
+    def inner_final(cond):
+        inner_grad_total(wt.f2, cond)
+        keep(wt.f2.near, wt.f2.result, cond)
+        inner_grad_total(wt.f1, cond)
+        size = wt.f1.count // P_IN
+        for tile in range(Z):
+            dst = unit_columns(wt.f1.result, tile, q)
+            for j, (q_to, device) in enumerate(in_plane):
+                src = wt.f1.near.at[part(q_to, size), part(tile, 256)]
+                send(src, dst, unit_last + 3 * tile + j, device, cond)
+            keep(wt.f1.near.at[part(q, size), part(tile, 256)], dst, cond)
 
     def last_wait(name):
         for j, (q_from, _) in enumerate(in_plane):
@@ -733,7 +733,7 @@
         for copy in name.own_copy:
             copy.wait()
         unsort_columns(name)
-        result_copies.append(local(name.raw, name.result))
+        keep(name.raw, name.result)
 
     def unit_last_wait():
         for tile in range(Z):
@@ -741,54 +741,110 @@
                 place = unit_columns(wt.f1.result, tile, q_from)
                 arrived(place, unit_last + 3 * tile + j)
 
+    def piece(name, index, h, parts):
+        size = L // parts
+        return name.at[part(index * parts + h, size)]
+
+    def half_major(name, index, h, parts=2):
+        return name.at[part(h * P_IN + index, HALF)]
+
+    def gather_open(name, cond=None, parts=1, lay=piece):
+        return name, slot(3 * parts), [], cond, parts, lay
+
+    def gather_part(ticket, h, cond=None):
+        name, k, records, usual, parts, lay = ticket
+        cond = usual if cond is None else cond
+        own = lay(name, q, h, parts)
+        records.append(send(own, own, k + 3 * h, dev_x, cond))
+        records.append(send(own, own, k + 3 * h + 1, dev_core, cond))
+
     def gather_start(name, cond=None):
-        k = slot(3)
-        first = send(rows(name, q), rows(name, q), k, dev_x, cond)
-        second = send(rows(name, q), rows(name, q), k + 1, dev_core, cond)
-        return name, k, [first, second], cond
+        ticket = gather_open(name, cond)
+        gather_part(ticket, 0)
+        return ticket
+
+    def gather_relay_part(ticket, h):
+        name, k, records, cond, parts, lay = ticket
+        other = lay(name, q_x, h, parts)
+        arrived(other, k + 3 * h, cond)
+        records.append(send(other, other, k + 3 * h + 2, dev_core, cond))
+
+    def gather_ready_part(ticket, h):
+        name, k, _, cond, parts, lay = ticket
+        arrived(lay(name, q_core, h, parts), k + 3 * h + 1, cond)
+        arrived(lay(name, q_xc, h, parts), k + 3 * h + 2, cond)
 
     def gather_relay(ticket):
-        name, k, records, cond = ticket
-        arrived(rows(name, q_x), k, cond)
-        records.append(send(rows(name, q_x), rows(name, q_x), k + 2, dev_core, cond))
+        for h in range(ticket[4]):
+            gather_relay_part(ticket, h)
 
     def gather_ready(ticket):
-        name, k, _, cond = ticket
-        arrived(rows(name, q_core), k + 1, cond)
-        arrived(rows(name, q_xc), k + 2, cond)
+        for h in range(ticket[4]):
+            gather_ready_part(ticket, h)
 
     def gather_finish(ticket):
         gather_relay(ticket)
         gather_ready(ticket)
 
     def reduce_start(which, cond=None):
-        k = slot(3)
+        k = slot(4)
         out = which.parts
         first = send(rows(out, q_xc), rows(which.core, 1), k, dev_core, cond)
         second = send(rows(out, q_core), rows(which.core, 0), k + 1, dev_core, cond)
-        return which, k, [first, second], cond
-
-    def reduce_relay(ticket):
-        which, k, records, cond = ticket
-        out = which.parts
-        arrived(rows(which.core, 1), k, cond)
+        return which, k, [first, second], cond, piece
+
+    def reduce_open(which, cond):
+        return which, slot(6), [], cond, half_major
+
+    def reduce_start_half(ticket, h):
+        which, k, records, cond, lay = ticket
+        for j, index in ((1, q_xc), (0, q_core)):
+            src, dst = lay(which.parts, index, h), piece(which.core, j, h, 2)
+            records.append(send(src, dst, k + 4 * h + 1 - j, dev_core, cond))
+
+    def reduce_relay_half(ticket, h):
+        which, k, records, cond, lay = ticket
+        landed = piece(which.core, 1, h, 2)
+        if lay is half_major:
+            arrived(landed, k + 4 * h, cond)
+        elif h == 0:
+            arrived(rows(which.core, 1), k, cond)
+        mine = lay(which.parts, q_x, h, 2)
 
         def add():
             def one(i):
-                mine = rows(out, q_x)
                 place = part(i, TILE)
-                total = mine[place, :].astype(F32) + rows(which.core, 1)[place, :].astype(F32)
+                total = mine[place, :].astype(F32) + landed[place, :].astype(F32)
                 mine[place, :] = total.astype(BF16)
 
-            loop(L // TILE, one)
+            loop(TILES, one)
 
         run_if(cond, add)
-        records.append(send(rows(out, q_x), which.across, k + 2, dev_x, cond))
+        dst = which.across.at[part(h, HALF)]
+        records.append(send(mine, dst, k + 2 + h, dev_x, cond))
+        return records[-1]
+
+    def reduce_relay(ticket):
+        reduce_relay_half(ticket, 0)
+        reduce_relay_half(ticket, 1)
+
+    def reduce_relay_paced(ticket):
+        record = reduce_relay_half(ticket, 0)
+        ticket[2][:] = [other for other in ticket[2] if other is not record]
+        sent(record)
+        reduce_relay_half(ticket, 1)
+
+    def reduce_ready_half(ticket, h):
+        which, k, _, cond, lay = ticket
+        if lay is half_major:
+            arrived(piece(which.core, 0, h, 2), k + 4 * h + 1, cond)
+        elif h == 0:
+            arrived(rows(which.core, 0), k + 1, cond)
+        arrived(which.across.at[part(h, HALF)], k + 2 + h, cond)
 
     def reduce_ready(ticket):
-        which, k, _, cond = ticket
-        arrived(rows(which.core, 0), k + 1, cond)
-        arrived(which.across, k + 2, cond)
+        reduce_ready_half(ticket, 0)
+        reduce_ready_half(ticket, 1)
 
     def reduced(ticket, place):
         which = ticket[0]
@@ -796,39 +852,46 @@
         total = total + rows(which.core, 0)[place, :].astype(F32)
         return total + which.across[place, :].astype(F32)
 
+    def fold(ticket, dst, halves=(0, 1)):
+        which, lay = ticket[0], ticket[4]
+        for h in halves:
+            mine, landed = lay(which.parts, q, h, 2), piece(which.core, 0, h, 2)
+
+            def one(i, h=h, mine=mine, landed=landed):
+                place, here = part(i, TILE), part(i + h * TILES, TILE)
+                total = mine[place, :].astype(F32) + landed[place, :].astype(F32)
+                dst[here, :] = (total + which.across[here, :].astype(F32)).astype(BF16)
+
+            loop(TILES, one)
+
     def reduce_done(ticket):
         for record in ticket[2]:
             sent(record)
 
-    def spread_start(name, src):
+    def spread_start(place):
         k = slot(8)
-        place = name.at[q, z]
-        copy = None
-        if src is not None:
-            copy = local(src, place)
-        else:
-            src = place
-        send(src, place, k, dev_adj)
-        send(src, place, k + 1, dev_opp, mid)
-        send(src, place, k + 2, dev_diag, end)
-        return name, k, copy
+        send(place(z), place(z), k, dev_adj)
+        send(place(z), place(z), k + 1, dev_opp, mid)
+        send(place(z), place(z), k + 2, dev_diag, end)
+        return place, k
 
     def spread_relay(ticket):
-        name, k, copy = ticket
-        arrived(name.at[q, z_opp], k + 1, mid)
-        send(name.at[q, z_opp], name.at[q, z_opp], k + 3, dev_adj, mid)
-        arrived(name.at[q, z_diag], k + 2, mid)
-        send(name.at[q, z_diag], name.at[q, z_diag], k + 4, dev_adj, mid)
-        arrived(name.at[q, z_adj], k)
-        arrived(name.at[q, z_diag], k + 3, end)
-        arrived(name.at[q, z_opp], k + 4, end)
-        if copy is not None:
-            copy.wait()
+        place, k = ticket
+        arrived(place(z_opp), k + 1, mid)
+        send(place(z_opp), place(z_opp), k + 3, dev_adj, mid)
+        arrived(place(z_diag), k + 2, mid)
+        send(place(z_diag), place(z_diag), k + 4, dev_adj, mid)
+        arrived(place(z_adj), k)
+        arrived(place(z_diag), k + 3, end)
+        arrived(place(z_opp), k + 4, end)
+
+    def spread_plane(ticket, name):
+        k = ticket[1]
         for j, (_, device) in enumerate(in_plane):
             send(name.at[q], name.at[q], k + 5 + j, device)
 
-    def spread_ready(ticket):
-        name, k, _ = ticket
+    def spread_ready(ticket, name):
+        k = ticket[1]
         for j, (q_from, _) in enumerate(in_plane):
             arrived(name.at[q_from], k + 5 + j)
 
@@ -846,15 +909,18 @@
 
         loop(count, one)
 
-    def matmul_back(left, right, dst):
+    def matmul_back(left, right, dst, at=slice(0, T)):
         def one(j):
-            dst[:, lanes(j)] = nt(left[...], right[lanes(j), :]).astype(BF16)
+            dst[at, lanes(j)] = nt(left[at, :], right[lanes(j), :]).astype(BF16)
 
         loop(right.shape[0] // 256, one)
 
-    def weight_grad(left, right, name):
+    def weight_grad(left, right, name, more=False):
         def one(j):
-            name.grad[lanes(j), :] = tn(left[:, lanes(j)], right[...]).astype(BF16)
+            total = tn(left[:, lanes(j)], right[...])
+            if more:
+                total = total + name.grad[lanes(j), :].astype(F32)
+            name.grad[lanes(j), :] = total.astype(BF16)
 
         loop(left.shape[1] // 256, one)
 
@@ -920,16 +986,16 @@
 
         loop(count, one)
 
-    def norm(load, index, dst):
+    def norm(load, index, dst, halves=(0, 1)):
         def one(i):
             place = part(i, TILE)
             normed, _ = whiten(load(place))
             gain, shift = buf.vec[index:index + 1, :], buf.vec[index + 3:index + 4, :]
             rows(dst, q)[place, :] = (normed * gain + shift).astype(BF16)
 
-        loop(L // TILE, one)
-
-    def norm_back(load, incoming, index, base, dst, low, out_row=None):
+        loop(TILES * len(halves), one, first=TILES * halves[0])
+
+    def norm_back(load, incoming, index, base, dst, low, out_row=None, halves=(0, 1)):
         zero = jnp.zeros((1, D), F32)
 
         def one(i, carry):
@@ -951,11 +1017,13 @@
                 out_sum + jnp.sum(rounded.astype(F32), 0, keepdims=True),
             )
 
-        gain_sum, shift_sum, out_sum = lax.fori_loop(0, L // TILE, one, (zero, zero, zero))
-        buf.sg[index:index + 1, :] = gain_sum
-        buf.sg[index + 3:index + 4, :] = shift_sum
+        first = TILES * halves[0]
+        last = first + TILES * len(halves)
+        gain_sum, shift_sum, out_sum = lax.fori_loop(first, last, one, (zero, zero, zero))
+        buf.sg[index:index + 1, :] = buf.sg[index:index + 1, :] + gain_sum
+        buf.sg[index + 3:index + 4, :] = buf.sg[index + 3:index + 4, :] + shift_sum
         if out_row is not None:
-            buf.sg[out_row:out_row + 1, :] = out_sum
+            buf.sg[out_row:out_row + 1, :] = buf.sg[out_row:out_row + 1, :] + out_sum
 
     gate = pltpu.get_barrier_semaphore()
     partners = [device for _, device in in_plane] + [dev_adj, dev_opp, dev_diag]
@@ -982,10 +1050,14 @@
     sort_columns(wt.qkv)
     pl.semaphore_wait(gate, len(partners))
 
-    sv = spread_start(buf.sva, None)
+    sv = spread_start(lambda plane: buf.sva.at[q, plane])
     swap_start(wt.qkv)
     k_prev, k_cot, k_mem = slot(), slot(), slot(n_sec)
     send(io.prev, buf.hb, k_prev, ((s + 1) % n_sec, d))
+    for weight in (wt.so, wt.co):
+        send_inward(weight, weight.source)
+        send_across(weight, weight.source)
+        weight_outward(weight, weight.source)
     mem_slot = rows(buf.m, q)
     for j in range(1, n_sec):
         send(io.mem, mem_slot.at[:, part(s, mem_cols)], k_mem + j, ((s + j) % n_sec, d))
@@ -998,12 +1070,14 @@
         sort_columns(weight)
         swap_start(weight)
 
-    spread_relay(sv)
     swap_wait(wt.qkv)
     send_inward(wt.qkv, block(wt.qkv, z))
     send_across(wt.qkv, block(wt.qkv, z))
     weight_outward(wt.qkv, block(wt.qkv, z))
-    spread_ready(sv)
+    unit_swap_start()
+    spread_relay(sv)
+    spread_plane(sv, buf.sva)
+    spread_ready(sv, buf.sva)
 
     for tile in range(D // 128):
         pair = buf.sva[2 * (tile % 2), tile // 2].astype(F32)
@@ -1037,8 +1111,6 @@
     a1 = gather_start(buf.a1)
     relay_inward(wt.qkv)
     relay_near(wt.qkv)
-    weight_outward(wt.so, wt.so.source)
-    send_inward(wt.so, wt.so.source)
     swap_wait(wt.ckv)
     send_inward(wt.ckv, block(wt.ckv, z))
     for j in range(1, n_sec):
@@ -1047,22 +1119,26 @@
     mem_copy.wait()
     gather_relay(a1)
     memory = gather_start(buf.m)
-    unit_swap_start()
-    send_across(wt.so, wt.so.source)
     relay_inward(wt.so)
     swap_wait(wt.cq)
     send_inward(wt.cq, block(wt.cq, z))
-    send_inward(wt.co, wt.co.source)
     relay_far(wt.qkv)
     arrived(rows(buf.e3, q), k_cot)
-    k_units = slot(4)
-    to_middle = send(rows(buf.e3, q), rows(buf.e3b, q), k_units, dev_adj, end)
+    k_units = slot(16)
+    to_middle = [send(rows(buf.e3, q), rows(buf.e3, q), k_units + 9, dev_x, end)]
+
+    def cot_inward(index, k):
+        for h in range(2):
+            src, dst = piece(buf.e3, index, h, 2), half_major(buf.e3b, index, h)
+            to_middle.append(send(src, dst, k + h, dev_adj, end))
+
+    cot_inward(q, k_units)
     gather_ready(a1)
+    unit_swap_wait(end)
+    send_inward(wt.f1, block(wt.f1, z))
     weight_ready(wt.qkv)
     matmul(buf.a1, wt.qkv.weight, buf.qkv, buf.bias, 0)
     send_across(wt.ckv, block(wt.ckv, z))
-    unit_swap_wait(end)
-    send_inward(wt.f1, block(wt.f1, z))
     attention(buf.qkv, 0, buf.qkv, 2, 4, True, 13, buf.p1, buf.o1)
     relay_inward(wt.ckv)
     relay_near(wt.so)
@@ -1077,10 +1153,11 @@
     relay_inward(wt.cq)
     weight_outward(wt.cq, block(wt.cq, z))
     reduce_relay(step)
+    arrived(rows(buf.e3, q_x), k_units + 9, end)
+    cot_inward(q_x, k_units + 2)
     relay_near(wt.ckv)
     gather_finish(memory)
     relay_far(wt.ckv)
-    send_across(wt.co, wt.co.source)
     relay_inward(wt.co)
     unit_swap_wait(mid)
     send_across(wt.f1, block(wt.f1, z))
@@ -1095,7 +1172,6 @@
     a2 = gather_start(buf.a2)
     reduce_done(step)
     relay_near(wt.cq)
-    weight_outward(wt.co, wt.co.source)
     relay_far(wt.cq)
     weight_ready(wt.ckv)
     matmul(buf.m, wt.ckv.weight, buf.kv, buf.bias, 1, 1)
@@ -1115,51 +1191,46 @@
     step = reduce_start(set_b)
     relay_inward(wt.f2)
     gather_finish(e3)
-    reduce_relay(step)
-    reduce_ready(step)
+    reduce_relay_paced(step)
 
     def after_cross(i):
         place = part(i, TILE)
         buf.h2[place, :] = buf.h1[place, :] + (reduced(step, place) + buf.vec[7:8, :])
 
-    loop(L // TILE, after_cross)
-    norm(lambda place: buf.h2[place, :], 2, buf.a3)
-    send(rows(buf.a3, q), rows(buf.a3b, q), k_units + 1, dev_adj, end)
-    a3 = gather_start(buf.a3, mid)
+    a3 = gather_open(buf.a3, mid, 2)
+    for h in range(2):
+        reduce_ready_half(step, h)
+        loop(TILES, after_cross, first=h * TILES)
+        norm(lambda place: buf.h2[place, :], 2, buf.a3, (h,))
+        send(piece(buf.a3, q, h, 2), half_major(buf.a3b, q, h), k_units + 10 + h, dev_adj, end)
+        gather_part(a3, h)
     reduce_done(step)
 
-    def units(normed, activs, slopes):
+    def units(normed, activs, slopes, at=slice(0, T)):
         def one(j):
-            value = nn(normed[...], wt.f1.weight[:, lanes(j)]) + buf.bias[2:3, lanes(j)]
+            value = nn(normed[at, :], wt.f1.weight[:, lanes(j)]) + buf.bias[2:3, lanes(j)]
             activ, slope = gelu_pair(value)
-            activs[:, lanes(j)] = activ.astype(BF16)
-            slopes[:, lanes(j)] = slope.astype(BF16)
-
-        loop(FL // 256, one)
-
-    def units_back(grad, slopes):
+            activs[at, lanes(j)] = activ.astype(BF16)
+            slopes[at, lanes(j)] = slope.astype(BF16)
+
+        loop(FL // 256, one, 2)
+
+    def units_back(grad, slopes, at=slice(0, T)):
         def one(j):
-            value = nt(grad[...], wt.f2.weight[lanes(j), :])
-            low = (value * slopes[:, lanes(j)].astype(F32)).astype(BF16)
-            slopes[:, lanes(j)] = low
+            value = nt(grad[at, :], wt.f2.weight[lanes(j), :])
+            low = (value * slopes[at, lanes(j)].astype(F32)).astype(BF16)
+            slopes[at, lanes(j)] = low
             total = jnp.sum(low.astype(F32), 0, keepdims=True)
             buf.sg[10:11, lanes(j)] = buf.sg[10:11, lanes(j)] + total
 
         loop(FL // 256, one)
 
-    def weight_grads(left, right, left_b, right_b, name):
+    def weight_grads(left, right, left_b, right_b, name, first, count):
         def one(j):
             total = tn(left[:, lanes(j)], right[...]) + tn(left_b[:, lanes(j)], right_b[...])
             name.grad[lanes(j), :] = total.astype(BF16)
 
-        loop(left.shape[1] // 256, one)
-
-    def fold(ticket, dst):
-        def one(i):
-            place = part(i, TILE)
-            dst[place, :] = reduced(ticket, place).astype(BF16)
-
-        loop(L // TILE, one)
+        loop(count, one, first=first)
 
     def on_mid(fn, *args):
         run_if(mid, lambda: fn(*args))
@@ -1169,39 +1240,49 @@
 
     buf.sg[8:9, :] = lax.fori_loop(0, L // TILE, cot_sum, jnp.zeros((1, D), F32))
 
+    for index, k in ((q, k_units), (q_x, k_units + 2)):
+        for h in range(2):
+            landed = half_major(buf.e3b, index, h)
+            arrived(landed, k + h, mid)
+            send(landed, landed, k + 4 + h, dev_core, mid)
     gather_relay(a3)
-    arrived(rows(buf.e3b, q), k_units, mid)
-    e3b = gather_start(buf.e3b, mid)
+    a3b = gather_open(buf.a3b, mid, 2, half_major)
+    arrived(half_major(buf.a3b, q, 0), k_units + 10, mid)
+    gather_part(a3b, 0)
     gather_ready(a3)
     inner_ready(wt.f1)
     on_mid(units, buf.a3, buf.g, buf.gp)
+    arrived(half_major(buf.a3b, q, 1), k_units + 11, mid)
+    gather_part(a3b, 1)
+    on_mid(weight_grad, buf.g, buf.e3, wt.f2)
     wt.f2.own_copy[0].wait()
     inner_ready(wt.f2)
     on_mid(units_back, buf.e3, buf.gp)
-    arrived(rows(buf.a3b, q), k_units + 1, mid)
-    a3b = gather_start(buf.a3b, mid)
-    gather_relay(e3b)
     on_mid(matmul_back, buf.gp, wt.f1.weight, set_a.parts)
     step = reduce_start(set_a, mid)
-    gather_ready(e3b)
-    gather_finish(a3b)
-    reduce_relay(step)
-    on_mid(units, buf.a3b, buf.gb, buf.gpb)
-    on_mid(units_back, buf.e3b, buf.gpb)
-    on_mid(matmul_back, buf.gpb, wt.f1.weight, set_b.parts)
-    step_b = reduce_start(set_b, mid)
-    on_mid(matmul, buf.gb, wt.f2.weight, set_c.parts)
-    reduce_relay(step_b)
-    final = reduce_start(set_c, mid)
-    on_mid(weight_grads, buf.g, buf.e3, buf.gb, buf.e3b, wt.f2)
-    inner_grad_far(wt.f2)
-    on_mid(weight_grads, buf.a3, buf.gp, buf.a3b, buf.gpb, wt.f1)
-    inner_grad_far(wt.f1)
-    inner_grad_near(wt.f2)
-    inner_grad_near(wt.f1)
-    reduce_ready(step_b)
-    on_mid(fold, step_b, buf.back)
-    send(buf.back, buf.back, k_units + 2, dev_adj, mid)
+    for index, k in ((q_core, k_units + 4), (q_xc, k_units + 6)):
+        for h in range(2):
+            arrived(half_major(buf.e3b, index, h), k + h, mid)
+    step_b = reduce_open(set_b, mid)
+    for h in range(2):
+        at = slice(h * T // 2, (h + 1) * T // 2)
+        if h == 0:
+            gather_relay(a3b)
+            gather_ready_part(a3b, 0)
+            reduce_relay(step)
+        else:
+            gather_ready_part(a3b, 1)
+            reduce_relay_half(step_b, 0)
+        on_mid(units, buf.a3b, buf.gb, buf.gpb, at)
+        on_mid(units_back, buf.e3b, buf.gpb, at)
+        on_mid(matmul_back, buf.gpb, wt.f1.weight, set_b.parts, at)
+        reduce_start_half(step_b, h)
+
+    def back_outward(h):
+        reduce_ready_half(step_b, h)
+        on_mid(fold, step_b, buf.back, (h,))
+        ready = buf.back.at[part(h, HALF)]
+        send(ready, ready, k_units + 12 + h, dev_adj, mid)
 
     def store(name):
         def low(place, value):
@@ -1209,19 +1290,40 @@
 
         return low
 
-    def units_norm_back(incoming):
+    def units_norm_back(incoming, halves):
         norm_back(
             lambda place: buf.h2[place, :], incoming, 2,
-            lambda place: rows(buf.e3, q)[place, :].astype(F32), buf.dh, store(buf.e2), 7,
+            lambda place: rows(buf.e3, q)[place, :].astype(F32), buf.dh, store(buf.e2), 7, halves,
         )
 
     reduce_done(e3)
-    sent(to_middle)
+    for record in to_middle:
+        sent(record)
+    back_outward(0)
+    reduce_relay_half(step_b, 1)
+    on_mid(weight_grad, buf.gb, buf.e3b, wt.f2, True)
+    inner_grad_far(wt.f2)
+    inner_grad_near(wt.f2)
     reduce_ready(step)
-    on_mid(units_norm_back, lambda place: reduced(step, place))
-    arrived(buf.back, k_units + 2, end)
-    run_if(end, lambda: units_norm_back(lambda place: buf.back[place, :].astype(F32)))
-    e2 = gather_start(buf.e2)
+    on_mid(units_norm_back, lambda place: reduced(step, place), (0, 1))
+    e2 = gather_open(buf.e2, None, 2)
+    gather_part(e2, 0, mid)
+    back_outward(1)
+    gather_part(e2, 1, mid)
+    on_mid(weight_grads, buf.a3, buf.gp, buf.a3b, buf.gpb, wt.f1, 0, Z)
+    inner_grad_far(wt.f1)
+    inner_grad_near(wt.f1)
+    on_mid(matmul, buf.gb, wt.f2.weight, set_c.parts)
+    final = reduce_open(set_c, mid)
+    reduce_start_half(final, 0)
+    reduce_start_half(final, 1)
+    for h in range(2):
+        arrived(buf.back.at[part(h, HALF)], k_units + 12 + h, end)
+        run_if(
+            end,
+            lambda h=h: units_norm_back(lambda place: buf.back[place, :].astype(F32), (h,)),
+        )
+        gather_part(e2, h, end)
     reduce_done(step)
     reduce_done(step_b)
     gather_finish(e2)
@@ -1244,9 +1346,10 @@
     column_sums(buf.kv, 1, 1, 9, 3)
     reduce_ready(final)
     on_mid(fold, final, buf.tail)
-    send(buf.tail, buf.tail, k_units + 3, dev_adj, mid)
+    send(buf.tail, buf.tail, k_units + 14, dev_adj, mid)
     reduce_done(final)
     grad_combine(wt.co)
+    inner_grad_combine(wt.f2)
     reduce_ready(step)
     norm_back(
         lambda place: buf.h1[place, :], lambda place: reduced(step, place), 1,
@@ -1255,25 +1358,26 @@
     e1 = gather_start(buf.e3)
     reduce_done(step)
     grad_combine(wt.cq)
-    grad_outward(wt.co)
     gather_finish(e1)
     reduce_relay(mem_step)
+    grad_combine(wt.ckv)
 
     weight_grad(buf.o1, buf.e3, wt.so)
     grad_send(wt.so)
     matmul_back(buf.e3, wt.so.weight, buf.do)
     attention_back(buf.qkv, 0, buf.qkv, 2, 4, buf.p1, buf.do)
+    inner_grad_combine(wt.f1)
+    grad_outward(wt.co)
+    inner_final(mid)
     weight_grad(buf.a1, buf.qkv, wt.qkv)
     far_part = grad_send_far(wt.qkv)
     matmul_back(buf.qkv, wt.qkv.weight, set_b.parts)
     step = reduce_start(set_b)
     column_sums(buf.qkv, 0, 1, 9, 0)
     column_sums(buf.qkv, 2, 1, 9, 1)
-    inner_grad_combine(wt.f2)
-    inner_grad_combine(wt.f1)
+    grad_outward(wt.cq)
     reduce_relay(step)
-    grad_combine(wt.ckv)
-    grad_outward(wt.cq)
+    grad_combine(wt.so)
     on_mid(matmul, buf.g, wt.f2.weight, set_c.parts)
     final = reduce_start(set_c, mid)
 
@@ -1285,6 +1389,7 @@
         send(buf.mb.at[:, part(to, mem_cols)], buf.ml.at[j], k_back + j, (to, d))
     sent(far_part)
     middle_part = grad_send_middle(wt.qkv)
+    grad_combine_far(wt.qkv)
     grad_outward(wt.ckv)
     reduce_ready(step)
 
@@ -1297,12 +1402,23 @@
     )
     k_in = slot()
     send(buf.ig, io.input_grad, k_in, ((s + n_sec - 1) % n_sec, d))
-    buf.sga[q, z] = buf.sg[...].astype(BF16)
-    sums = spread_start(buf.sga, None)
+    buf.sga[z] = buf.sg[...].astype(BF16)
+    sums = spread_start(lambda plane: buf.sga.at[plane])
+    inner_final(end)
+    for weight in (wt.co, wt.cq):
+        grad_final(weight)
     reduce_relay(final)
-    grad_combine(wt.so)
     sent(middle_part)
     grad_send_near(wt.qkv)
+    grad_combine_middle(wt.qkv)
+    grad_outward(wt.so)
+    grad_final(wt.ckv)
+    spread_relay(sums)
+    planes = buf.sga[0].astype(F32)
+    for plane in range(1, Z):
+        planes = planes + buf.sga[plane].astype(F32)
+    buf.sgp[q] = planes.astype(BF16)
+    spread_plane(sums, buf.sgp)
 
     def finish(incoming):
         def one(i):
@@ -1312,7 +1428,7 @@
 
         loop(L // TILE, one)
 
-    arrived(buf.tail, k_units + 3, end)
+    arrived(buf.tail, k_units + 14, end)
     run_if(end, lambda: finish(lambda place: buf.tail[place, :].astype(F32)))
     for j in range(1, n_sec):
         arrived(buf.ml.at[j], k_back + j)
@@ -1325,29 +1441,20 @@
         buf.mo[place, :] = total.astype(BF16)
 
     loop(L // TILE, memory_total)
-    result_copies.append(local(buf.mo, io.memory_grad))
-    grad_outward(wt.so)
-    grad_combine_far(wt.qkv)
-    for weight in (wt.co, wt.cq, wt.ckv, wt.f2, wt.f1):
-        grad_final(weight)
-    spread_relay(sums)
-    grad_combine_middle(wt.qkv)
+    keep(buf.mo, io.memory_grad)
+    grad_outward(wt.qkv)
+    grad_final(wt.so)
+    grad_final(wt.qkv)
+    unit_last_wait()
+    last_wait(wt.cq)
+    last_wait(wt.ckv)
     reduce_ready(final)
     on_mid(finish, lambda place: reduced(final, place))
-    result_copies.append(local(buf.stage, io.output))
-    grad_outward(wt.qkv)
-    grad_final(wt.so)
-    last_wait(wt.ckv)
-    last_wait(wt.cq)
-    unit_last_wait()
-    grad_final(wt.qkv)
-    spread_ready(sums)
+    keep(buf.stage, io.output)
+    spread_ready(sums, buf.sgp)
 
     def per_unit(q_at, at):
-        total = buf.sga[q_at, 0, :, at].astype(F32)
-        for plane in range(1, Z):
-            total = total + buf.sga[q_at, plane, :, at].astype(F32)
-        return total
+        return buf.sgp[q_at, :, at].astype(F32)
 
     at = part(d // 2, 128)
     feature = per_unit(0, at)
@@ -1369,11 +1476,11 @@
     buf.sums[10:11, :] = jnp.where(half, low_head, high_head)[9:10]
     buf.sums[11:12, :] = per_unit(q, part(2 * z, 128))[10:11]
     buf.sums[12:13, :] = per_unit(q, part(2 * z + 1, 128))[10:11]
-    result_copies.append(local(buf.sums, io.sums_out))
+    keep(buf.sums, io.sums_out)
     last_wait(wt.qkv)
     arrived(io.input_grad, k_in)
-    for copy in result_copies:
-        copy.wait()
+    for copy, cond in result_copies:
+        run_if(cond, copy.wait)
     for record in list(started):
         sent(record)
     assert counter[0] <= SEMS
@@ -1383,7 +1490,8 @@
     tokens, row = (T, D), (L, D)
     shapes = dict(
         sva=(P_IN, Z, 16, 128),
-        sga=(P_IN, Z, 16, D),
+        sga=(Z, 16, D),
+        sgp=(P_IN, 16, D),
         hb=row, ig=row, stage=row, mb=row,
         ml=(n_sec, L, mem_cols),
         mo=(L, mem_cols),

time: 268 us -> 245 us (0.914)
  Pallas kernels: 262 us -> 240 us
    pallas_call x1, Pallas kernels: 258 us -> 235 us  [on_device_planes(): pl.pallas_call(functools.partial(whole_kernel, n_sec, mem_cols), out_shap...]
where the time goes in v4:
time: 245 us
  Pallas kernels  240 us (98%)
  local copies, waits for them, and re-layouts  2.6 us (1%)
    pallas_call x1, Pallas kernels, on_device_planes(): pl.pallas_call(functools.partial(whole_kernel, n_sec, mem_cols), out_shap...  235 us

profile of v4, /device:TPU:1, one launch (start us, length us, event | category | flops | bytes accessed | tf_op | source)
XLA Modules:
  0.0 244.5 jit_solution(16581524863300873641)
XLA Ops:
  1.9 235.1 %shard_map.297 = (bf16[192,1024]{1,0:T(8,128)(2,1)}, bf16[192,1024]{1,0:T(8,128)(2,1)}, bf16[192,512]{1,0:T(8,128)(2,1)}, bf16[64,3072]{1,0:T(8,128)(2,1)}, bf16...) custom-call(bf16[192,1024]{1,0:T(8,128)(2,1)} %bitcast.29, ...), custom_call_target="tpu_custom_call" | custom-call | flops 20999999488 | bytes 20971520 | tf_op jit(solution)/shard_map/pallas_call | solution.py:1593
  237.0 4.9 %shard_map.298 = (bf16[192,1024]{1,0:T(8,128)(2,1)}, bf16[192,1024]{1,0:T(8,128)(2,1)}, bf16[192,512]{1,0:T(8,128)(2,1)}, f32[64,3072]{1,0:T(8,128)}, f32[64,102...) custom-call(bf16[192,1024]{1,0:T(8,128)(2,1)} %get-tuple-element.43., ...), custom_call_target="tpu_custom_call" | custom-call | bytes 9437184 | tf_op jit(solution)/shard_map/pallas_call | solution.py:1608
  241.9 0.0 copy-start.2
  241.9 0.7 copy-done.2
  242.6 0.0 copy-start.1
  242.6 0.6 copy.34
  243.1 0.1 copy-done.1
  243.3 0.0 copy-start
  243.3 0.6 copy.35
  243.8 0.1 copy-done
  243.9 0.6 copy.36
Async XLA Ops:
  241.9 0.7 copy-start.2
  242.6 0.7 copy-start.1
  243.3 0.7 copy-start

commit v5 on v4

--- a/solution.py
+++ b/solution.py
@@ -496,10 +496,18 @@
     for name, (count, _, by_column) in WEIGHTS.items():
         weight = getattr(wt, name)
         weight.count, weight.by_column = count, by_column
+        weight.pieces, weight.piece = 1, 0
         weight.to_use, weight.swap, weight.to_sum, weight.last = slot(5), slot(3), slot(6), slot(3)
 
     def block(name, index):
-        return name.weight.at[part(index, name.count)]
+        return name.weight.at[part(index * name.pieces + name.piece, name.count)]
+
+    first_weights = [
+        SimpleNamespace(
+            weight=wt.qkv.weight, count=wt.qkv.count // 2, pieces=2, piece=h, to_use=slot(5)
+        )
+        for h in range(2)
+    ]
 
     def send_inward(name, src):
         send(src, block(name, z), name.to_use, dev_adj, end)
@@ -828,12 +836,6 @@
         reduce_relay_half(ticket, 0)
         reduce_relay_half(ticket, 1)
 
-    def reduce_relay_paced(ticket):
-        record = reduce_relay_half(ticket, 0)
-        ticket[2][:] = [other for other in ticket[2] if other is not record]
-        sent(record)
-        reduce_relay_half(ticket, 1)
-
     def reduce_ready_half(ticket, h):
         which, k, _, cond, lay = ticket
         if lay is half_major:
@@ -870,20 +872,14 @@
 
     def spread_start(place):
         k = slot(8)
-        send(place(z), place(z), k, dev_adj)
-        send(place(z), place(z), k + 1, dev_opp, mid)
-        send(place(z), place(z), k + 2, dev_diag, end)
+        for j, device in enumerate((dev_diag, dev_opp, dev_adj)):
+            send(place(z), place(z), k + j, device)
         return place, k
 
-    def spread_relay(ticket):
+    def spread_wait(ticket):
         place, k = ticket
-        arrived(place(z_opp), k + 1, mid)
-        send(place(z_opp), place(z_opp), k + 3, dev_adj, mid)
-        arrived(place(z_diag), k + 2, mid)
-        send(place(z_diag), place(z_diag), k + 4, dev_adj, mid)
-        arrived(place(z_adj), k)
-        arrived(place(z_diag), k + 3, end)
-        arrived(place(z_opp), k + 4, end)
+        for j, plane in enumerate((z_diag, z_opp, z_adj)):
+            arrived(place(plane), k + j)
 
     def spread_plane(ticket, name):
         k = ticket[1]
@@ -1054,10 +1050,6 @@
     swap_start(wt.qkv)
     k_prev, k_cot, k_mem = slot(), slot(), slot(n_sec)
     send(io.prev, buf.hb, k_prev, ((s + 1) % n_sec, d))
-    for weight in (wt.so, wt.co):
-        send_inward(weight, weight.source)
-        send_across(weight, weight.source)
-        weight_outward(weight, weight.source)
     mem_slot = rows(buf.m, q)
     for j in range(1, n_sec):
         send(io.mem, mem_slot.at[:, part(s, mem_cols)], k_mem + j, ((s + j) % n_sec, d))
@@ -1065,18 +1057,20 @@
     send(io.cot, rows(buf.e3, q), k_cot, ((s + n_sec - 1) % n_sec, d))
     for weight in (wt.so, wt.co, wt.f2):
         weight.own_copy = [local(weight.source, block(weight, z))]
+    send_inward(wt.so, wt.so.source)
+    send_across(wt.so, wt.so.source)
+    weight_outward(wt.so, wt.so.source)
+    swap_wait(wt.qkv)
+    for weight in first_weights:
+        send_inward(weight, block(weight, z))
+        send_across(weight, block(weight, z))
+        weight_outward(weight, block(weight, z))
+    spread_wait(sv)
+    spread_plane(sv, buf.sva)
     for weight, copy in ((wt.ckv, raw_copies[1]), (wt.cq, raw_copies[2])):
         copy.wait()
         sort_columns(weight)
         swap_start(weight)
-
-    swap_wait(wt.qkv)
-    send_inward(wt.qkv, block(wt.qkv, z))
-    send_across(wt.qkv, block(wt.qkv, z))
-    weight_outward(wt.qkv, block(wt.qkv, z))
-    unit_swap_start()
-    spread_relay(sv)
-    spread_plane(sv, buf.sva)
     spread_ready(sv, buf.sva)
 
     for tile in range(D // 128):
@@ -1102,6 +1096,8 @@
         buf.bias[2:3, 256 * tile + 128:256 * tile + 256] = unit[12:13]
     buf.sg[...] = jnp.zeros((16, D), F32)
 
+    relay_inward(first_weights[0])
+    relay_near(first_weights[0])
     arrived(buf.hb, k_prev)
 
     def hidden(place):
@@ -1109,20 +1105,21 @@
 
     norm(hidden, 0, buf.a1)
     a1 = gather_start(buf.a1)
-    relay_inward(wt.qkv)
-    relay_near(wt.qkv)
+    unit_swap_start()
+    relay_inward(first_weights[1])
+    relay_near(first_weights[1])
+    relay_inward(wt.so)
     swap_wait(wt.ckv)
     send_inward(wt.ckv, block(wt.ckv, z))
+    swap_wait(wt.cq)
+    send_inward(wt.cq, block(wt.cq, z))
+    send_inward(wt.co, wt.co.source)
+    send_across(wt.ckv, block(wt.ckv, z))
     for j in range(1, n_sec):
         origin = (s + n_sec - j) % n_sec
         arrived(mem_slot.at[:, part(origin, mem_cols)], k_mem + j)
     mem_copy.wait()
-    gather_relay(a1)
     memory = gather_start(buf.m)
-    relay_inward(wt.so)
-    swap_wait(wt.cq)
-    send_inward(wt.cq, block(wt.cq, z))
-    relay_far(wt.qkv)
     arrived(rows(buf.e3, q), k_cot)
     k_units = slot(16)
     to_middle = [send(rows(buf.e3, q), rows(buf.e3, q), k_units + 9, dev_x, end)]
@@ -1133,45 +1130,52 @@
             to_middle.append(send(src, dst, k + h, dev_adj, end))
 
     cot_inward(q, k_units)
+    relay_far(first_weights[0])
+    gather_relay(a1)
+    relay_far(first_weights[1])
+    relay_near(wt.so)
+    relay_inward(wt.ckv)
     gather_ready(a1)
     unit_swap_wait(end)
     send_inward(wt.f1, block(wt.f1, z))
-    weight_ready(wt.qkv)
+    for weight in first_weights:
+        weight_ready(weight)
     matmul(buf.a1, wt.qkv.weight, buf.qkv, buf.bias, 0)
-    send_across(wt.ckv, block(wt.ckv, z))
-    attention(buf.qkv, 0, buf.qkv, 2, 4, True, 13, buf.p1, buf.o1)
-    relay_inward(wt.ckv)
-    relay_near(wt.so)
     relay_far(wt.so)
     weight_outward(wt.ckv, block(wt.ckv, z))
     send_across(wt.cq, block(wt.cq, z))
+    attention(buf.qkv, 0, buf.qkv, 2, 4, True, 13, buf.p1, buf.o1)
+    relay_inward(wt.cq)
+    send_across(wt.co, wt.co.source)
     wt.so.own_copy[0].wait()
     weight_ready(wt.so)
     matmul(buf.o1, wt.so.weight, set_a.parts)
     step = reduce_start(set_a)
     send_inward(wt.f2, wt.f2.source)
-    relay_inward(wt.cq)
+    relay_inward(wt.co)
+    relay_near(wt.ckv)
     weight_outward(wt.cq, block(wt.cq, z))
     reduce_relay(step)
     arrived(rows(buf.e3, q_x), k_units + 9, end)
     cot_inward(q_x, k_units + 2)
-    relay_near(wt.ckv)
     gather_finish(memory)
     relay_far(wt.ckv)
-    relay_inward(wt.co)
     unit_swap_wait(mid)
     send_across(wt.f1, block(wt.f1, z))
-    reduce_ready(step)
 
     def after_self(i):
         place = part(i, TILE)
         buf.h1[place, :] = hidden(place) + (reduced(step, place) + buf.vec[6:7, :])
 
-    loop(L // TILE, after_self)
-    norm(lambda place: buf.h1[place, :], 1, buf.a2)
-    a2 = gather_start(buf.a2)
+    a2 = gather_open(buf.a2, None, 2)
+    for h in range(2):
+        reduce_ready_half(step, h)
+        loop(TILES, after_self, first=h * TILES)
+        norm(lambda place: buf.h1[place, :], 1, buf.a2, (h,))
+        gather_part(a2, h)
     reduce_done(step)
     relay_near(wt.cq)
+    weight_outward(wt.co, wt.co.source)
     relay_far(wt.cq)
     weight_ready(wt.ckv)
     matmul(buf.m, wt.ckv.weight, buf.kv, buf.bias, 1, 1)
@@ -1191,7 +1195,7 @@
     step = reduce_start(set_b)
     relay_inward(wt.f2)
     gather_finish(e3)
-    reduce_relay_paced(step)
+    reduce_relay(step)
 
     def after_cross(i):
         place = part(i, TILE)
@@ -1231,6 +1235,14 @@
             name.grad[lanes(j), :] = total.astype(BF16)
 
         loop(count, one, first=first)
+
+    def finish(incoming):
+        def one(i):
+            place = part(i, TILE)
+            total = buf.h2[place, :] + (incoming(place) + buf.vec[8:9, :])
+            buf.stage[place, :] = total.astype(BF16)
+
+        loop(L // TILE, one)
 
     def on_mid(fn, *args):
         run_if(mid, lambda: fn(*args))
@@ -1255,26 +1267,31 @@
     arrived(half_major(buf.a3b, q, 1), k_units + 11, mid)
     gather_part(a3b, 1)
     on_mid(weight_grad, buf.g, buf.e3, wt.f2)
-    wt.f2.own_copy[0].wait()
-    inner_ready(wt.f2)
-    on_mid(units_back, buf.e3, buf.gp)
-    on_mid(matmul_back, buf.gp, wt.f1.weight, set_a.parts)
-    step = reduce_start(set_a, mid)
     for index, k in ((q_core, k_units + 4), (q_xc, k_units + 6)):
         for h in range(2):
             arrived(half_major(buf.e3b, index, h), k + h, mid)
+    gather_relay_part(a3b, 0)
+    wt.f2.own_copy[0].wait()
+    inner_ready(wt.f2)
+    on_mid(matmul, buf.g, wt.f2.weight, set_c.parts)
+    final = reduce_start(set_c, mid)
+    gather_ready_part(a3b, 0)
     step_b = reduce_open(set_b, mid)
     for h in range(2):
         at = slice(h * T // 2, (h + 1) * T // 2)
+        if h == 1:
+            gather_ready_part(a3b, 1)
+        on_mid(units, buf.a3b, buf.gb, buf.gpb, at)
         if h == 0:
-            gather_relay(a3b)
-            gather_ready_part(a3b, 0)
-            reduce_relay(step)
+            reduce_relay(final)
         else:
-            gather_ready_part(a3b, 1)
             reduce_relay_half(step_b, 0)
-        on_mid(units, buf.a3b, buf.gb, buf.gpb, at)
+            on_mid(weight_grad, buf.gb, buf.e3b, wt.f2, True)
+            inner_grad_far(wt.f2)
+            inner_grad_near(wt.f2)
         on_mid(units_back, buf.e3b, buf.gpb, at)
+        if h == 0:
+            gather_relay_part(a3b, 1)
         on_mid(matmul_back, buf.gpb, wt.f1.weight, set_b.parts, at)
         reduce_start_half(step_b, h)
 
@@ -1284,6 +1301,21 @@
         ready = buf.back.at[part(h, HALF)]
         send(ready, ready, k_units + 12 + h, dev_adj, mid)
 
+    reduce_relay_half(step_b, 1)
+    on_mid(units_back, buf.e3, buf.gp)
+    back_outward(0)
+    on_mid(matmul_back, buf.gp, wt.f1.weight, set_a.parts)
+    reduce_ready(final)
+    on_mid(finish, lambda place: reduced(final, place))
+    reduce_done(final)
+    step = reduce_start(set_a, mid)
+    back_outward(1)
+    reduce_relay(step)
+    on_mid(weight_grads, buf.a3, buf.gp, buf.a3b, buf.gpb, wt.f1, 0, Z)
+    inner_grad_far(wt.f1)
+    inner_grad_near(wt.f1)
+    on_mid(matmul, buf.gb, wt.f2.weight, set_c.parts)
+
     def store(name):
         def low(place, value):
             rows(name, q)[place, :] = value
@@ -1299,24 +1331,15 @@
     reduce_done(e3)
     for record in to_middle:
         sent(record)
-    back_outward(0)
-    reduce_relay_half(step_b, 1)
-    on_mid(weight_grad, buf.gb, buf.e3b, wt.f2, True)
-    inner_grad_far(wt.f2)
-    inner_grad_near(wt.f2)
     reduce_ready(step)
+    final_b = reduce_open(set_c, mid)
+    reduce_start_half(final_b, 0)
+    reduce_start_half(final_b, 1)
     on_mid(units_norm_back, lambda place: reduced(step, place), (0, 1))
     e2 = gather_open(buf.e2, None, 2)
     gather_part(e2, 0, mid)
-    back_outward(1)
     gather_part(e2, 1, mid)
-    on_mid(weight_grads, buf.a3, buf.gp, buf.a3b, buf.gpb, wt.f1, 0, Z)
-    inner_grad_far(wt.f1)
-    inner_grad_near(wt.f1)
-    on_mid(matmul, buf.gb, wt.f2.weight, set_c.parts)
-    final = reduce_open(set_c, mid)
-    reduce_start_half(final, 0)
-    reduce_start_half(final, 1)
+    inner_grad_combine(wt.f2)
     for h in range(2):
         arrived(buf.back.at[part(h, HALF)], k_units + 12 + h, end)
         run_if(
@@ -1327,7 +1350,7 @@
     reduce_done(step)
     reduce_done(step_b)
     gather_finish(e2)
-    reduce_relay(final)
+    reduce_relay(final_b)
 
     weight_grad(buf.o2, buf.e2, wt.co)
     grad_send(wt.co)
@@ -1344,42 +1367,44 @@
     mem_step = reduce_start(set_a)
     column_sums(buf.q2, 0, 1, 9, 2)
     column_sums(buf.kv, 1, 1, 9, 3)
-    reduce_ready(final)
-    on_mid(fold, final, buf.tail)
+    reduce_ready(final_b)
+    on_mid(fold, final_b, buf.tail)
     send(buf.tail, buf.tail, k_units + 14, dev_adj, mid)
-    reduce_done(final)
+    reduce_done(final_b)
     grad_combine(wt.co)
-    inner_grad_combine(wt.f2)
-    reduce_ready(step)
-    norm_back(
-        lambda place: buf.h1[place, :], lambda place: reduced(step, place), 1,
-        lambda place: buf.dh[place, :], buf.dh, store(buf.e3), 6,
-    )
-    e1 = gather_start(buf.e3)
+    inner_grad_combine(wt.f1)
+    grad_combine(wt.cq)
+    e1 = gather_open(buf.e3, None, 2)
+    for h in range(2):
+        reduce_ready_half(step, h)
+        norm_back(
+            lambda place: buf.h1[place, :], lambda place: reduced(step, place), 1,
+            lambda place: buf.dh[place, :], buf.dh, store(buf.e3), 6, (h,),
+        )
+        gather_part(e1, h)
     reduce_done(step)
-    grad_combine(wt.cq)
+    grad_combine(wt.ckv)
     gather_finish(e1)
     reduce_relay(mem_step)
-    grad_combine(wt.ckv)
 
     weight_grad(buf.o1, buf.e3, wt.so)
     grad_send(wt.so)
     matmul_back(buf.e3, wt.so.weight, buf.do)
     attention_back(buf.qkv, 0, buf.qkv, 2, 4, buf.p1, buf.do)
-    inner_grad_combine(wt.f1)
     grad_outward(wt.co)
-    inner_final(mid)
-    weight_grad(buf.a1, buf.qkv, wt.qkv)
-    far_part = grad_send_far(wt.qkv)
+    grad_combine(wt.so)
+    run_if(end, lambda: weight_grad(buf.a1, buf.qkv, wt.qkv))
+    grad_send_far(wt.qkv)
+    grad_send_middle(wt.qkv)
     matmul_back(buf.qkv, wt.qkv.weight, set_b.parts)
     step = reduce_start(set_b)
+    on_mid(weight_grad, buf.a1, buf.qkv, wt.qkv)
     column_sums(buf.qkv, 0, 1, 9, 0)
     column_sums(buf.qkv, 2, 1, 9, 1)
     grad_outward(wt.cq)
     reduce_relay(step)
-    grad_combine(wt.so)
-    on_mid(matmul, buf.g, wt.f2.weight, set_c.parts)
-    final = reduce_start(set_c, mid)
+    inner_final(mid)
+    grad_combine_far(wt.qkv)
 
     reduce_ready(mem_step)
     fold(mem_step, buf.mb)
@@ -1387,9 +1412,6 @@
     for j in range(1, n_sec):
         to = (s + j) % n_sec
         send(buf.mb.at[:, part(to, mem_cols)], buf.ml.at[j], k_back + j, (to, d))
-    sent(far_part)
-    middle_part = grad_send_middle(wt.qkv)
-    grad_combine_far(wt.qkv)
     grad_outward(wt.ckv)
     reduce_ready(step)
 
@@ -1404,29 +1426,22 @@
     send(buf.ig, io.input_grad, k_in, ((s + n_sec - 1) % n_sec, d))
     buf.sga[z] = buf.sg[...].astype(BF16)
     sums = spread_start(lambda plane: buf.sga.at[plane])
+    grad_combine_middle(wt.qkv)
+    grad_outward(wt.so)
     inner_final(end)
     for weight in (wt.co, wt.cq):
         grad_final(weight)
-    reduce_relay(final)
-    sent(middle_part)
     grad_send_near(wt.qkv)
-    grad_combine_middle(wt.qkv)
-    grad_outward(wt.so)
+    grad_outward(wt.qkv)
     grad_final(wt.ckv)
-    spread_relay(sums)
+    spread_wait(sums)
     planes = buf.sga[0].astype(F32)
     for plane in range(1, Z):
         planes = planes + buf.sga[plane].astype(F32)
     buf.sgp[q] = planes.astype(BF16)
     spread_plane(sums, buf.sgp)
-
-    def finish(incoming):
-        def one(i):
-            place = part(i, TILE)
-            total = buf.h2[place, :] + (incoming(place) + buf.vec[8:9, :])
-            buf.stage[place, :] = total.astype(BF16)
-
-        loop(L // TILE, one)
+    grad_final(wt.so)
+    grad_final(wt.qkv)
 
     arrived(buf.tail, k_units + 14, end)
     run_if(end, lambda: finish(lambda place: buf.tail[place, :].astype(F32)))
@@ -1442,14 +1457,9 @@
 
     loop(L // TILE, memory_total)
     keep(buf.mo, io.memory_grad)
-    grad_outward(wt.qkv)
-    grad_final(wt.so)
-    grad_final(wt.qkv)
     unit_last_wait()
     last_wait(wt.cq)
     last_wait(wt.ckv)
-    reduce_ready(final)
-    on_mid(finish, lambda place: reduced(final, place))
     keep(buf.stage, io.output)
     spread_ready(sums, buf.sgp)
 
@@ -1535,7 +1545,8 @@
 def finish_kernel(*refs):
     moved, low, sums = refs[:3], refs[3:10], refs[10]
     moved_out, high, small = refs[11:14], refs[14:21], refs[21:27]
-    low_buf, high_buf, moved_buf, sems = refs[27:34], refs[34:41], refs[41:44], refs[44]
+    low_buf, high_buf, moved_buf = refs[27:34], refs[34:41], refs[41:44]
+    small_buf, sems = refs[44:50], refs[50]
     inward = [
         pltpu.make_async_copy(src, dst, sems.at[i])
         for i, (src, dst) in enumerate(zip(low + moved, low_buf + moved_buf))
@@ -1543,7 +1554,7 @@
     for copy in inward:
         copy.start()
     outward = []
-    gain, shift, out_bias, self_bias, cross_bias, unit_bias = small
+    gain, shift, out_bias, self_bias, cross_bias, unit_bias = small_buf
     gain[0] = sums[0:3, 0:64]
     shift[0] = sums[3:6, 0:64]
     out_bias[0] = sums[6:9, 0:64]
@@ -1551,6 +1562,10 @@
     cross_bias[...] = sums[10:11, :]
     unit_bias[:, 0:128] = sums[11:12, :]
     unit_bias[:, 128:256] = sums[12:13, :]
+    for i, (src, dst) in enumerate(zip(small_buf, small)):
+        back = pltpu.make_async_copy(src, dst, sems.at[20 + i])
+        back.start()
+        outward.append(back)
     for i, copy in enumerate(inward[:7]):
         copy.wait()
         rows_in = low_buf[i].shape[0]
@@ -1604,18 +1619,20 @@
         ),
     )(*operands)
     shapes = [result.shape for result in results]
+    small_shapes = [(1, 3, 64)] * 3 + [(1, 128), (1, 128), (1, 256)]
     vmem = pl.BlockSpec(memory_space=pltpu.VMEM)
     finished = pl.pallas_call(
         finish_kernel,
         out_shape=[jax.ShapeDtypeStruct(shape, BF16) for shape in shapes[:3]]
         + [jax.ShapeDtypeStruct(shape, F32) for shape in shapes[3:10]]
-        + [jax.ShapeDtypeStruct(shape, F32) for shape in [(1, 3, 64)] * 3 + [(1, 128), (1, 128), (1, 256)]],
+        + [jax.ShapeDtypeStruct(shape, F32) for shape in small_shapes],
         in_specs=10 * [anywhere] + [vmem],
-        out_specs=10 * [anywhere] + 6 * [vmem],
+        out_specs=16 * [anywhere],
         scratch_shapes=[pltpu.VMEM(shape, BF16) for shape in shapes[3:10]]
         + [pltpu.VMEM(shape, F32) for shape in shapes[3:10]]
         + [pltpu.VMEM(shape, BF16) for shape in shapes[:3]]
-        + [pltpu.SemaphoreType.DMA((20,))],
+        + [pltpu.VMEM(shape, F32) for shape in small_shapes]
+        + [pltpu.SemaphoreType.DMA((26,))],
         compiler_params=pltpu.CompilerParams(vmem_limit_bytes=63 * 2**20),
         cost_estimate=pl.CostEstimate(flops=0, bytes_accessed=9 * 2**20, transcendentals=0),
     )(*results)

time: 245 us -> 238 us (0.971)
  Pallas kernels: 240 us -> 233 us
    pallas_call x1, Pallas kernels: 235 us -> 229 us  [on_device_planes(): pl.pallas_call(functools.partial(whole_kernel, n_sec, mem_cols), out_shap...]
where the time goes in v5:
time: 238 us; the launch traced here: 237 us
  Pallas kernels  233 us (98%)
  local copies, waits for them, and re-layouts  2.6 us (1%)
    pallas_call x1, Pallas kernels, on_device_planes(): pl.pallas_call(functools.partial(whole_kernel, n_sec, mem_cols), out_shap...  229 us

profile of v5, /device:TPU:1, one launch (start us, length us, event | category | flops | bytes accessed | tf_op | source)
XLA Modules:
  0.0 237.4 jit_solution(13064417190494872174)
XLA Ops:
  1.9 228.6 %shard_map.297 = (bf16[192,1024]{1,0:T(8,128)(2,1)}, bf16[192,1024]{1,0:T(8,128)(2,1)}, bf16[192,512]{1,0:T(8,128)(2,1)}, bf16[64,3072]{1,0:T(8,128)(2,1)}, bf16...) custom-call(bf16[192,1024]{1,0:T(8,128)(2,1)} %bitcast.29, ...), custom_call_target="tpu_custom_call" | custom-call | flops 20999999488 | bytes 20971520 | tf_op jit(solution)/shard_map/pallas_call | solution.py:1608
  230.5 4.3 %shard_map.298 = (bf16[192,1024]{1,0:T(8,128)(2,1)}, bf16[192,1024]{1,0:T(8,128)(2,1)}, bf16[192,512]{1,0:T(8,128)(2,1)}, f32[64,3072]{1,0:T(8,128)}, f32[64,102...) custom-call(bf16[192,1024]{1,0:T(8,128)(2,1)} %get-tuple-element.43., ...), custom_call_target="tpu_custom_call" | custom-call | bytes 9437184 | tf_op jit(solution)/shard_map/pallas_call | solution.py:1624
  234.8 0.0 copy-start.2
  234.8 0.7 copy-done.2
  235.5 0.0 copy-start.1
  235.5 0.6 copy.34
  236.1 0.1 copy-done.1
  236.2 0.0 copy-start
  236.2 0.6 copy.35
  236.7 0.1 copy-done
  236.9 0.6 copy.36
Async XLA Ops:
  234.8 0.7 copy-start.2
  235.5 0.7 copy-start.1
  236.2 0.7 copy-start

commit v6 on v5

--- a/solution.py
+++ b/solution.py
@@ -629,7 +629,6 @@
     def grad_send(name):
         grad_send_far(name)
         grad_send_middle(name)
-        grad_send_near(name)
 
     def add_rows(count, body):
         size = min(count, 64)
@@ -1361,8 +1360,12 @@
     weight_grad(buf.a2, buf.q2, wt.cq)
     grad_send(wt.cq)
     reduce_relay(step)
+    grad_combine(wt.co)
+    grad_combine(wt.cq)
     weight_grad(buf.m, buf.kv, wt.ckv)
     grad_send(wt.ckv)
+    grad_send_near(wt.co)
+    grad_send_near(wt.cq)
     matmul_back(buf.kv, wt.ckv.weight, set_a.parts)
     mem_step = reduce_start(set_a)
     column_sums(buf.q2, 0, 1, 9, 2)
@@ -1371,9 +1374,7 @@
     on_mid(fold, final_b, buf.tail)
     send(buf.tail, buf.tail, k_units + 14, dev_adj, mid)
     reduce_done(final_b)
-    grad_combine(wt.co)
     inner_grad_combine(wt.f1)
-    grad_combine(wt.cq)
     e1 = gather_open(buf.e3, None, 2)
     for h in range(2):
         reduce_ready_half(step, h)
@@ -1394,8 +1395,9 @@
     grad_outward(wt.co)
     grad_combine(wt.so)
     run_if(end, lambda: weight_grad(buf.a1, buf.qkv, wt.qkv))
-    grad_send_far(wt.qkv)
-    grad_send_middle(wt.qkv)
+    grad_send(wt.qkv)
+    grad_send_near(wt.ckv)
+    grad_send_near(wt.so)
     matmul_back(buf.qkv, wt.qkv.weight, set_b.parts)
     step = reduce_start(set_b)
     on_mid(weight_grad, buf.a1, buf.qkv, wt.qkv)
@@ -1413,6 +1415,8 @@
         to = (s + j) % n_sec
         send(buf.mb.at[:, part(to, mem_cols)], buf.ml.at[j], k_back + j, (to, d))
     grad_outward(wt.ckv)
+    grad_combine_middle(wt.qkv)
+    grad_outward(wt.so)
     reduce_ready(step)
 
     def store_stage(place, value):
@@ -1426,8 +1430,6 @@
     send(buf.ig, io.input_grad, k_in, ((s + n_sec - 1) % n_sec, d))
     buf.sga[z] = buf.sg[...].astype(BF16)
     sums = spread_start(lambda plane: buf.sga.at[plane])
-    grad_combine_middle(wt.qkv)
-    grad_outward(wt.so)
     inner_final(end)
     for weight in (wt.co, wt.cq):
         grad_final(weight)
@@ -1555,9 +1557,10 @@
         copy.start()
     outward = []
     gain, shift, out_bias, self_bias, cross_bias, unit_bias = small_buf
-    gain[0] = sums[0:3, 0:64]
-    shift[0] = sums[3:6, 0:64]
-    out_bias[0] = sums[6:9, 0:64]
+    for row in range(3):
+        gain[row] = sums[row:row + 1, 0:64]
+        shift[row] = sums[row + 3:row + 4, 0:64]
+        out_bias[row] = sums[row + 6:row + 7, 0:64]
     self_bias[...] = sums[9:10, :]
     cross_bias[...] = sums[10:11, :]
     unit_bias[:, 0:128] = sums[11:12, :]
@@ -1619,7 +1622,7 @@
         ),
     )(*operands)
     shapes = [result.shape for result in results]
-    small_shapes = [(1, 3, 64)] * 3 + [(1, 128), (1, 128), (1, 256)]
+    small_shapes = [(3, 1, 64)] * 3 + [(1, 128), (1, 128), (1, 256)]
     vmem = pl.BlockSpec(memory_space=pltpu.VMEM)
     finished = pl.pallas_call(
         finish_kernel,
@@ -1644,8 +1647,8 @@
         output[None, None],
         input_grad[None, None],
         memory_grad[None],
-        gain,
-        shift,
+        gain.transpose(1, 0, 2),
+        shift.transpose(1, 0, 2),
         g_qkv[None],
         self_biases,
         g_so[None],
@@ -1653,7 +1656,7 @@
         g_ckv[None],
         cross_biases,
         g_co[None],
-        biases,
+        biases.transpose(1, 0, 2),
         g_f1[None],
         units,
         g_f2[None],

time: 238 us -> 234 us (0.983)
  local copies, waits for them, and re-layouts: 2.6 us -> 0 us
    unnamed x9 -> x0, local copies, waits for them, and re-layouts: 2.6 us -> none
where the time goes in v6:
time: 234 us; the launch traced here: 233 us
  Pallas kernels  231 us (99%)
    pallas_call x1, Pallas kernels, on_device_planes(): pl.pallas_call(functools.partial(whole_kernel, n_sec, mem_cols), out_shap...  226 us

profile of v6, /device:TPU:1, one launch (start us, length us, event | category | flops | bytes accessed | tf_op | source)
XLA Modules:
  0.0 232.9 jit_solution(15373328815210763148)
XLA Ops:
  1.9 226.4 %shard_map.297 = (bf16[192,1024]{1,0:T(8,128)(2,1)}, bf16[192,1024]{1,0:T(8,128)(2,1)}, bf16[192,512]{1,0:T(8,128)(2,1)}, bf16[64,3072]{1,0:T(8,128)(2,1)}, bf16...) custom-call(bf16[192,1024]{1,0:T(8,128)(2,1)} %bitcast.32, ...), custom_call_target="tpu_custom_call" | custom-call | flops 20999999488 | bytes 20971520 | tf_op jit(solution)/shard_map/pallas_call | solution.py:1611
  228.4 4.3 %shard_map.298 = (bf16[192,1024]{1,0:T(8,128)(2,1)}, bf16[192,1024]{1,0:T(8,128)(2,1)}, bf16[192,512]{1,0:T(8,128)(2,1)}, f32[64,3072]{1,0:T(8,128)}, f32[64,102...) custom-call(bf16[192,1024]{1,0:T(8,128)(2,1)} %get-tuple-element.43., ...), custom_call_target="tpu_custom_call" | custom-call | bytes 9437184 | tf_op jit(solution)/shard_map/pallas_call | solution.py:1627

commit v7 on v6

--- a/solution.py
+++ b/solution.py
@@ -496,7 +496,7 @@
     for name, (count, _, by_column) in WEIGHTS.items():
         weight = getattr(wt, name)
         weight.count, weight.by_column = count, by_column
-        weight.pieces, weight.piece = 1, 0
+        weight.pieces, weight.piece, weight.last_copies = 1, 0, []
         weight.to_use, weight.swap, weight.to_sum, weight.last = slot(5), slot(3), slot(6), slot(3)
 
     def block(name, index):
@@ -671,6 +671,13 @@
     def inner_grad_near(name):
         send(grad_block(name, z_opp), name.near, name.to_sum + 1, dev_opp, mid)
 
+    def f2_half(rows_of, h):
+        return rows_of.at[part(h, wt.f2.count // 2)]
+
+    def f2_near(h):
+        src = f2_half(grad_block(wt.f2, z_opp), h)
+        send(src, f2_half(wt.f2.near, h), wt.f2.to_sum + 1 + 2 * h, dev_opp, mid)
+
     def inner_grad_combine(name):
         k = name.to_sum
 
@@ -686,46 +693,50 @@
         run_if(mid, add)
         send(name.far, name.near, k + 2, dev_adj, mid)
 
-    def inner_grad_total(name, cond):
+    def grad_total(name, cond):
         k = name.to_sum
-        if cond is end:
-            arrived(name.near, k + 2, end)
-        else:
-            arrived(name.near, k + 1, mid)
-            run_if(mid, lambda: grad_add(name, name.near, z))
-
-    def grad_total(name):
-        k = name.to_sum
-        arrived(name.near, k + 5, end)
-        arrived(name.near, k + 2, mid)
-        arrived(name.far, k + 4, mid)
-
-        def add_far():
+        arrived(name.near, k + (5 if cond is end else 2), cond)
+        if cond is mid:
+            arrived(name.far, k + 4, mid)
+
+        def add():
             def one(place):
-                total = name.near[place, :].astype(F32) + name.far[place, :].astype(F32)
+                total = name.near[place, :].astype(F32)
+                if cond is mid:
+                    total = total + name.far[place, :].astype(F32)
                 name.near[place, :] = (total + grad_block(name, z)[place, :].astype(F32)).astype(BF16)
 
             add_rows(name.count, one)
 
-        run_if(mid, add_far)
-        run_if(end, lambda: grad_add(name, name.near, z))
-
-    def grad_final(name):
-        grad_total(name)
+        run_if(cond, add)
+
+    def grad_final(name, cond):
+        grad_total(name, cond)
         if name.by_column:
             size = name.count // P_IN
             for j, (q_to, device) in enumerate(in_plane):
                 src = name.near.at[part(q_to, size)]
-                send(src, name.sorted.at[q], name.last + j, device)
+                send(src, name.sorted.at[q], name.last + j, device, cond)
             src = name.near.at[part(q, size)]
-            name.own_copy = [local(src, name.sorted.at[q])]
+            name.last_copies.append((local(src, name.sorted.at[q], cond), cond))
         else:
-            keep(name.near, name.result)
-
-    def inner_final(cond):
-        inner_grad_total(wt.f2, cond)
+            keep(name.near, name.result, cond)
+
+    def f2_final(cond):
+        if cond is end:
+            arrived(wt.f2.near, wt.f2.to_sum + 2, end)
+        else:
+            for h in range(2):
+                arrived(f2_half(wt.f2.near, h), wt.f2.to_sum + 1 + 2 * h, mid)
+            run_if(mid, lambda: grad_add(wt.f2, wt.f2.near, z))
         keep(wt.f2.near, wt.f2.result, cond)
-        inner_grad_total(wt.f1, cond)
+
+    def f1_final(cond):
+        if cond is end:
+            arrived(wt.f1.near, wt.f1.to_sum + 2, end)
+        else:
+            arrived(wt.f1.near, wt.f1.to_sum + 1, mid)
+            run_if(mid, lambda: grad_add(wt.f1, wt.f1.near, z))
         size = wt.f1.count // P_IN
         for tile in range(Z):
             dst = unit_columns(wt.f1.result, tile, q)
@@ -737,8 +748,8 @@
     def last_wait(name):
         for j, (q_from, _) in enumerate(in_plane):
             arrived(name.sorted.at[q_from], name.last + j)
-        for copy in name.own_copy:
-            copy.wait()
+        for copy, cond in name.last_copies:
+            run_if(cond, copy.wait)
         unsort_columns(name)
         keep(name.raw, name.result)
 
@@ -1287,7 +1298,7 @@
             reduce_relay_half(step_b, 0)
             on_mid(weight_grad, buf.gb, buf.e3b, wt.f2, True)
             inner_grad_far(wt.f2)
-            inner_grad_near(wt.f2)
+            f2_near(0)
         on_mid(units_back, buf.e3b, buf.gpb, at)
         if h == 0:
             gather_relay_part(a3b, 1)
@@ -1330,14 +1341,14 @@
     reduce_done(e3)
     for record in to_middle:
         sent(record)
-    reduce_ready(step)
+    e2 = gather_open(buf.e2, None, 2)
+    for h in range(2):
+        reduce_ready_half(step, h)
+        on_mid(units_norm_back, lambda place: reduced(step, place), (h,))
+        gather_part(e2, h, mid)
     final_b = reduce_open(set_c, mid)
     reduce_start_half(final_b, 0)
     reduce_start_half(final_b, 1)
-    on_mid(units_norm_back, lambda place: reduced(step, place), (0, 1))
-    e2 = gather_open(buf.e2, None, 2)
-    gather_part(e2, 0, mid)
-    gather_part(e2, 1, mid)
     inner_grad_combine(wt.f2)
     for h in range(2):
         arrived(buf.back.at[part(h, HALF)], k_units + 12 + h, end)
@@ -1364,8 +1375,7 @@
     grad_combine(wt.cq)
     weight_grad(buf.m, buf.kv, wt.ckv)
     grad_send(wt.ckv)
-    grad_send_near(wt.co)
-    grad_send_near(wt.cq)
+    grad_send_near(wt.ckv)
     matmul_back(buf.kv, wt.ckv.weight, set_a.parts)
     mem_step = reduce_start(set_a)
     column_sums(buf.q2, 0, 1, 9, 2)
@@ -1396,8 +1406,6 @@
     grad_combine(wt.so)
     run_if(end, lambda: weight_grad(buf.a1, buf.qkv, wt.qkv))
     grad_send(wt.qkv)
-    grad_send_near(wt.ckv)
-    grad_send_near(wt.so)
     matmul_back(buf.qkv, wt.qkv.weight, set_b.parts)
     step = reduce_start(set_b)
     on_mid(weight_grad, buf.a1, buf.qkv, wt.qkv)
@@ -1405,7 +1413,7 @@
     column_sums(buf.qkv, 2, 1, 9, 1)
     grad_outward(wt.cq)
     reduce_relay(step)
-    inner_final(mid)
+    f1_final(mid)
     grad_combine_far(wt.qkv)
 
     reduce_ready(mem_step)
@@ -1415,7 +1423,6 @@
         to = (s + j) % n_sec
         send(buf.mb.at[:, part(to, mem_cols)], buf.ml.at[j], k_back + j, (to, d))
     grad_outward(wt.ckv)
-    grad_combine_middle(wt.qkv)
     grad_outward(wt.so)
     reduce_ready(step)
 
@@ -1430,20 +1437,25 @@
     send(buf.ig, io.input_grad, k_in, ((s + n_sec - 1) % n_sec, d))
     buf.sga[z] = buf.sg[...].astype(BF16)
     sums = spread_start(lambda plane: buf.sga.at[plane])
-    inner_final(end)
+    grad_combine_middle(wt.qkv)
+    f2_near(1)
+    for weight in (wt.qkv, wt.cq, wt.co, wt.so):
+        grad_send_near(weight)
+    f2_final(end)
+    f1_final(end)
     for weight in (wt.co, wt.cq):
-        grad_final(weight)
-    grad_send_near(wt.qkv)
+        grad_final(weight, end)
     grad_outward(wt.qkv)
-    grad_final(wt.ckv)
+    grad_final(wt.ckv, end)
+    grad_final(wt.so, end)
+    grad_final(wt.ckv, mid)
     spread_wait(sums)
     planes = buf.sga[0].astype(F32)
     for plane in range(1, Z):
         planes = planes + buf.sga[plane].astype(F32)
     buf.sgp[q] = planes.astype(BF16)
     spread_plane(sums, buf.sgp)
-    grad_final(wt.so)
-    grad_final(wt.qkv)
+    grad_final(wt.qkv, mid)
 
     arrived(buf.tail, k_units + 14, end)
     run_if(end, lambda: finish(lambda place: buf.tail[place, :].astype(F32)))
@@ -1459,6 +1471,10 @@
 
     loop(L // TILE, memory_total)
     keep(buf.mo, io.memory_grad)
+    grad_final(wt.qkv, end)
+    for weight in (wt.cq, wt.co, wt.so):
+        grad_final(weight, mid)
+    f2_final(mid)
     unit_last_wait()
     last_wait(wt.cq)
     last_wait(wt.ckv)
@@ -1495,7 +1511,7 @@
         run_if(cond, copy.wait)
     for record in list(started):
         sent(record)
-    assert counter[0] <= SEMS
+    assert counter[0] <= SEMS and local_counter[0] <= 64
 
 
 def buffer_shapes(n_sec, mem_cols):
@@ -1540,7 +1556,7 @@
     return scratch + [
         pltpu.SemaphoreType.DMA((SEMS,)),
         pltpu.SemaphoreType.DMA((SEMS,)),
-        pltpu.SemaphoreType.DMA((48,)),
+        pltpu.SemaphoreType.DMA((64,)),
     ]
 
 

time: 234 us -> 230 us (0.983)
  Pallas kernels: 231 us -> 226 us
    pallas_call x1, Pallas kernels: 226 us -> 222 us  [on_device_planes(): pl.pallas_call(functools.partial(whole_kernel, n_sec, mem_cols), out_shap...]
where the time goes in v7:
time: 230 us; the launch traced here: 228 us
  Pallas kernels  226 us (98%)
    pallas_call x1, Pallas kernels, on_device_planes(): pl.pallas_call(functools.partial(whole_kernel, n_sec, mem_cols), out_shap...  222 us

profile of v7, /device:TPU:1, one launch (start us, length us, event | category | flops | bytes accessed | tf_op | source)
XLA Modules:
  0.0 227.9 jit_solution(12974410489916568281)
XLA Ops:
  1.9 221.5 %shard_map.297 = (bf16[192,1024]{1,0:T(8,128)(2,1)}, bf16[192,1024]{1,0:T(8,128)(2,1)}, bf16[192,512]{1,0:T(8,128)(2,1)}, bf16[64,3072]{1,0:T(8,128)(2,1)}, bf16...) custom-call(bf16[192,1024]{1,0:T(8,128)(2,1)} %bitcast.32, ...), custom_call_target="tpu_custom_call" | custom-call | flops 20999999488 | bytes 20971520 | tf_op jit(solution)/shard_map/pallas_call | solution.py:1627
  223.5 4.3 %shard_map.298 = (bf16[192,1024]{1,0:T(8,128)(2,1)}, bf16[192,1024]{1,0:T(8,128)(2,1)}, bf16[192,512]{1,0:T(8,128)(2,1)}, f32[64,3072]{1,0:T(8,128)}, f32[64,102...) custom-call(bf16[192,1024]{1,0:T(8,128)(2,1)} %get-tuple-element.43., ...), custom_call_target="tpu_custom_call" | custom-call | bytes 9437184 | tf_op jit(solution)/shard_map/pallas_call | solution.py:1643

commit v8 on v7

--- a/solution.py
+++ b/solution.py
@@ -1296,9 +1296,6 @@
             reduce_relay(final)
         else:
             reduce_relay_half(step_b, 0)
-            on_mid(weight_grad, buf.gb, buf.e3b, wt.f2, True)
-            inner_grad_far(wt.f2)
-            f2_near(0)
         on_mid(units_back, buf.e3b, buf.gpb, at)
         if h == 0:
             gather_relay_part(a3b, 1)
@@ -1311,6 +1308,9 @@
         ready = buf.back.at[part(h, HALF)]
         send(ready, ready, k_units + 12 + h, dev_adj, mid)
 
+    on_mid(weight_grad, buf.gb, buf.e3b, wt.f2, True)
+    inner_grad_far(wt.f2)
+    f2_near(0)
     reduce_relay_half(step_b, 1)
     on_mid(units_back, buf.e3, buf.gp)
     back_outward(0)
@@ -1424,6 +1424,7 @@
         send(buf.mb.at[:, part(to, mem_cols)], buf.ml.at[j], k_back + j, (to, d))
     grad_outward(wt.ckv)
     grad_outward(wt.so)
+    grad_combine_middle(wt.qkv)
     reduce_ready(step)
 
     def store_stage(place, value):
@@ -1437,7 +1438,6 @@
     send(buf.ig, io.input_grad, k_in, ((s + n_sec - 1) % n_sec, d))
     buf.sga[z] = buf.sg[...].astype(BF16)
     sums = spread_start(lambda plane: buf.sga.at[plane])
-    grad_combine_middle(wt.qkv)
     f2_near(1)
     for weight in (wt.qkv, wt.cq, wt.co, wt.so):
         grad_send_near(weight)
@@ -1449,13 +1449,13 @@
     grad_final(wt.ckv, end)
     grad_final(wt.so, end)
     grad_final(wt.ckv, mid)
+    grad_final(wt.qkv, mid)
     spread_wait(sums)
     planes = buf.sga[0].astype(F32)
     for plane in range(1, Z):
         planes = planes + buf.sga[plane].astype(F32)
     buf.sgp[q] = planes.astype(BF16)
     spread_plane(sums, buf.sgp)
-    grad_final(wt.qkv, mid)
 
     arrived(buf.tail, k_units + 14, end)
     run_if(end, lambda: finish(lambda place: buf.tail[place, :].astype(F32)))
@@ -1569,8 +1569,9 @@
         pltpu.make_async_copy(src, dst, sems.at[i])
         for i, (src, dst) in enumerate(zip(low + moved, low_buf + moved_buf))
     ]
-    for copy in inward:
-        copy.start()
+    order = (7, 8, 5, 6, 0, 2, 9, 1, 4, 3)
+    for i in order:
+        inward[i].start()
     outward = []
     gain, shift, out_bias, self_bias, cross_bias, unit_bias = small_buf
     for row in range(3):
@@ -1585,21 +1586,19 @@
         back = pltpu.make_async_copy(src, dst, sems.at[20 + i])
         back.start()
         outward.append(back)
-    for i, copy in enumerate(inward[:7]):
-        copy.wait()
-        rows_in = low_buf[i].shape[0]
-
-        def one(j, i=i):
-            place = part(j, 16)
-            high_buf[i][place, :] = low_buf[i][place, :].astype(F32)
-
-        loop(rows_in // 16, one)
-        back = pltpu.make_async_copy(high_buf[i], high[i], sems.at[10 + i])
-        back.start()
-        outward.append(back)
-    for i, copy in enumerate(inward[7:]):
-        copy.wait()
-        back = pltpu.make_async_copy(moved_buf[i], moved_out[i], sems.at[17 + i])
+    for i in order:
+        inward[i].wait()
+        if i < 7:
+            src, dst = high_buf[i], high[i]
+
+            def one(j, i=i):
+                place = part(j, 16)
+                high_buf[i][place, :] = low_buf[i][place, :].astype(F32)
+
+            loop(low_buf[i].shape[0] // 16, one)
+        else:
+            src, dst = moved_buf[i - 7], moved_out[i - 7]
+        back = pltpu.make_async_copy(src, dst, sems.at[10 + i])
         back.start()
         outward.append(back)
     for copy in outward:

time: 230 us -> 229 us (level)
  no operation moved by 1% of the time
where the time goes in v8:
time: 229 us
  Pallas kernels  226 us (99%)
    pallas_call x1, Pallas kernels, on_device_planes(): pl.pallas_call(functools.partial(whole_kernel, n_sec, mem_cols), out_shap...  222 us

profile of v8, /device:TPU:1, one launch (start us, length us, event | category | flops | bytes accessed | tf_op | source)
XLA Modules:
  0.0 228.6 jit_solution(4320684190263522442)
XLA Ops:
  1.9 222.1 %shard_map.297 = (bf16[192,1024]{1,0:T(8,128)(2,1)}, bf16[192,1024]{1,0:T(8,128)(2,1)}, bf16[192,512]{1,0:T(8,128)(2,1)}, bf16[64,3072]{1,0:T(8,128)(2,1)}, bf16...) custom-call(bf16[192,1024]{1,0:T(8,128)(2,1)} %bitcast.32, ...), custom_call_target="tpu_custom_call" | custom-call | flops 20999999488 | bytes 20971520 | tf_op jit(solution)/shard_map/pallas_call | solution.py:1626
  224.1 4.3 %shard_map.298 = (bf16[192,1024]{1,0:T(8,128)(2,1)}, bf16[192,1024]{1,0:T(8,128)(2,1)}, bf16[192,512]{1,0:T(8,128)(2,1)}, f32[64,3072]{1,0:T(8,128)}, f32[64,102...) custom-call(bf16[192,1024]{1,0:T(8,128)(2,1)} %get-tuple-element.43., ...), custom_call_target="tpu_custom_call" | custom-call | bytes 9437184 | tf_op jit(solution)/shard_map/pallas_call | solution.py:1642

commit v9 on v8

--- a/solution.py
+++ b/solution.py
@@ -1185,8 +1185,8 @@
         gather_part(a2, h)
     reduce_done(step)
     relay_near(wt.cq)
+    relay_far(wt.cq)
     weight_outward(wt.co, wt.co.source)
-    relay_far(wt.cq)
     weight_ready(wt.ckv)
     matmul(buf.m, wt.ckv.weight, buf.kv, buf.bias, 1, 1)
     relay_near(wt.co)

time: 229 us -> 229 us (level)
  no operation moved by 1% of the time
where the time goes in v9:
time: 229 us
  Pallas kernels  226 us (99%)
    pallas_call x1, Pallas kernels, on_device_planes(): pl.pallas_call(functools.partial(whole_kernel, n_sec, mem_cols), out_shap...  222 us

profile of v9, /device:TPU:1, one launch (start us, length us, event | category | flops | bytes accessed | tf_op | source)
XLA Modules:
  0.0 228.6 jit_solution(10335432845969203048)
XLA Ops:
  1.9 222.1 %shard_map.297 = (bf16[192,1024]{1,0:T(8,128)(2,1)}, bf16[192,1024]{1,0:T(8,128)(2,1)}, bf16[192,512]{1,0:T(8,128)(2,1)}, bf16[64,3072]{1,0:T(8,128)(2,1)}, bf16...) custom-call(bf16[192,1024]{1,0:T(8,128)(2,1)} %bitcast.32, ...), custom_call_target="tpu_custom_call" | custom-call | flops 20999999488 | bytes 20971520 | tf_op jit(solution)/shard_map/pallas_call | solution.py:1626
  224.1 4.3 %shard_map.298 = (bf16[192,1024]{1,0:T(8,128)(2,1)}, bf16[192,1024]{1,0:T(8,128)(2,1)}, bf16[192,512]{1,0:T(8,128)(2,1)}, f32[64,3072]{1,0:T(8,128)}, f32[64,102...) custom-call(bf16[192,1024]{1,0:T(8,128)(2,1)} %get-tuple-element.43., ...), custom_call_target="tpu_custom_call" | custom-call | bytes 9437184 | tf_op jit(solution)/shard_map/pallas_call | solution.py:1642
